TPU v7x, 256 devices: a whole 4x4x8 slice. The times are simulated.
256 devices in a mesh: ctx: 64 (over x, z, core), tp: 4 (over y).
Axes of the slice: x: 4, y: 4, z: 8, core: 2. Of those that a mesh axis runs over, the one named last changes fastest.
Arguments:
- layer_input: bfloat16 [8192, 4096], P(('ctx', 'tp')), may hold values from -8 to 8
- dt_weight: bfloat16 [4096, 128], P(None, 'tp'), may hold values from -1 to 1
- dt_bias: float32 [128], P('tp'), may hold values from -5.5 to -4.5
- a_log: float32 [128], P('tp'), may hold values from -4.5 to 1.5
- ssm_input: bfloat16 [8192, 8192], P('ctx', 'tp'), may hold values from -6 to 6
- b_in: bfloat16 [8192, 1024], P('ctx', 'tp'), may hold values from -6 to 6
- c_in: bfloat16 [8192, 1024], P('ctx', 'tp'), may hold values from -6 to 6
- out_grad: bfloat16 [8192, 8192], P('ctx', 'tp'), may hold values from -3 to 3
Outputs:
- grad_ssm_input: bfloat16 [8192, 8192], P('ctx', 'tp')
- grad_b_in: bfloat16 [8192, 1024], P('ctx', 'tp')
- grad_c_in: bfloat16 [8192, 1024], P('ctx', 'tp')
- grad_layer_input: bfloat16 [8192, 4096], P(('ctx', 'tp'))
- grad_dt_weight: float32 [4096, 128], P(None, 'tp')
- grad_dt_bias: float32 [128], P('tp')
- grad_a_log: float32 [128], P('tp')
All inputs are finite; a program needn't handle non-finite values.
Results may differ from a plain program's by a relative error of at most 0.0095.
Values may be sent and summed in bfloat16 or wider, within the bound.
No kernel may reach another device: no remote copies, remote signals or barrier semaphores. Data moves between devices by JAX's collectives and lax.ppermute only.
A program may use at most 320 MiB of HBM per device.

v0:
```python
import jax
import jax.numpy as jnp
from jax import lax
from jax.sharding import PartitionSpec as P

HEAD_DIM = 64
STATE = 128
SPAN = 128


def entering(value, axis, combine, identity, reverse):
    count, place = (lax.axis_size(axis), lax.axis_index(axis))
    everything = jax.tree.map(lambda part: lax.all_gather(part, axis), value)
    start = jax.tree.map(
        lambda part, zero: jnp.broadcast_to(jnp.asarray(zero, part.dtype), part.shape),
        value,
        identity,
    )

    def step(k, before):
        at = count - 1 - k if reverse else k
        reached = at > place if reverse else at < place
        new = combine(before, jax.tree.map(lambda part: part[at], everything))
        return jax.tree.map(lambda a, b: jnp.where(reached, a, b), new, before)

    return lax.fori_loop(0, count, step, start)


def product(form, left, right):
    return jnp.einsum(form, left, right, preferred_element_type=jnp.float32)


def chain_combine(earlier, latter):
    return (earlier[0] * latter[0], latter[0][:, :, None, None] * earlier[1] + latter[1])


def span_operands(inputs, grad_out, step_block, log_cum):
    final_cum = log_cum[..., -1:, :, :]
    remain = jnp.exp(final_cum - log_cum)
    growth = jnp.exp(log_cum)
    scaled = step_block[..., None] * inputs.astype(jnp.float32)
    in_weighted = (remain[..., None] * scaled).astype(jnp.bfloat16)
    out_weighted = (growth[..., None] * grad_out.astype(jnp.float32)).astype(jnp.bfloat16)
    return (scaled, in_weighted, out_weighted)


def span_grads(
    inputs,
    grad_out,
    b_block,
    c_block,
    step_block,
    log_cum,
    scaled,
    in_weighted,
    out_weighted,
    start_state,
    end_cot,
):
    length = log_cum.shape[0]
    grads_f = grad_out.astype(jnp.float32)
    scaled_bf = scaled.astype(jnp.bfloat16)
    start_bf = start_state.astype(jnp.bfloat16)
    end_bf = end_cot.astype(jnp.bfloat16)
    scores = product("tgn,sgn->gts", c_block, b_block)
    cum_heads = jnp.transpose(log_cum, (1, 2, 0))
    row_ids = lax.broadcasted_iota(jnp.int32, (length, length), 0)
    col_ids = lax.broadcasted_iota(jnp.int32, (length, length), 1)
    lower_mask = row_ids >= col_ids
    spread = jnp.minimum(cum_heads[..., :, None] - cum_heads[..., None, :], 0.0)
    decay_mat = jnp.where(lower_mask, jnp.exp(spread), 0.0)
    mixing = scores[:, None] * decay_mat
    mixing_bf = mixing.astype(jnp.bfloat16)
    grad_mixing = product("tghp,sghp->ghts", grad_out, scaled_bf)
    grad_scores = jnp.sum(grad_mixing * decay_mat, axis=1).astype(jnp.bfloat16)
    pulled = product("ghpn,sgn->sghp", end_bf, b_block)
    from_state = product("ghpn,tgn->tghp", start_bf, c_block)
    final_cum = log_cum[length - 1]
    remain = jnp.exp(final_cum[None] - log_cum)
    growth = jnp.exp(log_cum)
    grad_scaled = product("ghts,tghp->sghp", mixing_bf, grad_out) + remain[..., None] * pulled
    grad_b = product("gts,tgn->sgn", grad_scores, c_block) + product(
        "sghp,ghpn->sgn", in_weighted, end_bf
    )
    grad_c = product("gts,sgn->tgn", grad_scores, b_block) + product(
        "tghp,ghpn->tgn", out_weighted, start_bf
    )
    weighted = grad_mixing * mixing
    grad_cum = jnp.transpose(jnp.sum(weighted, axis=3) - jnp.sum(weighted, axis=2), (2, 0, 1))
    grad_cum = grad_cum + growth * jnp.sum(grads_f * from_state, axis=3)
    touched = remain * jnp.sum(scaled * pulled, axis=3)
    last_term = jnp.sum(touched, axis=0) + jnp.exp(final_cum) * jnp.sum(
        end_cot * start_state, axis=(2, 3)
    )
    grad_cum = grad_cum - touched
    grad_cum = grad_cum.at[length - 1].add(last_term)
    grad_log = jnp.cumsum(grad_cum[::-1], axis=0)[::-1]
    grad_x = step_block[..., None] * grad_scaled
    grad_step = jnp.sum(inputs.astype(jnp.float32) * grad_scaled, axis=3)
    return (grad_x, grad_b, grad_c, grad_step, grad_log)


def local(layer_input, dt_weight, dt_bias, a_log, ssm_input, b_in, c_in, out_grad):
    tokens_here = ssm_input.shape[0]
    heads_here = dt_weight.shape[1]
    groups_here = b_in.shape[1] // STATE
    per_group = heads_here // groups_here
    span_count = tokens_here // SPAN
    gathered = lax.all_gather(layer_input, "tp", axis=0, tiled=True)
    projected = jnp.dot(gathered, dt_weight, preferred_element_type=jnp.float32)
    pre_step = projected + dt_bias[None, :]
    step_size = jax.nn.softplus(pre_step)
    decay_rate = jnp.exp(a_log)
    block_shape = (span_count, SPAN, groups_here, per_group)
    step_blocks = step_size.reshape(block_shape)
    log_cum = jnp.cumsum(((-decay_rate)[None, :] * step_size).reshape(block_shape), axis=1)
    wide_shape = (span_count, SPAN, groups_here, per_group, HEAD_DIM)
    input_blocks = ssm_input.reshape(wide_shape)
    grad_blocks = out_grad.reshape(wide_shape)
    b_blocks = b_in.reshape(span_count, SPAN, groups_here, STATE)
    c_blocks = c_in.reshape(span_count, SPAN, groups_here, STATE)
    scaled, in_weighted, out_weighted = span_operands(
        input_blocks, grad_blocks, step_blocks, log_cum
    )
    block_decay = jnp.exp(log_cum[:, SPAN - 1])
    block_states = product("ksghp,ksgn->kghpn", in_weighted, b_blocks)
    block_pulls = product("ktghp,ktgn->kghpn", out_weighted, c_blocks)
    identity = (
        jnp.ones((groups_here, per_group), jnp.float32),
        jnp.zeros((groups_here, per_group, HEAD_DIM, STATE), jnp.float32),
    )

    def fold_step(carried, block_item):
        return (chain_combine(carried, block_item), carried)

    (device_decay, device_state), prefix = lax.scan(
        fold_step, identity, (block_decay, block_states)
    )
    (_, device_cot), suffix = lax.scan(
        fold_step, identity, (block_decay, block_pulls), reverse=True
    )
    incoming = entering((device_decay, device_state), "ctx", chain_combine, identity, False)[1]
    outgoing = entering((device_decay, device_cot), "ctx", chain_combine, identity, True)[1]
    start_states = prefix[1] + prefix[0][..., None, None] * incoming[None]
    end_cots = suffix[1] + suffix[0][..., None, None] * outgoing[None]

    def one_span(block_item):
        (
            inputs,
            grad_out,
            b_block,
            c_block,
            step_block,
            cum_block,
            scaled_block,
            in_block,
            out_block,
            start_state,
            end_cot,
        ) = block_item
        return span_grads(
            inputs,
            grad_out,
            b_block,
            c_block,
            step_block,
            cum_block,
            scaled_block,
            in_block,
            out_block,
            start_state,
            end_cot,
        )

    results = lax.map(
        one_span,
        (
            input_blocks,
            grad_blocks,
            b_blocks,
            c_blocks,
            step_blocks,
            log_cum,
            scaled,
            in_weighted,
            out_weighted,
            start_states,
            end_cots,
        ),
    )
    grad_ssm_input = results[0].reshape(tokens_here, heads_here * HEAD_DIM).astype(jnp.bfloat16)
    grad_b_in = results[1].reshape(tokens_here, groups_here * STATE).astype(jnp.bfloat16)
    grad_c_in = results[2].reshape(tokens_here, groups_here * STATE).astype(jnp.bfloat16)
    step_local = results[3].reshape(tokens_here, heads_here)
    grad_log = results[4].reshape(tokens_here, heads_here)
    grad_step = step_local - decay_rate[None, :] * grad_log
    rate_part = -jnp.sum(grad_log * step_size, axis=0)
    grad_pre = grad_step * jax.nn.sigmoid(pre_step)
    zed_grad = grad_pre.astype(jnp.bfloat16)
    bias_part = jnp.sum(grad_pre, axis=0)
    weight_part = jnp.einsum("rd,rh->dh", gathered, zed_grad, preferred_element_type=jnp.float32)
    grad_layer_input = lax.psum_scatter(
        jnp.einsum("rh,dh->rd", zed_grad, dt_weight, preferred_element_type=jnp.float32),
        "tp",
        scatter_dimension=0,
        tiled=True,
    ).astype(jnp.bfloat16)
    grad_dt_weight, grad_dt_bias, rate_total = lax.psum((weight_part, bias_part, rate_part), "ctx")
    grad_a_log = decay_rate * rate_total
    return (
        grad_ssm_input,
        grad_b_in,
        grad_c_in,
        grad_layer_input,
        grad_dt_weight,
        grad_dt_bias,
        grad_a_log,
    )


def solution(mesh):
    placed = (
        P(("ctx", "tp"), None),
        P(None, "tp"),
        P("tp"),
        P("tp"),
        P("ctx", "tp"),
        P("ctx", "tp"),
        P("ctx", "tp"),
        P("ctx", "tp"),
    )
    return jax.shard_map(
        local,
        mesh=mesh,
        in_specs=placed,
        out_specs=(
            P("ctx", "tp"),
            P("ctx", "tp"),
            P("ctx", "tp"),
            P(("ctx", "tp"), None),
            P(None, "tp"),
            P("tp"),
            P("tp"),
        ),
        check_vma=False,
    )
```

profile of v0, /device:TPU:1, one launch (start us, length us, event | category | flops | bytes accessed | tf_op | source)
XLA Modules:
  0.0 891.4 jit_solution(7397954845618587898)
XLA Ops:
  11.4 27.9 %all-gather.7.cloned.1.call-done = bf16[128,4096]{1,0:T(8,128)(2,1)} async-done(((bf16[32,4096]{1,0:T(8,128)(2,1)}), bf16[128,4096]{1,0:T(8,128)(2,1)}) %all-gather.7.cloned.1.call-update) | async-done | bytes 1048592 | tf_op jit(solution)/shard_map/all_gather | solution.py:109
  39.3 2.3 compare_select_fusion
  47.8 1.7 fusion.50
  50.9 48.9 %all-gather = f32[64,1,2,16]{3,2,1,0:T(2,128)} all-gather(f32[1,1,2,16]{3,2,1,0:T(2,128)} %get-tuple-element.433), channel_id=2, replica_groups=mesh['ctx'=64,'tp'=4] {'ctx'}, dimensions={0}, use_global_device_ids=true | all-gather | bytes 8320 | tf_op jit(solution)/shard_map/all_gather | solution.py:13
  99.9 3.4 fusion.7
  103.3 179.1 %all-gather.9.cloned.1.call-done = f32[128,16,64,128]{3,2,1,0:T(8,128)} async-done(((f32[2,16,64,128]{3,2,1,0:T(8,128)}), f32[128,16,64,128]{3,2,1,0:T(8,128)}) %all-gather.9.cloned.1.call-update) | async-done | bytes 67108880 | tf_op jit(solution)/shard_map/all_gather | solution.py:13
  282.4 176.0 %while.21 = (s32[]{:T(128)}, f32[2,16,64,128]{3,2,1,0:T(8,128)S(1)}, s32[]{:T(128)}, f32[64,2,16]{2,1,0:T(2,128)}, f32[64,2,16,64,128]{4,3,2,1,0:T(8,128)}, /*index=5*/s32[]{:T(128)}, s32[]{:T(128)}, s32[]{:T(128)}, s32[]{:T(128)}) while((s32[]{:T(128)}, f32[2,16,64,128]{3,2,1,0:T(8,128)S(1)}, s32[]{:T(128)}, ...), condition=%wide.region_2.3_spmd.clone, body=%wide.region_1.2_spmd.clone.sunk | while | flops 1048584 | bytes 3146287 | solution.py:26
  286.3 1.5 fusion.69
  291.7 1.5 fusion.69
  294.4 1.6 fusion.69
  297.3 1.5 fusion.69
  300.0 1.5 fusion.69
  302.7 1.5 fusion.69
  305.4 1.5 fusion.69
  308.1 1.5 fusion.69
  313.5 1.5 fusion.69
  316.2 1.5 fusion.69
  318.9 1.5 fusion.69
  321.7 1.5 fusion.69
  324.4 1.5 fusion.69
  327.2 1.5 fusion.69
  329.9 1.5 fusion.69
  332.7 1.5 fusion.69
  335.4 1.5 fusion.69
  338.1 1.5 fusion.69
  340.8 1.5 fusion.69
  343.5 1.5 fusion.69
  346.2 1.5 fusion.69
  348.9 1.8 fusion.69
  351.9 1.8 fusion.69
  354.9 1.5 fusion.69
  357.7 1.5 fusion.69
  360.4 1.5 fusion.69
  365.8 1.5 fusion.69
  368.6 1.5 fusion.69
  376.7 1.5 fusion.69
  379.5 1.5 fusion.69
  387.7 1.5 fusion.69
  390.4 1.5 fusion.69
  398.5 1.8 fusion.69
  401.6 1.5 fusion.69
  409.7 1.6 fusion.69
  412.5 1.5 fusion.69
  415.2 1.5 fusion.69
  420.6 1.8 fusion.69
  423.6 1.5 fusion.69
  431.8 1.8 fusion.69
  434.8 1.5 fusion.69
  442.9 1.8 fusion.69
  446.0 1.5 fusion.69
  448.7 1.5 fusion.69
  454.1 1.5 fusion.69
  459.6 58.9 %all-gather.11.cloned.1.call-done = f32[128,16,64,128]{3,2,1,0:T(8,128)} async-done(((f32[2,16,64,128]{3,2,1,0:T(8,128)}), f32[128,16,64,128]{3,2,1,0:T(8,128)}) %all-gather.11.cloned.1.call-update) | async-done | bytes 67108880 | tf_op jit(solution)/shard_map/all_gather | solution.py:13
  518.5 136.9 %while.22 = (s32[]{:T(128)}, f32[2,16,64,128]{3,2,1,0:T(8,128)S(1)}, s32[]{:T(128)}, f32[64,2,16]{2,1,0:T(2,128)}, f32[64,2,16,64,128]{4,3,2,1,0:T(8,128)}, /*index=5*/s32[]{:T(128)}, s32[]{:T(128)}) while((s32[]{:T(128)}, f32[2,16,64,128]{3,2,1,0:T(8,128)S(1)}, s32[]{:T(128)}, f32[64,2,16]{2,1,0:T(2,128)}, ...), condition=%wide.region_5.6_spmd.clone, body=%wide.region_4.5_spmd.clone.sunk | while | flops 1048580 | bytes 3146225 | solution.py:26
  655.4 1.5 fusion.9
  657.8 2.0 multiply_reduce_fusion.2
  663.1 1.7 fusion.49
  664.8 1.6 rev.9
  668.7 1.8 fusion.41
  670.6 2.1 convolution_bitcast_fusion.4
  677.9 124.2 %all-reduce = (f32[32]{0:T(128)}, f32[32]{0:T(128)S(1)}) all-reduce(f32[32]{0:T(128)S(1)} %copy-done.29, f32[32]{0:T(128)S(1)} %neg.16), channel_id=1, replica_groups=mesh['ctx'=64,'tp'=4] {'ctx'}, use_global_device_ids=true, to_apply=%region_17.18 | all-reduce | flops 64 | bytes 512 | tf_op jit(solution)/shard_map/psum | solution.py:208
  802.7 1.8 convert_element_type.98
  804.5 78.5 %all-reduce.3.cloned.1.call-done = f32[4096,32]{0,1:T(8,128)} async-done(((f32[4096,32]{0,1:T(8,128)}), f32[4096,32]{0,1:T(8,128)}) %all-reduce.3.cloned.1.call-update) | async-done | bytes 524304 | tf_op jit(solution)/shard_map/psum | solution.py:208
  883.0 1.9 copy.127
  (325 shorter events, 266.7 us)
Async XLA Ops:
  7.2 32.1 %copy-start = (bf16[4096,32]{0,1:T(8,128)(2,1)S(1)}, bf16[4096,32]{0,1:T(8,128)(2,1)}, u32[]{:S(2)}) copy-start(bf16[4096,32]{0,1:T(8,128)(2,1)} %param.15) | copy-start | bytes 786436
  7.2 32.1 %all-gather.7.cloned.1.call-start = ((), (), s32[]{:S(2)}) async-start(), calls=%async_computation.1 | async-start | bytes 1310720 | tf_op jit(solution)/shard_map/all_gather | solution.py:109
  7.9 274.5 %all-gather.9.cloned.1.call-start = ((), (), s32[]{:S(2)}) async-start(), calls=%async_computation.4 | async-start | bytes 68157440 | tf_op jit(solution)/shard_map/all_gather | solution.py:13
  9.3 34.7 %copy-start.1 = (bf16[128,2048]{0,1:T(8,128)(2,1)}, bf16[128,2048]{0,1:T(8,128)(2,1)S(1)}, u32[]{:S(2)}) copy-start(bf16[128,2048]{0,1:T(8,128)(2,1)S(1)} %copy.68) | copy-start | bytes 1572868
  39.3 4.8 copy-start.7
  42.5 1.5 copy-start.27
  42.6 1.4 copy-start.16
  42.7 1.4 copy-start.14
  42.7 1.7 copy-start.12
  42.7 1.6 copy-start.23
  44.0 474.5 %all-gather.11.cloned.1.call-start = ((), (), s32[]{:S(2)}) async-start(), calls=%async_computation.5 | async-start | bytes 68157440 | tf_op jit(solution)/shard_map/all_gather | solution.py:13
  45.7 757.0 %reduce-scatter.2.cloned.1.call-start = ((), (), s32[]{:S(2)}) async-start(), calls=%async_computation.2 | async-start | bytes 2621440 | tf_op jit(solution)/shard_map/reduce_scatter | solution.py:202
  655.4 2.4 copy-start.2
  655.4 2.3 copy-start.4
  655.4 2.3 copy-start.13
  655.4 2.3 copy-start.17
  655.4 2.3 copy-start.18
  655.4 2.3 copy-start.26
  657.7 2.0 copy-start.24
  657.7 2.0 copy-start.25
  657.8 2.0 copy-start.28
  657.8 4.3 copy-start.22
  657.8 9.6 %copy-start.21 = (f32[128,32]{0,1:T(8,128)S(1)}, f32[128,32]{0,1:T(8,128)}, u32[]{:S(2)}) copy-start(f32[128,32]{0,1:T(8,128)} %get-tuple-element.444) | copy-start | bytes 49156
  668.7 1.8 copy-start.19
  668.7 1.9 copy-start.15
  670.5 3.4 copy-start.6
  670.5 212.5 %all-reduce.3.cloned.1.call-start = ((), (), s32[]{:S(2)}) async-start(), calls=%async_computation.3 | async-start | bytes 1048576 | tf_op jit(solution)/shard_map/psum | solution.py:208
  670.6 3.4 copy-start.10
  670.6 3.5 copy-start.3
  670.6 3.5 copy-start.20
  672.8 2.5 copy-start.5
  672.8 2.5 copy-start.9
  672.8 2.5 copy-start.11
  672.8 2.7 copy-start.8
  673.9 4.0 copy-start.30
  673.9 4.0 copy-start.29
  673.9 128.3 %copy-start.31 = (f32[32]{0:T(128)S(1)}, f32[32]{0:T(128)}, u32[]{:S(2)}) copy-start(f32[32]{0:T(128)} %param.17) | copy-start | bytes 388
Sparse Core Ops, SparseCore 0:
  9.8 29.4 all-gather.6
  44.1 238.2 all-gather.8
  285.2 233.2 all-gather.10
  670.6 28.8 reduce-scatter.1
  703.9 179.0 all-reduce.2
where the time goes:
time: 899 us; the launch traced here: 891 us
  waiting for transfers between devices  345 us (38%)
  other arithmetic  198 us (22%)
  blocking collectives  173 us (19%)
  local copies, waits for them, and re-layouts  136 us (15%)
  matrix products  21.2 us (2%)
  between operations  14.2 us (2%)
    all_gather x2, waiting for transfers between devices, entering(): everything = jax.tree.map(lambda part: lax.all_gather(part, axis), value)  238 us
    select_n x128, other arithmetic, step(): return jax.tree.map(lambda a, b: jnp.where(reached, a, b), new, before)  189 us
    psum x1, blocking collectives, local(): lax.psum((weight_part, bias_part, rate_part), 'ctx')  124 us
    mul x128, local copies, waits for them, and re-layouts, chain_combine(): latter[0][:, :, None, None] * earlier[1] + latter[1]  121 us
    psum x1, waiting for transfers between devices, local(): lax.psum((weight_part, bias_part, rate_part), 'ctx')  78.5 us
    all_gather x1, blocking collectives, entering(): everything = jax.tree.map(lambda part: lax.all_gather(part, axis), value)  48.9 us
    all_gather x1, waiting for transfers between devices, local(): gathered = lax.all_gather(layer_input, 'tp', axis=0, tiled=True)  27.9 us
  transfers between devices with their start and end apart: 5, of which 4 were waited for; matrix products, arithmetic and copies ran while one was open for 22% of the time, Pallas kernels for 0%

commit v1 on v0

v1 whole, which is shorter than its diff:
```python
import jax
import jax.numpy as jnp
from jax import lax
from jax.experimental import pallas as pl
from jax.experimental.pallas import tpu as pltpu
from jax.sharding import Mesh
from jax.sharding import PartitionSpec as P

BF = jnp.bfloat16
F32 = jnp.float32
CHIPS, CORES, TP = 32, 2, 4
SPAN = 128
N = 128
HD = 64
HH = 16
W = HH * HD
D = 4096
PIECE = 32


def dot(a, b):
    return lax.dot_general(a, b, (((1,), (0,)), ((), ())), preferred_element_type=F32)


def dot_nt(a, b):
    return lax.dot_general(a, b, (((1,), (1,)), ((), ())), preferred_element_type=F32)


def split3(v):
    hi = v.astype(BF).astype(F32)
    rest = v - hi
    mid = rest.astype(BF).astype(F32)
    return [hi, mid, rest - mid]


def iota(shape, dim):
    return lax.broadcasted_iota(jnp.int32, shape, dim)


def triangle(keep):
    return jnp.where(keep(iota((SPAN, SPAN), 0), iota((SPAN, SPAN), 1)), 1.0, 0.0).astype(BF)


def sum_by(rows, matrix):
    r = rows.shape[0]
    out = dot(jnp.concatenate(split3(rows), 0).astype(BF), matrix)
    return out[:r] + out[r : 2 * r] + out[2 * r :]


def columns(first, second):
    stack = split3(first) + split3(second) + [jnp.zeros((32, SPAN), F32)]
    return jnp.concatenate(stack, 0).T.astype(BF)


def spread_maps():
    row = lax.broadcasted_iota(jnp.int32, (128, 2 * W), 0)
    col = lax.broadcasted_iota(jnp.int32, (128, 2 * W), 1)
    part = row // 48
    same = (row % 16) == (col % W) // HD
    return jnp.where(same & (part == col // W), 1.0, 0.0).astype(BF)


def project_kernel(scal, w, l0, l1, l2, l3, own, other):
    rows = jnp.concatenate([l0[...], l1[...], l2[...], l3[...]], 0)
    acc = pltpu.roll(dot_nt(w[...], rows), scal[0], 1)
    own[...] = acc[:HH]
    other[...] = acc[HH:]


def state_kernel(
    scal, po, pp, bias, alog, xo, xp, yo, yp, bo, bp, co, cp, maps,
    msg, s_first, p_second, small, decay,
    s_all, p_all,
):
    pre = jnp.concatenate([po[...] + bias[...], pp[...] + bias[...]], 0)
    step = jnp.maximum(pre, 0.0) + jnp.log1p(jnp.exp(-jnp.abs(pre)))
    rate = jnp.exp(alog[...])
    rate = jnp.concatenate([rate, rate], 0)
    cum = sum_by(-rate * step, triangle(lambda u, t: u <= t))
    small[0] = pre
    small[1] = step
    small[2] = cum
    remain_step = jnp.exp(cum[:, SPAN - 1 :] - cum) * step
    growth = jnp.exp(cum)
    for b, (x, y, bm, cm) in enumerate(((xo, yo, bo, co), (xp, yp, bp, cp))):
        rows = slice(b * HH, (b + 1) * HH)
        weights = columns(remain_step[rows], growth[rows])
        b_t = bm[...].astype(F32).T.astype(BF)
        c_t = cm[...].astype(F32).T.astype(BF)
        for k in range(W // 256):
            cols = slice(k * 256, (k + 1) * 256)
            w_in = dot(weights, maps[:, cols])
            s_all[b, :, cols] = dot(b_t, (w_in * x[:, cols].astype(F32)).astype(BF))
            w_out = dot(weights, maps[:, W + k * 256 : W + (k + 1) * 256])
            p_all[b, :, cols] = dot(c_t, (w_out * y[:, cols].astype(F32)).astype(BF))
            decay[b, :, cols] = jnp.broadcast_to(w_out[SPAN - 1 :], (8, 256))
    first = scal[1]
    second = 1 - first
    for k in range(W // 128):
        cols = slice(k * 128, (k + 1) * 128)
        d_first, d_second = decay[first, 0:1, cols], decay[second, 0:1, cols]
        s_f, p_s = s_all[first, :, cols], p_all[second, :, cols]
        forward = (d_second * s_f + s_all[second, :, cols]).astype(BF)
        backward = (p_all[first, :, cols] + d_first * p_s).astype(BF)
        s_first[:, cols] = s_f.astype(BF)
        p_second[:, cols] = p_s.astype(BF)
        d3 = jnp.concatenate(split3(d_first * d_second) + [jnp.zeros((13, 128), F32)], 0).astype(BF)
        for r in range(N // PIECE):
            at = k * (N // PIECE) + r
            msg[at, 0:PIECE, :] = forward[r * PIECE : (r + 1) * PIECE]
            msg[at, PIECE : 2 * PIECE, :] = backward[r * PIECE : (r + 1) * PIECE]
            msg[at, 2 * PIECE : 2 * PIECE + 16, :] = d3


def fold_kernel(msg, out):
    decays = []
    for k in range(CHIPS):
        d = msg[k, 2 * PIECE : 2 * PIECE + 16, :].astype(F32)
        decays.append(d[0:1] + d[1:2] + d[2:3])
    total = jnp.zeros((PIECE, 128), F32)
    for k in range(CHIPS):
        out[k, 0:PIECE, :] = total.astype(BF)
        total = total * decays[k] + msg[k, 0:PIECE, :].astype(F32)
    total = jnp.zeros((PIECE, 128), F32)
    for k in reversed(range(CHIPS)):
        out[k, PIECE : 2 * PIECE, :] = total.astype(BF)
        total = total * decays[k] + msg[k, PIECE : 2 * PIECE, :].astype(F32)


def intra_kernel(small, xo, xp, yo, yp, bo, bp, co, cp, gs, gb, gc, rows_out, cols_out):
    lane = iota((SPAN, 128), 1)
    low = lane < HD
    later = lane >= iota((SPAN, SPAN), 0)
    step_t = jnp.concatenate([small[1], jnp.zeros((96, 128), F32)], 0).T
    cum_t = jnp.concatenate([small[2], jnp.zeros((96, 128), F32)], 0).T
    sums = jnp.zeros((SPAN, 128), F32)
    zero = jnp.zeros((SPAN, 128), BF)
    for b, (x, y, bm, cm) in enumerate(((xo, yo, bo, co), (xp, yp, bp, cp))):
        scores = dot_nt(bm[...], cm[...])
        grad_scores = jnp.zeros((SPAN, SPAN), F32)
        for pair in range(HH // 2):
            cols = slice(pair * 128, (pair + 1) * 128)
            xs, ys = x[:, cols], y[:, cols]
            halves = []
            for side in range(2):
                h = b * HH + pair * 2 + side
                mine = jnp.where(low if side == 0 else ~low, xs, zero)
                grad_mixing = dot_nt(mine, ys)
                spread = small[2, h : h + 1, :] - cum_t[:, h : h + 1]
                decay = jnp.where(later, jnp.exp(jnp.minimum(spread, 0.0)), 0.0)
                mixing = scores * decay
                halves.append(dot(mixing.astype(BF), ys))
                scaled = grad_mixing * step_t[:, h : h + 1]
                grad_scores = grad_scores + scaled * decay
                rows_out[h : h + 1, :] = jnp.sum(scaled * mixing, axis=0, keepdims=True)
                col = jnp.sum(grad_mixing * mixing, axis=1, keepdims=True)
                sums = jnp.where(lane == h, col, sums)
            gs[b, :, cols] = jnp.where(low, halves[0], halves[1])
        gs_bf = grad_scores.astype(BF)
        gb[b] = dot(gs_bf, cm[...])
        gc[b] = dot(grad_scores.T.astype(BF), bm[...])
    cols_out[...] = sums.T[: 2 * HH]


def assemble(scal, got, s_first, p_second, decay, start, end, exact):
    first = scal[1]
    second = 1 - first
    for k in range(W // 128):
        cols = slice(k * 128, (k + 1) * 128)
        d_first, d_second = decay[first, 0:1, cols], decay[second, 0:1, cols]
        for r in range(N // PIECE):
            at = k * (N // PIECE) + r
            rows = slice(r * PIECE, (r + 1) * PIECE)
            s_in, e_in = got[at, 0:PIECE, :], got[at, PIECE : 2 * PIECE, :]
            start[first, rows, cols] = s_in
            end[second, rows, cols] = e_in
            s_f, e_f = s_in.astype(F32), e_in.astype(F32)
            s_next = d_first * s_f + s_first[rows, cols].astype(F32)
            e_next = d_second * e_f + p_second[rows, cols].astype(F32)
            start[second, rows, cols] = s_next.astype(BF)
            end[first, rows, cols] = e_next.astype(BF)
            if exact is not None:
                one = jnp.sum(s_f * e_next, axis=0, keepdims=True)
                two = jnp.sum(s_next * e_f, axis=0, keepdims=True)
                if r == 0:
                    sum_one, sum_two = one, two
                else:
                    sum_one, sum_two = sum_one + one, sum_two + two
        if exact is not None:
            exact[first, 0:1, cols] = sum_one
            exact[second, 0:1, cols] = sum_two


def head_map(shape, head_dim, chan_dim):
    return jnp.where(iota(shape, chan_dim) // HD == iota(shape, head_dim), 1.0, 0.0).astype(BF)


def pre_kernel(
    scal, got, s_first, p_second, decay, small, rows_in, cols_in, alog,
    xo, xp, yo, yp, bo, bp, co, cp, lo, lp,
    zed_out, msg,
    start, end, exact,
):
    assemble(scal, got, s_first, p_second, decay, start, end, exact)
    by_head = head_map((W, 128), 1, 0)
    sums = []
    joint = []
    for b, (x, y, bm, cm) in enumerate(((xo, yo, bo, co), (xp, yp, bp, cp))):
        for grad, mat, state in ((x, bm, end), (y, cm, start)):
            total = jnp.zeros((SPAN, 128), F32)
            for k in range(W // 256):
                cols = slice(k * 256, (k + 1) * 256)
                prod = dot(mat[...], state[b, :, cols]) * grad[:, cols].astype(F32)
                hi = prod.astype(BF)
                lo_part = (prod - hi.astype(F32)).astype(BF)
                total = total + dot(hi, by_head[cols]) + dot(lo_part, by_head[cols])
            sums.append(total.T[:HH])
        rows8 = jnp.concatenate(split3(exact[b, 0:1, :]) + [jnp.zeros((5, W), F32)], 0).astype(BF)
        joint.append(jnp.sum(dot_nt(head_map((HH, W), 0, 1), rows8), axis=1, keepdims=True))
    x_pulled = jnp.concatenate([sums[0], sums[2]], 0)
    y_state = jnp.concatenate([sums[1], sums[3]], 0)
    joint = jnp.concatenate(joint, 0)
    pre, step, cum = small[0], small[1], small[2]
    last = cum[:, SPAN - 1 :]
    rate = jnp.exp(alog[...])
    rate = jnp.concatenate([rate, rate], 0)
    q = jnp.exp(last - cum) * x_pulled
    cols = cols_in[...]
    u = rows_in[...] - step * cols + jnp.exp(cum) * y_state
    grad_log = (
        sum_by(u, triangle(lambda u, t: u >= t))
        + sum_by(step * q, triangle(lambda u, t: u < t))
        + jnp.exp(last) * joint
    )
    grad_step = cols + q - rate * grad_log
    grad_pre = grad_step * jax.nn.sigmoid(pre)
    for b in range(2):
        where = scal[1] if b == 0 else 1 - scal[1]
        zed_out[where] = grad_pre[b * HH : (b + 1) * HH].astype(BF)
    rolled = pltpu.roll(grad_pre, scal[2], 1).astype(BF)
    diagonal = iota((HH, 128), 0) == iota((HH, 128), 1)

    def as_row(v):
        v = v[:HH] + v[HH:]
        v = jnp.sum(v, axis=1, keepdims=True)
        return jnp.sum(jnp.where(diagonal, v, 0.0), axis=0, keepdims=True)

    extra = split3(as_row(grad_pre)) + split3(as_row(-grad_log * step))
    extra = jnp.concatenate(extra + [jnp.zeros((10, 128), F32)], 0).astype(BF)
    for k in range(D // 256):
        cols = slice(k * 256, (k + 1) * 256)
        part = dot(rolled[:HH], lo[:, cols]) + dot(rolled[HH:], lp[:, cols])
        for j in range(2):
            msg[2 * k + j, 0:HH, :] = part[:, j * 128 : (j + 1) * 128].astype(BF)
            msg[2 * k + j, HH : 2 * HH, :] = extra


def sum_kernel(msg, out, totals):
    total = jnp.zeros((2 * HH, 128), F32)
    for k in range(CHIPS):
        total = total + msg[k].astype(F32)
    rounded = total[:HH].astype(BF)
    for k in range(CHIPS):
        out[k] = rounded
    e = total[HH:]
    bias = e[0:1] + e[1:2] + e[2:3]
    rate = e[3:4] + e[4:5] + e[5:6]
    totals[...] = jnp.concatenate([bias, rate, jnp.zeros((6, 128), F32)], 0)


def grads_kernel(
    scal, got, s_first, p_second, decay, small, gs, gb, gc, maps,
    xo, xp, yo, yp, bo, bp, co, cp,
    gx_out, gb_out, gc_out,
    start, end,
):
    assemble(scal, got, s_first, p_second, decay, start, end, None)
    step, cum = small[1], small[2]
    remain = jnp.exp(cum[:, SPAN - 1 :] - cum)
    growth = jnp.exp(cum)
    for b, (x, y, bm, cm) in enumerate(((xo, yo, bo, co), (xp, yp, bp, cp))):
        rows = slice(b * HH, (b + 1) * HH)
        w_a = columns(remain[rows], growth[rows])
        w_b = columns(step[rows], step[rows])
        grad_b, grad_c = gb[b], gc[b]
        for k in range(W // 256):
            cols = slice(k * 256, (k + 1) * 256)
            wide = slice(W + k * 256, W + (k + 1) * 256)
            remain_w = dot(w_a, maps[:, cols])
            step_w = dot(w_b, maps[:, cols])
            growth_w = dot(w_a, maps[:, wide])
            pulled = dot(bm[...], end[b, :, cols])
            gx_out[b, :, cols] = (step_w * (gs[b, :, cols] + remain_w * pulled)).astype(BF)
            in_w = (remain_w * (step_w * x[:, cols].astype(F32))).astype(BF)
            out_w = (growth_w * y[:, cols].astype(F32)).astype(BF)
            grad_b = grad_b + dot_nt(in_w, end[b, :, cols])
            grad_c = grad_c + dot_nt(out_w, start[b, :, cols])
        gb_out[b] = grad_b.astype(BF)
        gc_out[b] = grad_c.astype(BF)


def weight_kernel(scal, own, other, out):
    first = scal[1]
    for j in range(CHIPS):
        a, b = own[j].astype(F32), other[j].astype(F32)
        low = jnp.where(first == 0, a, b)
        high = jnp.where(first == 0, b, a)
        out[j * 128 : (j + 1) * 128, :] = jnp.concatenate([low, high], 0).T


def call(kernel, outs, args, scratch=(), flops=0, moved=0, limit=40):
    vmem = pl.BlockSpec(memory_space=pltpu.VMEM)
    specs = [
        pl.BlockSpec(memory_space=pltpu.SMEM) if a.dtype == jnp.int32 else vmem for a in args
    ]
    return pl.pallas_call(
        kernel,
        out_shape=[jax.ShapeDtypeStruct(s, t) for s, t in outs],
        in_specs=specs,
        out_specs=[vmem] * len(outs),
        scratch_shapes=[pltpu.VMEM(s, t) for s, t in scratch],
        compiler_params=pltpu.CompilerParams(vmem_limit_bytes=limit * 2**20),
        cost_estimate=pl.CostEstimate(flops=flops, bytes_accessed=moved, transcendentals=0),
    )(*args)


def swap(v):
    return lax.ppermute(v, "core", [(0, 1), (1, 0)])


def local(layer_input, dt_weight, dt_bias, a_log, ssm_input, b_in, c_in, out_grad):
    core = lax.axis_index("core")
    tp = lax.axis_index("tp")
    scal = jnp.stack([32 * tp, core, (128 - 32 * tp) % 128]).astype(jnp.int32)

    def half(v, which, width, axis):
        return lax.dynamic_slice_in_dim(v, which * width, width, axis)

    pieces = [layer_input] + [
        lax.ppermute(layer_input, "tp", [((i + k) % TP, i) for i in range(TP)]) for k in (1, 3, 2)
    ]
    pieces = [pieces[0], pieces[1], pieces[3], pieces[2]]
    weight_t = dt_weight.T
    weight_mine = jnp.concatenate(
        [half(weight_t, core, HH, 0), half(weight_t, 1 - core, HH, 0)], 0
    )
    operands = []
    for v, width in ((ssm_input, W), (out_grad, W), (b_in, N), (c_in, N)):
        operands += [half(v, core, width, 1), swap(half(v, 1 - core, width, 1))]
    bias = jnp.broadcast_to(half(dt_bias, core, HH, 0)[:, None], (HH, 128))
    alog = jnp.broadcast_to(half(a_log, core, HH, 0)[:, None], (HH, 128))
    maps = spread_maps()

    proj_own, proj_other = call(
        project_kernel, [((HH, 128), F32)] * 2, [scal, weight_mine] + pieces, flops=2**26, moved=2**21
    )
    proj_other = swap(proj_other)
    msg, s_first, p_second, small, decay = call(
        state_kernel,
        [
            ((CHIPS, 2 * PIECE + 16, 128), BF),
            ((N, W), BF),
            ((N, W), BF),
            ((3, 2 * HH, 128), F32),
            ((2, 8, W), F32),
        ],
        [scal, proj_own, proj_other, bias, alog] + operands + [maps],
        [((2, N, W), F32), ((2, N, W), F32)],
        flops=2**28,
        moved=2**22,
    )
    got = lax.all_to_all(msg, "chip", 0, 0, tiled=True)

    weight_t, _ = lax.optimization_barrier((weight_t, small))
    weight_all = lax.all_gather(weight_t, "tp", axis=0, tiled=True)
    rows_own = jnp.concatenate(pieces, 0)
    rows_other = swap(rows_own)
    gs, gb, gc, row_sums, col_sums = call(
        intra_kernel,
        [((2, SPAN, W), F32), ((2, SPAN, N), F32), ((2, SPAN, N), F32)] + [((2 * HH, 128), F32)] * 2,
        [small] + operands,
        flops=2**33,
        moved=2**22,
    )

    (folded,) = call(
        fold_kernel, [((CHIPS, 2 * PIECE, 128), BF)], [got], flops=2**20, moved=2**20
    )
    states = lax.all_to_all(folded, "chip", 0, 0, tiled=True)

    zed, parts = call(
        pre_kernel,
        [((2, HH, 128), BF), ((CHIPS, 2 * HH, 128), BF)],
        [scal, states, s_first, p_second, decay, small, row_sums, col_sums, alog]
        + operands
        + [rows_own, rows_other],
        [((2, N, W), BF), ((2, N, W), BF), ((2, 8, W), F32)],
        flops=2**29,
        moved=2**23,
    )
    shares = lax.all_to_all(parts, "chip", 0, 0, tiled=True)
    zed = jnp.transpose(zed.reshape(CORES, HH, TP, 32), (0, 2, 1, 3)).reshape(CORES * TP, HH, 32)
    zed = lax.all_to_all(zed, ("core", "tp"), 0, 0, tiled=True)
    zed = jnp.transpose(zed.reshape(CORES, TP, HH, 32), (3, 1, 0, 2)).reshape(32, TP * CORES * HH)
    grad_layer_input = dot(zed, weight_all).astype(BF)

    gx, gb, gc = call(
        grads_kernel,
        [((2, SPAN, W), BF), ((2, SPAN, N), BF), ((2, SPAN, N), BF)],
        [scal, states, s_first, p_second, decay, small, gs, gb, gc, maps] + operands,
        [((2, N, W), BF), ((2, N, W), BF)],
        flops=2**32,
        moved=2**23,
    )

    def join(mine, other, axis):
        return jnp.where(
            core == 0,
            jnp.concatenate([mine, other], axis),
            jnp.concatenate([other, mine], axis),
        )

    grad_ssm_input = join(gx[0], swap(gx[1]), 1)
    grad_b_in = join(gb[0], swap(gb[1]), 1)
    grad_c_in = join(gc[0], swap(gc[1]), 1)

    total, totals = call(
        sum_kernel, [((CHIPS, HH, 128), BF), ((8, 128), F32)], [shares], flops=2**20, moved=2**20
    )
    weight_own = lax.all_to_all(total, "chip", 0, 0, tiled=True)
    totals = join(totals[:2, :HH], swap(totals[:2, :HH]), 1)
    grad_dt_bias = totals[0]
    grad_a_log = jnp.exp(a_log) * totals[1]
    (grad_dt_weight,) = call(
        weight_kernel,
        [((D, 2 * HH), F32)],
        [scal, weight_own, swap(weight_own)],
        flops=2**20,
        moved=2**22,
    )
    return (
        grad_ssm_input,
        grad_b_in,
        grad_c_in,
        grad_layer_input,
        grad_dt_weight,
        grad_dt_bias,
        grad_a_log,
    )


def solution(mesh):
    fine = Mesh(mesh.devices.reshape(CHIPS, CORES, TP), ("chip", "core", "tp"))
    ctx = ("chip", "core")
    everything = ("chip", "core", "tp")
    placed = (
        P(everything, None),
        P(None, "tp"),
        P("tp"),
        P("tp"),
        P(ctx, "tp"),
        P(ctx, "tp"),
        P(ctx, "tp"),
        P(ctx, "tp"),
    )
    return jax.shard_map(
        local,
        mesh=fine,
        in_specs=placed,
        out_specs=(
            P(ctx, "tp"),
            P(ctx, "tp"),
            P(ctx, "tp"),
            P(everything, None),
            P(None, "tp"),
            P("tp"),
            P("tp"),
        ),
        check_vma=False,
    )
```

time: 899 us -> 159 us (0.18)
  waiting for transfers between devices: 345 us -> 42.2 us
  other arithmetic: 198 us -> 4.35 us
  blocking collectives: 173 us -> 0 us
  local copies, waits for them, and re-layouts: 136 us -> 23 us
  starting transfers between devices: 0.2 us -> 52.5 us
  Pallas kernels: 0 us -> 19 us
  matrix products: 21.2 us -> 2.24 us
    all_gather x3 -> x1, waiting for transfers between devices: 266 us -> 0.02 us  [local(): weight_all = lax.all_gather(weight_t, 'tp', axis=0, tiled=True)]
    select_n x128 -> x4, other arithmetic: 189 us -> 3.32 us  [join(): jnp.where(core == 0, jnp.concatenate([mine, other], axis), jnp.concatenat...]
    psum x1 -> x0, blocking collectives: 124 us -> none  [local(): lax.psum((weight_part, bias_part, rate_part), 'ctx')]
    mul x128 -> x0, local copies, waits for them, and re-layouts: 121 us -> none  [chain_combine(): latter[0][:, :, None, None] * earlier[1] + latter[1]]
    psum x1 -> x0, waiting for transfers between devices: 78.5 us -> none  [local(): lax.psum((weight_part, bias_part, rate_part), 'ctx')]
    all_gather x1 -> x0, blocking collectives: 48.9 us -> none  [entering(): everything = jax.tree.map(lambda part: lax.all_gather(part, axis), value)]
    all_to_all x0 -> x5, waiting for transfers between devices: none -> 32.8 us  [the longest x1 14.8 us: local(): got = lax.all_to_all(msg, 'chip', 0, 0, tiled=True)]
    all_to_all x0 -> x5, starting transfers between devices: none -> 32 us  [the longest x1 11 us: local(): got = lax.all_to_all(msg, 'chip', 0, 0, tiled=True)]
  transfers between devices with their start and end apart: 5 -> 20, of which waited for: 4 -> 9; matrix products, arithmetic and copies ran while one was open for 22% -> 8% of each run, Pallas kernels for 0% -> 9%
where the time goes in v1:
time: 159 us; the launch traced here: 158 us
  starting transfers between devices  52.5 us (33%)
  waiting for transfers between devices  42.2 us (27%)
  local copies, waits for them, and re-layouts  23 us (14%)
  Pallas kernels  19 us (12%)
  between operations  14.5 us (9%)
  other arithmetic  4.35 us (3%)
  matrix products  2.24 us (1%)
    unnamed x90, local copies, waits for them, and re-layouts  19.2 us
    pallas_call x8, Pallas kernels, call(): pl.pallas_call(kernel, out_shape=[jax.ShapeDtypeStruct(s, t) for s, t in...  19 us
    ppermute x11, starting transfers between devices, swap(): return lax.ppermute(v, 'core', [(0, 1), (1, 0)])  15.7 us
    all_to_all x1, waiting for transfers between devices, local(): got = lax.all_to_all(msg, 'chip', 0, 0, tiled=True)  14.8 us
    all_to_all x1, starting transfers between devices, local(): got = lax.all_to_all(msg, 'chip', 0, 0, tiled=True)  11 us
    ppermute x3, waiting for transfers between devices, local(): lax.ppermute(layer_input, 'tp', [((i + k) % TP, i) for i in range(TP)])  8.56 us
    all_to_all x1, waiting for transfers between devices, local(): weight_own = lax.all_to_all(total, 'chip', 0, 0, tiled=True)  8.54 us
    all_to_all x1, starting transfers between devices, local(): states = lax.all_to_all(folded, 'chip', 0, 0, tiled=True)  8.15 us
  transfers between devices with their start and end apart: 20, of which 9 were waited for; matrix products, arithmetic and copies ran while one was open for 8% of the time, Pallas kernels for 9%

profile of v1, /device:TPU:1, one launch (start us, length us, event | category | flops | bytes accessed | tf_op | source)
XLA Modules:
  0.0 157.8 jit_solution(12469802587360380585)
XLA Ops:
  7.2 3.6 %collective-permute-start = (bf16[32,4096]{1,0:T(8,128)(2,1)}, bf16[32,4096]{1,0:T(8,128)(2,1)S(1)}, u32[]{:S(2)}, u32[]{:S(2)}) collective-permute-start(bf16[32,4096]{1,0:T(8,128)(2,1)} %l0.1), channel_id=1, source_target_pairs={{1,0},{2,1},{3,2},{0,3},{5,4},{6,5},{7,6},{4,7},{9,8},{10,9},{11,1... | collective-permute-start | bytes 786440 | tf_op jit(solution)/shard_map/ppermute | solution.py:340
  10.8 0.3 collective-permute-start.1
  11.2 0.7 collective-permute-start.2
  11.9 1.1 constant_dynamic-slice_fusion.6
  13.0 1.6 %collective-permute-start.4 = (bf16[128,1024]{1,0:T(8,128)(2,1)S(1)}, bf16[128,1024]{1,0:T(8,128)(2,1)S(1)}, u32[]{:S(2)}, u32[]{:S(2)}) collective-permute-start(bf16[128,1024]{1,0:T(8,128)(2,1)S(1)} %get-tuple-element.72), channel_id=1, source_target_pairs={{0,4},{4,0},{1,5},{5,1},{2,6},{6,2},{3,7},{7,3},{8,12},{12,8},{9,1... | collective-permute-start | bytes 786440 | tf_op jit(solution)/shard_map/ppermute | solution.py:328
  14.6 1.1 constant_dynamic-slice_fusion.4
  16.1 5.6 %collective-permute-done.l1 = bf16[32,4096]{1,0:T(8,128)(2,1)S(1)} collective-permute-done((bf16[32,4096]{1,0:T(8,128)(2,1)}, bf16[32,4096]{1,0:T(8,128)(2,1)S(1)}, u32[]{:S(2)}, u32[]{:S(2)}) %collective-permute-start) | collective-permute-done | bytes 262176 | tf_op jit(solution)/shard_map/ppermute | solution.py:340
  21.6 1.7 %collective-permute-start.6 = (bf16[128,128]{1,0:T(8,128)(2,1)S(1)}, bf16[128,128]{1,0:T(8,128)(2,1)S(1)}, u32[]{:S(2)}, u32[]{:S(2)}) collective-permute-start(bf16[128,128]{1,0:T(8,128)(2,1)S(1)} %get-tuple-element.82), channel_id=1, source_target_pairs={{0,4},{4,0},{1,5},{5,1},{2,6},{6,2},{3,7},{7,3},{8,12},{12,8},{9,1... | collective-permute-start | bytes 98312 | tf_op jit(solution)/shard_map/ppermute | solution.py:328
  23.4 3.0 %collective-permute-done.2.l3 = bf16[32,4096]{1,0:T(8,128)(2,1)S(1)} collective-permute-done((bf16[32,4096]{1,0:T(8,128)(2,1)}, bf16[32,4096]{1,0:T(8,128)(2,1)S(1)}, u32[]{:S(2)}, u32[]{:S(2)}) %collective-permute-start.2) | collective-permute-done | bytes 262176 | tf_op jit(solution)/shard_map/ppermute | solution.py:340
  26.4 1.0 shard_map.135
  27.5 0.5 collective-permute-start.3
  28.0 0.4 select_convert_fusion.maps
  29.0 2.8 %shard_map.136 = (bf16[32,80,128]{2,1,0:T(8,128)(2,1)}, bf16[128,1024]{1,0:T(8,128)(2,1)S(1)}, bf16[128,1024]{1,0:T(8,128)(2,1)S(1)}, f32[3,32,128]{2,1,0:T(8,128)S(1)}, f32[2,8,1024]{2,1,0:T(8,128)S(1)}) custom-call(s32[3]{0:T(128)S(1)} %pad_add_fusion.scal, f32[16,128]{1,0:T(8,128)S(1)} %get-tuple-element.27.po, f32[16,128]{1,0:T(8,128)S(1)} %collective-permute-done.3.pp, ...), custom_call_target="tpu_custom_call" | custom-call | flops 268435456 | bytes 4194304 | tf_op jit(solution)/shard_map/pallas_call | solution.py:316
  31.8 0.7 copy-done.10
  32.5 0.7 copy-done.12
  33.2 0.6 copy-done.20
  33.8 11.0 %all-to-all-start = ((bf16[32,80,128]{2,1,0:T(8,128)(2,1)}), bf16[32,80,128]{2,1,0:T(8,128)(2,1)S(1)}, u32[]{:S(2)}, u32[]{:S(2)}) async-start(bf16[32,80,128]{2,1,0:T(8,128)(2,1)} %get-tuple-element.29), calls=%async_computation | async-start | bytes 1310720 | tf_op jit(solution)/shard_map/all_to_all | solution.py:372
  44.9 1.0 constant_dynamic-update-slice_fusion.2
  45.9 1.0 constant_dynamic-update-slice_fusion.1
  46.9 14.8 %all-to-all-done.msg = bf16[32,80,128]{2,1,0:T(8,128)(2,1)S(1)} async-done(((bf16[32,80,128]{2,1,0:T(8,128)(2,1)}), bf16[32,80,128]{2,1,0:T(8,128)(2,1)S(1)}, u32[]{:S(2)}, u32[]{:S(2)}) %all-to-all-start) | async-done | bytes 655392 | tf_op jit(solution)/shard_map/all_to_all | solution.py:372
  61.7 0.9 shard_map.137
  62.6 8.2 %all-to-all-start.1 = ((bf16[32,64,128]{2,1,0:T(8,128)(2,1)}), bf16[32,64,128]{2,1,0:T(8,128)(2,1)S(1)}, u32[]{:S(2)}, u32[]{:S(2)}) async-start(bf16[32,64,128]{2,1,0:T(8,128)(2,1)} %shard_map.137), calls=%async_computation.1 | async-start | bytes 1048576 | tf_op jit(solution)/shard_map/all_to_all | solution.py:389
  70.9 1.5 collective-permute-start.11
  72.4 0.7 copy-done.6
  73.2 0.8 copy-done.8
  73.9 0.8 copy-done.16
  74.7 0.8 copy-done.18
  75.5 0.8 copy-done.25
  76.3 4.4 %shard_map.138 = (f32[2,128,1024]{2,1,0:T(8,128)S(1)}, f32[2,128,128]{2,1,0:T(8,128)S(1)}, f32[2,128,128]{2,1,0:T(8,128)S(1)}, f32[32,128]{1,0:T(8,128)S(1)}, f32[32,128]{1,0:T(8,128)S(1)}) custom-call(f32[3,32,128]{2,1,0:T(8,128)S(1)} %copy-done.25, bf16[128,1024]{1,0:T(8,128)(2,1)S(1)} %get-tuple-element.73.xo, ...), custom_call_target="tpu_custom_call" | custom-call | flops 8589934592 | bytes 4194304 | tf_op jit(solution)/shard_map/pallas_call | solution.py:316
  80.6 0.6 copy-done.27
  81.2 0.6 copy-done.29
  81.8 1.0 copy-done.31
  82.8 0.7 copy-done.33
  83.5 0.7 copy-done.35
  84.1 0.8 all-to-all-done.1.got
  84.9 0.9 copy-done.13
  85.9 0.8 copy-done.21
  86.7 0.8 copy-done.26
  87.5 1.2 copy-done.32
  88.7 0.9 copy-done.34
  89.6 0.9 copy-done.36
  90.5 2.4 %shard_map.139 = (bf16[2,128,1024]{2,1,0:T(8,128)(2,1)S(1)}, bf16[2,128,128]{2,1,0:T(8,128)(2,1)S(1)}, bf16[2,128,128]{2,1,0:T(8,128)(2,1)S(1)}) custom-call(s32[3]{0:T(128)S(1)} %pad_add_fusion.scal, bf16[32,64,128]{2,1,0:T(8,128)(2,1)S(1)} %all-to-all-done.1.got, bf16[128,1024]{1,0:T(8,128)(2,1)S(1)} %copy-done.11, bf16[128,1024]{1,0:T(8,128)(2,1)S(1)} %copy-done.13, ...), custom_call_target="tpu_custom_call" | custom-call | flops 4294967296 | bytes 8388608 | tf_op jit(solution)/shard_map/pallas_call | solution.py:316
  93.0 0.7 slice_bitcast_fusion.1
  93.7 4.1 %collective-permute-start.8 = (bf16[128,1024]{1,0:T(8,128)(2,1)}, bf16[128,1024]{1,0:T(8,128)(2,1)}, u32[]{:S(2)}, u32[]{:S(2)}) collective-permute-start(bf16[128,1024]{1,0:T(8,128)(2,1)} %get-tuple-element.69), channel_id=1, source_target_pairs={{0,4},{4,0},{1,5},{5,1},{2,6},{6,2},{3,7},{7,3},{8,12},{12,8},{9,1... | collective-permute-start | bytes 786440 | tf_op jit(solution)/shard_map/ppermute | solution.py:328
  98.0 5.9 %shard_map.140 = (bf16[2,16,128]{2,1,0:T(8,128)(2,1)S(1)}, bf16[32,32,128]{2,1,0:T(8,128)(2,1)}) custom-call(s32[3]{0:T(128)S(1)} %pad_add_fusion.scal, bf16[32,64,128]{2,1,0:T(8,128)(2,1)S(1)} %all-to-all-done.1.got, bf16[128,1024]{1,0:T(8,128)(2,1)S(1)} %copy-done.11, bf16[128,1024]{1,0:T(8,128)(2,1)S(1)} %copy-done.14, f32[2,8,1024]{2,1,0:T(8,128)S(1)} %copy-done.21, ...), custom_call_target="tpu_custom_call" | custom-call | flops 536870912 | bytes 8388608 | tf_op jit(solution)/shard_map/pallas_call | solution.py:316
  104.0 0.7 reshape.29
  104.7 3.7 %all-to-all-start.2 = ((bf16[8,2,256]{2,1,0:T(2,128)(2,1)}), bf16[8,2,256]{2,1,0:T(2,128)(2,1)S(1)}, u32[]{:S(2)}, u32[]{:S(2)}) async-start(bf16[8,2,256]{2,1,0:T(2,128)(2,1)} %reshape.29), calls=%async_computation.2 | async-start | bytes 16384 | tf_op jit(solution)/shard_map/all_to_all | solution.py:403
  108.5 4.7 %all-to-all-done.2 = bf16[8,2,256]{2,1,0:T(2,128)(2,1)S(1)} async-done(((bf16[8,2,256]{2,1,0:T(2,128)(2,1)}), bf16[8,2,256]{2,1,0:T(2,128)(2,1)S(1)}, u32[]{:S(2)}, u32[]{:S(2)}) %all-to-all-start.2) | async-done | bytes 8224 | tf_op jit(solution)/shard_map/all_to_all | solution.py:403
  113.2 5.0 %all-to-all-start.3 = ((bf16[32,32,128]{2,1,0:T(8,128)(2,1)}), bf16[32,32,128]{2,1,0:T(8,128)(2,1)S(1)}, u32[]{:S(2)}, u32[]{:S(2)}) async-start(bf16[32,32,128]{2,1,0:T(8,128)(2,1)} %get-tuple-element.44), calls=%async_computation.3 | async-start | bytes 524288 | tf_op jit(solution)/shard_map/all_to_all | solution.py:401
  118.4 2.2 %convolution_convert_fusion = bf16[32,4096]{1,0:T(8,128)(2,1)} fusion(bf16[32,128]{0,1:T(8,128)(2,1)S(1)} %bitcast.34, bf16[128,4096]{1,0:T(8,128)(2,1)} %all-gather.2.cloned.1.call-done), kind=kOutput, calls=%fused_computation | convolution fusion | flops 33685504 | bytes 1318912 | tf_op jit(solution)/shard_map/dot_general | solution.py:22
  120.6 0.6 maximum_select_fusion.1
  121.3 0.6 maximum_select_fusion.2
  121.9 1.9 %maximum_select_fusion = bf16[128,2048]{1,0:T(8,128)(2,1)} fusion(bf16[128,1024]{1,0:T(8,128)(2,1)} %collective-permute-done.8, bf16[128,1024]{1,0:T(8,128)(2,1)S(1)} %get-tuple-element.68, pred[]{:T(512)S(6)} %eq.21), kind=kLoop, calls=%fused_computation.17 | loop fusion | flops 2359296 | bytes 1048577 | tf_op jit(solution)/shard_map/jit(_where)/select_n | solution.py:417
  123.9 4.1 %all-to-all-done.3.msg = bf16[32,32,128]{2,1,0:T(8,128)(2,1)S(1)} async-done(((bf16[32,32,128]{2,1,0:T(8,128)(2,1)}), bf16[32,32,128]{2,1,0:T(8,128)(2,1)S(1)}, u32[]{:S(2)}, u32[]{:S(2)}) %all-to-all-start.3) | async-done | bytes 262176 | tf_op jit(solution)/shard_map/all_to_all | solution.py:401
  127.9 0.7 shard_map.141
  128.6 3.7 %collective-permute-start.13 = (f32[2,16]{1,0:T(2,128)S(1)}, f32[2,16]{1,0:T(2,128)S(1)}, u32[]{:S(2)}, u32[]{:S(2)}) collective-permute-start(f32[2,16]{1,0:T(2,128)S(1)} %slice.50), channel_id=1, source_target_pairs={{0,4},{4,0},{1,5},{5,1},{2,6},{6,2},{3,7},{7,3},{8,12},{12,8},{9,1... | collective-permute-start | bytes 392 | tf_op jit(solution)/shard_map/ppermute | solution.py:328
  132.3 4.1 %all-to-all-start.4 = ((bf16[32,16,128]{2,1,0:T(8,128)(2,1)}), bf16[32,16,128]{2,1,0:T(8,128)(2,1)S(1)}, u32[]{:S(2)}, u32[]{:S(2)}) async-start(bf16[32,16,128]{2,1,0:T(8,128)(2,1)} %get-tuple-element.45), calls=%async_computation.4 | async-start | bytes 262144 | tf_op jit(solution)/shard_map/all_to_all | solution.py:430
  136.6 0.5 bitcast_multiply_fusion
  137.1 8.5 %all-to-all-done.4.own = bf16[32,16,128]{2,1,0:T(8,128)(2,1)S(1)} async-done(((bf16[32,16,128]{2,1,0:T(8,128)(2,1)}), bf16[32,16,128]{2,1,0:T(8,128)(2,1)S(1)}, u32[]{:S(2)}, u32[]{:S(2)}) %all-to-all-start.4) | async-done | bytes 131104 | tf_op jit(solution)/shard_map/all_to_all | solution.py:430
  145.6 2.1 %collective-permute-start.12 = (bf16[32,16,128]{2,1,0:T(8,128)(2,1)S(1)}, bf16[32,16,128]{2,1,0:T(8,128)(2,1)S(1)}, u32[]{:S(2)}, u32[]{:S(2)}) collective-permute-start(bf16[32,16,128]{2,1,0:T(8,128)(2,1)S(1)} %all-to-all-done.4.own), channel_id=1, source_target_pairs={{0,4},{4,0},{1,5},{5,1},{2,6},{6,2},{3,7},{7,3},{8,12},{12,8},{9,1... | collective-permute-start | bytes 393224 | tf_op jit(solution)/shard_map/ppermute | solution.py:328
  147.7 0.5 slice_bitcast_fusion.6
  148.2 0.5 collective-permute-done.12.other
  148.7 0.9 shard_map.142
  149.6 1.4 copy.18
  (108 shorter events, 1.8 us)
Async XLA Ops:
  7.2 19.2 %copy-start = (bf16[32,4096]{1,0:T(8,128)(2,1)S(1)}, bf16[32,4096]{1,0:T(8,128)(2,1)}, u32[]{:S(2)}) copy-start(bf16[32,4096]{1,0:T(8,128)(2,1)} %l0.1) | copy-start | bytes 786436
  7.2 8.7 %copy-start.37 = (bf16[4096,32]{0,1:T(8,128)(2,1)S(1)}, bf16[4096,32]{0,1:T(8,128)(2,1)}, u32[]{:S(2)}) copy-start(bf16[4096,32]{0,1:T(8,128)(2,1)} %param.9) | copy-start | bytes 786436
  7.2 8.8 %copy-start.38 = (bf16[128,256]{1,0:T(8,128)(2,1)S(1)}, bf16[128,256]{1,0:T(8,128)(2,1)}, u32[]{:S(2)}) copy-start(bf16[128,256]{1,0:T(8,128)(2,1)} %param.13) | copy-start | bytes 196612
  7.2 8.8 %copy-start.39 = (bf16[128,256]{1,0:T(8,128)(2,1)S(1)}, bf16[128,256]{1,0:T(8,128)(2,1)}, u32[]{:S(2)}) copy-start(bf16[128,256]{1,0:T(8,128)(2,1)} %param.14) | copy-start | bytes 196612
  7.2 14.4 %collective-permute-start = (bf16[32,4096]{1,0:T(8,128)(2,1)}, bf16[32,4096]{1,0:T(8,128)(2,1)S(1)}, u32[]{:S(2)}, u32[]{:S(2)}) collective-permute-start(bf16[32,4096]{1,0:T(8,128)(2,1)} %l0.1), channel_id=1, source_target_pairs={{1,0},{2,1},{3,2},{0,3},{5,4},{6,5},{7,6},{4,7},{9,8},{10,9},{11,1... | collective-permute-start | bytes 786440 | tf_op jit(solution)/shard_map/ppermute | solution.py:340
  10.8 12.5 %collective-permute-start.1 = (bf16[32,4096]{1,0:T(8,128)(2,1)}, bf16[32,4096]{1,0:T(8,128)(2,1)S(1)}, u32[]{:S(2)}, u32[]{:S(2)}) collective-permute-start(bf16[32,4096]{1,0:T(8,128)(2,1)} %l0.1), channel_id=1, source_target_pairs={{2,0},{3,1},{0,2},{1,3},{6,4},{7,5},{4,6},{5,7},{10,8},{11,9},{8,1... | collective-permute-start | bytes 786440 | tf_op jit(solution)/shard_map/ppermute | solution.py:340
  11.2 15.2 %collective-permute-start.2 = (bf16[32,4096]{1,0:T(8,128)(2,1)}, bf16[32,4096]{1,0:T(8,128)(2,1)S(1)}, u32[]{:S(2)}, u32[]{:S(2)}) collective-permute-start(bf16[32,4096]{1,0:T(8,128)(2,1)} %l0.1), channel_id=1, source_target_pairs={{3,0},{0,1},{1,2},{2,3},{7,4},{4,5},{5,6},{6,7},{11,8},{8,9},{9,10... | collective-permute-start | bytes 786440 | tf_op jit(solution)/shard_map/ppermute | solution.py:340
  13.0 15.4 %copy-start.40 = (f32[32]{0:T(128)S(1)}, f32[32]{0:T(128)}, u32[]{:S(2)}) copy-start(f32[32]{0:T(128)} %param.10) | copy-start | bytes 388
  13.0 15.5 %copy-start.41 = (f32[32]{0:T(128)S(1)}, f32[32]{0:T(128)}, u32[]{:S(2)}) copy-start(f32[32]{0:T(128)} %param.11) | copy-start | bytes 388
  13.0 15.6 %collective-permute-start.4 = (bf16[128,1024]{1,0:T(8,128)(2,1)S(1)}, bf16[128,1024]{1,0:T(8,128)(2,1)S(1)}, u32[]{:S(2)}, u32[]{:S(2)}) collective-permute-start(bf16[128,1024]{1,0:T(8,128)(2,1)S(1)} %get-tuple-element.72), channel_id=1, source_target_pairs={{0,4},{4,0},{1,5},{5,1},{2,6},{6,2},{3,7},{7,3},{8,12},{12,8},{9,1... | collective-permute-start | bytes 786440 | tf_op jit(solution)/shard_map/ppermute | solution.py:328
  15.7 12.9 %collective-permute-start.5 = (bf16[128,1024]{1,0:T(8,128)(2,1)S(1)}, bf16[128,1024]{1,0:T(8,128)(2,1)S(1)}, u32[]{:S(2)}, u32[]{:S(2)}) collective-permute-start(bf16[128,1024]{1,0:T(8,128)(2,1)S(1)} %get-tuple-element.70), channel_id=1, source_target_pairs={{0,4},{4,0},{1,5},{5,1},{2,6},{6,2},{3,7},{7,3},{8,12},{12,8},{9,1... | collective-permute-start | bytes 786440 | tf_op jit(solution)/shard_map/ppermute | solution.py:328
  16.0 17.1 %copy-start.5 = (bf16[128,128]{1,0:T(8,128)(2,1)}, bf16[128,128]{1,0:T(8,128)(2,1)S(1)}, u32[]{:S(2)}) copy-start(bf16[128,128]{1,0:T(8,128)(2,1)S(1)} %get-tuple-element.83.bo) | copy-start | bytes 98308
  16.1 17.1 %copy-start.7 = (bf16[128,128]{1,0:T(8,128)(2,1)}, bf16[128,128]{1,0:T(8,128)(2,1)S(1)}, u32[]{:S(2)}) copy-start(bf16[128,128]{1,0:T(8,128)(2,1)S(1)} %get-tuple-element.81.co) | copy-start | bytes 98308
  21.6 11.6 %copy-start.3 = (bf16[32,4096]{1,0:T(8,128)(2,1)}, bf16[32,4096]{1,0:T(8,128)(2,1)S(1)}, u32[]{:S(2)}) copy-start(bf16[32,4096]{1,0:T(8,128)(2,1)S(1)} %collective-permute-done.l1) | copy-start | bytes 786436
  21.6 6.9 %collective-permute-start.6 = (bf16[128,128]{1,0:T(8,128)(2,1)S(1)}, bf16[128,128]{1,0:T(8,128)(2,1)S(1)}, u32[]{:S(2)}, u32[]{:S(2)}) collective-permute-start(bf16[128,128]{1,0:T(8,128)(2,1)S(1)} %get-tuple-element.82), channel_id=1, source_target_pairs={{0,4},{4,0},{1,5},{5,1},{2,6},{6,2},{3,7},{7,3},{8,12},{12,8},{9,1... | collective-permute-start | bytes 98312 | tf_op jit(solution)/shard_map/ppermute | solution.py:328
  23.3 4.7 %copy-start.4 = (bf16[32,4096]{1,0:T(8,128)(2,1)}, bf16[32,4096]{1,0:T(8,128)(2,1)S(1)}, u32[]{:S(2)}) copy-start(bf16[32,4096]{1,0:T(8,128)(2,1)S(1)} %collective-permute-done.1.l2) | copy-start | bytes 786436
  23.3 5.2 %collective-permute-start.7 = (bf16[128,128]{1,0:T(8,128)(2,1)S(1)}, bf16[128,128]{1,0:T(8,128)(2,1)S(1)}, u32[]{:S(2)}, u32[]{:S(2)}) collective-permute-start(bf16[128,128]{1,0:T(8,128)(2,1)S(1)} %get-tuple-element.80), channel_id=1, source_target_pairs={{0,4},{4,0},{1,5},{5,1},{2,6},{6,2},{3,7},{7,3},{8,12},{12,8},{9,1... | collective-permute-start | bytes 98312 | tf_op jit(solution)/shard_map/ppermute | solution.py:328
  26.4 6.8 %copy-start.1 = (bf16[32,4096]{1,0:T(8,128)(2,1)}, bf16[32,4096]{1,0:T(8,128)(2,1)S(1)}, u32[]{:S(2)}) copy-start(bf16[32,4096]{1,0:T(8,128)(2,1)S(1)} %collective-permute-done.2.l3) | copy-start | bytes 786436
  27.5 1.4 collective-permute-start.3
  28.5 4.7 %copy-start.15 = (bf16[128,128]{1,0:T(8,128)(2,1)}, bf16[128,128]{1,0:T(8,128)(2,1)S(1)}, u32[]{:S(2)}) copy-start(bf16[128,128]{1,0:T(8,128)(2,1)S(1)} %collective-permute-done.6.bp) | copy-start | bytes 98308
  28.5 4.7 %copy-start.17 = (bf16[128,128]{1,0:T(8,128)(2,1)}, bf16[128,128]{1,0:T(8,128)(2,1)S(1)}, u32[]{:S(2)}) copy-start(bf16[128,128]{1,0:T(8,128)(2,1)S(1)} %collective-permute-done.7.cp) | copy-start | bytes 98308
  31.8 0.7 copy-start.10
  32.5 0.7 copy-start.12
  33.2 0.6 copy-start.20
  33.2 0.6 copy-start.24
  33.8 27.9 %all-to-all-start = ((bf16[32,80,128]{2,1,0:T(8,128)(2,1)}), bf16[32,80,128]{2,1,0:T(8,128)(2,1)S(1)}, u32[]{:S(2)}, u32[]{:S(2)}) async-start(bf16[32,80,128]{2,1,0:T(8,128)(2,1)} %get-tuple-element.29), calls=%async_computation | async-start | bytes 1310720 | tf_op jit(solution)/shard_map/all_to_all | solution.py:372
  44.9 26.0 %copy-start.2 = (bf16[32,4096]{1,0:T(8,128)(2,1)S(1)}, bf16[32,4096]{1,0:T(8,128)(2,1)}, u32[]{:S(2)}) copy-start(bf16[32,4096]{1,0:T(8,128)(2,1)} %copy-done.1) | copy-start | bytes 786436
  62.6 22.3 %all-to-all-start.1 = ((bf16[32,64,128]{2,1,0:T(8,128)(2,1)}), bf16[32,64,128]{2,1,0:T(8,128)(2,1)S(1)}, u32[]{:S(2)}, u32[]{:S(2)}) async-start(bf16[32,64,128]{2,1,0:T(8,128)(2,1)} %shard_map.137), calls=%async_computation.1 | async-start | bytes 1048576 | tf_op jit(solution)/shard_map/all_to_all | solution.py:389
  70.8 47.6 %all-gather.2.cloned.1.call-start = ((), (), s32[]{:S(2)}) async-start(), calls=%async_computation.5 | async-start | bytes 1310720 | tf_op jit(solution)/shard_map/all_gather | solution.py:375
  70.9 27.1 %collective-permute-start.11 = (bf16[128,4096]{1,0:T(8,128)(2,1)S(1)}, bf16[128,4096]{1,0:T(8,128)(2,1)}, u32[]{:S(2)}, u32[]{:S(2)}) collective-permute-start(bf16[128,4096]{1,0:T(8,128)(2,1)S(1)} %constant_dynamic-update-slice_fusion.lo), channel_id=1, source_target_pairs={{0,4},{4,0},{1,5},{5,1},{2,6},{6,2},{3,7},{7,3},{8,12},{12,8},{9,1... | collective-permute-start | bytes 3145736 | tf_op jit(solution)/shard_map/ppermute | solution.py:328
  72.4 0.8 copy-start.6
  73.2 0.8 copy-start.8
  73.9 0.8 copy-start.16
  74.7 0.8 copy-start.18
  75.5 0.8 copy-start.25
  76.3 8.6 %copy-start.9 = (bf16[128,128]{1,0:T(8,128)(2,1)S(1)}, bf16[128,128]{1,0:T(8,128)(2,1)}, u32[]{:S(2)}) copy-start(bf16[128,128]{1,0:T(8,128)(2,1)} %copy-done.7) | copy-start | bytes 98308
  76.3 8.6 %copy-start.11 = (bf16[128,1024]{1,0:T(8,128)(2,1)S(1)}, bf16[128,1024]{1,0:T(8,128)(2,1)}, u32[]{:S(2)}) copy-start(bf16[128,1024]{1,0:T(8,128)(2,1)} %copy-done.10) | copy-start | bytes 786436
  76.3 8.6 %copy-start.19 = (bf16[128,128]{1,0:T(8,128)(2,1)S(1)}, bf16[128,128]{1,0:T(8,128)(2,1)}, u32[]{:S(2)}) copy-start(bf16[128,128]{1,0:T(8,128)(2,1)} %copy-done.17) | copy-start | bytes 98308
  80.6 0.6 copy-start.27
  81.2 0.6 copy-start.29
  81.8 1.0 copy-start.31
  82.8 0.7 copy-start.33
  83.5 0.7 copy-start.35
  84.9 1.0 copy-start.13
  85.9 0.8 copy-start.21
  86.7 0.8 copy-start.26
  87.5 1.2 copy-start.32
  88.7 0.9 copy-start.34
  89.6 0.9 copy-start.36
  90.5 7.4 %copy-start.14 = (bf16[128,1024]{1,0:T(8,128)(2,1)S(1)}, bf16[128,1024]{1,0:T(8,128)(2,1)}, u32[]{:S(2)}) copy-start(bf16[128,1024]{1,0:T(8,128)(2,1)} %copy-done.12) | copy-start | bytes 786436
  90.5 7.4 %copy-start.28 = (f32[32,128]{1,0:T(8,128)S(1)}, f32[32,128]{1,0:T(8,128)}, u32[]{:S(2)}) copy-start(f32[32,128]{1,0:T(8,128)} %copy-done.27) | copy-start | bytes 49156
  90.5 7.4 %copy-start.30 = (f32[32,128]{1,0:T(8,128)S(1)}, f32[32,128]{1,0:T(8,128)}, u32[]{:S(2)}) copy-start(f32[32,128]{1,0:T(8,128)} %copy-done.29) | copy-start | bytes 49156
  93.0 5.0 %copy-start.22 = (bf16[2,128,128]{2,1,0:T(8,128)(2,1)}, bf16[2,128,128]{2,1,0:T(8,128)(2,1)S(1)}, u32[]{:S(2)}) copy-start(bf16[2,128,128]{2,1,0:T(8,128)(2,1)S(1)} %get-tuple-element.39) | copy-start | bytes 196612
  93.7 28.2 %collective-permute-start.8 = (bf16[128,1024]{1,0:T(8,128)(2,1)}, bf16[128,1024]{1,0:T(8,128)(2,1)}, u32[]{:S(2)}, u32[]{:S(2)}) collective-permute-start(bf16[128,1024]{1,0:T(8,128)(2,1)} %get-tuple-element.69), channel_id=1, source_target_pairs={{0,4},{4,0},{1,5},{5,1},{2,6},{6,2},{3,7},{7,3},{8,12},{12,8},{9,1... | collective-permute-start | bytes 786440 | tf_op jit(solution)/shard_map/ppermute | solution.py:328
  97.8 22.8 %collective-permute-start.9 = (bf16[128,128]{1,0:T(8,128)(2,1)S(1)}, bf16[128,128]{1,0:T(8,128)(2,1)S(1)}, u32[]{:S(2)}, u32[]{:S(2)}) collective-permute-start(bf16[128,128]{1,0:T(8,128)(2,1)S(1)} %get-tuple-element.79), channel_id=1, source_target_pairs={{0,4},{4,0},{1,5},{5,1},{2,6},{6,2},{3,7},{7,3},{8,12},{12,8},{9,1... | collective-permute-start | bytes 98312 | tf_op jit(solution)/shard_map/ppermute | solution.py:328
  98.0 10.4 %copy-start.23 = (bf16[2,128,128]{2,1,0:T(8,128)(2,1)S(1)}, bf16[2,128,128]{2,1,0:T(8,128)(2,1)}, u32[]{:S(2)}) copy-start(bf16[2,128,128]{2,1,0:T(8,128)(2,1)} %copy-done.22) | copy-start | bytes 196612
  104.7 8.5 %all-to-all-start.2 = ((bf16[8,2,256]{2,1,0:T(2,128)(2,1)}), bf16[8,2,256]{2,1,0:T(2,128)(2,1)S(1)}, u32[]{:S(2)}, u32[]{:S(2)}) async-start(bf16[8,2,256]{2,1,0:T(2,128)(2,1)} %reshape.29), calls=%async_computation.2 | async-start | bytes 16384 | tf_op jit(solution)/shard_map/all_to_all | solution.py:403
  108.4 12.9 %collective-permute-start.10 = (bf16[128,128]{1,0:T(8,128)(2,1)S(1)}, bf16[128,128]{1,0:T(8,128)(2,1)S(1)}, u32[]{:S(2)}, u32[]{:S(2)}) collective-permute-start(bf16[128,128]{1,0:T(8,128)(2,1)S(1)} %get-tuple-element.77), channel_id=1, source_target_pairs={{0,4},{4,0},{1,5},{5,1},{2,6},{6,2},{3,7},{7,3},{8,12},{12,8},{9,1... | collective-permute-start | bytes 98312 | tf_op jit(solution)/shard_map/ppermute | solution.py:328
  113.2 14.7 %all-to-all-start.3 = ((bf16[32,32,128]{2,1,0:T(8,128)(2,1)}), bf16[32,32,128]{2,1,0:T(8,128)(2,1)S(1)}, u32[]{:S(2)}, u32[]{:S(2)}) async-start(bf16[32,32,128]{2,1,0:T(8,128)(2,1)} %get-tuple-element.44), calls=%async_computation.3 | async-start | bytes 524288 | tf_op jit(solution)/shard_map/all_to_all | solution.py:401
  128.6 7.9 %collective-permute-start.13 = (f32[2,16]{1,0:T(2,128)S(1)}, f32[2,16]{1,0:T(2,128)S(1)}, u32[]{:S(2)}, u32[]{:S(2)}) collective-permute-start(f32[2,16]{1,0:T(2,128)S(1)} %slice.50), channel_id=1, source_target_pairs={{0,4},{4,0},{1,5},{5,1},{2,6},{6,2},{3,7},{7,3},{8,12},{12,8},{9,1... | collective-permute-start | bytes 392 | tf_op jit(solution)/shard_map/ppermute | solution.py:328
  132.3 13.3 %all-to-all-start.4 = ((bf16[32,16,128]{2,1,0:T(8,128)(2,1)}), bf16[32,16,128]{2,1,0:T(8,128)(2,1)S(1)}, u32[]{:S(2)}, u32[]{:S(2)}) async-start(bf16[32,16,128]{2,1,0:T(8,128)(2,1)} %get-tuple-element.45), calls=%async_computation.4 | async-start | bytes 262144 | tf_op jit(solution)/shard_map/all_to_all | solution.py:430
  145.6 3.1 %collective-permute-start.12 = (bf16[32,16,128]{2,1,0:T(8,128)(2,1)S(1)}, bf16[32,16,128]{2,1,0:T(8,128)(2,1)S(1)}, u32[]{:S(2)}, u32[]{:S(2)}) collective-permute-start(bf16[32,16,128]{2,1,0:T(8,128)(2,1)S(1)} %all-to-all-done.4.own), channel_id=1, source_target_pairs={{0,4},{4,0},{1,5},{5,1},{2,6},{6,2},{3,7},{7,3},{8,12},{12,8},{9,1... | collective-permute-start | bytes 393224 | tf_op jit(solution)/shard_map/ppermute | solution.py:328
Sparse Core Ops, SparseCore 0:
  73.4 25.0 all-gather.1

commit v2 on v1

v2 whole, which is shorter than its diff:
```python
import jax
import jax.numpy as jnp
from jax import lax
from jax.experimental import pallas as pl
from jax.experimental.pallas import tpu as pltpu
from jax.sharding import Mesh
from jax.sharding import PartitionSpec as P

BF = jnp.bfloat16
F32 = jnp.float32
CHIPS, CORES, TP = 32, 2, 4
SPAN = 128
N = 128
HD = 64
HH = 16
W = HH * HD
D = 4096
PIECE = 32


def dot(a, b):
    return lax.dot_general(a, b, (((1,), (0,)), ((), ())), preferred_element_type=F32)


def dot_nt(a, b):
    return lax.dot_general(a, b, (((1,), (1,)), ((), ())), preferred_element_type=F32)


def split3(v):
    hi = v.astype(BF).astype(F32)
    rest = v - hi
    mid = rest.astype(BF).astype(F32)
    return [hi, mid, rest - mid]


def iota(shape, dim):
    return lax.broadcasted_iota(jnp.int32, shape, dim)


def triangle(keep):
    return jnp.where(keep(iota((SPAN, SPAN), 0), iota((SPAN, SPAN), 1)), 1.0, 0.0).astype(BF)


def sum_by(rows, matrix):
    r = rows.shape[0]
    out = dot(jnp.concatenate(split3(rows), 0).astype(BF), matrix)
    return out[:r] + out[r : 2 * r] + out[2 * r :]


def columns(first, second):
    stack = split3(first) + split3(second) + [jnp.zeros((32, SPAN), F32)]
    return jnp.concatenate(stack, 0).T.astype(BF)


def spread_maps():
    row = lax.broadcasted_iota(jnp.int32, (128, 2 * W), 0)
    col = lax.broadcasted_iota(jnp.int32, (128, 2 * W), 1)
    part = row // 48
    same = (row % 16) == (col % W) // HD
    return jnp.where(same & (part == col // W), 1.0, 0.0).astype(BF)


def copy_all(pairs, sems, first=0):
    copies = [pltpu.make_async_copy(a, b, sems.at[first + i]) for i, (a, b) in enumerate(pairs)]
    for c in copies:
        c.start()
    return copies


def wait_all(copies):
    for c in copies:
        c.wait()


def project_kernel(scal, w, bias, l0, l1, l2, l3, own, other, rows_out, sems):
    pieces = (l0, l1, l2, l3)
    copies = copy_all(
        [(v, rows_out.at[pl.ds(32 * k, 32)]) for k, v in enumerate(pieces)], sems
    )
    first = scal[1]
    head = iota((2 * HH, 2 * HH), 0)
    head = jnp.where(first == 0, head, lax.rem(head + HH, 2 * HH))
    mine = iota((2 * HH, 2 * HH), 1) == head
    add = jnp.sum(jnp.where(mine, bias[...], 0.0), axis=1, keepdims=True)
    rows = jnp.concatenate([v[...] for v in pieces], 0)
    acc = pltpu.roll(dot_nt(w[...], rows), scal[0], 1) + add
    own[...] = acc[:HH]
    other[...] = acc[HH:]
    wait_all(copies)


def state_kernel(
    scal, po, pp, alog, xo, xp, yo, yp, bo, bp, co, cp, maps,
    msg_out, keep_out, small_out,
    s_all, p_all, decay, msg, keep, small, sems,
):
    first = scal[1]
    second = 1 - first
    pre = jnp.concatenate([po[...], pp[...]], 0)
    step = jnp.maximum(pre, 0.0) + jnp.log1p(jnp.exp(-jnp.abs(pre)))
    mine = iota((2 * HH, 2 * HH), 1) == lax.rem(iota((2 * HH, 2 * HH), 0), HH) + HH * first
    rate = jnp.exp(jnp.sum(jnp.where(mine, alog[...], 0.0), axis=1, keepdims=True))
    rate = jnp.broadcast_to(rate, (2 * HH, 128))
    cum = sum_by(-rate * step, triangle(lambda u, t: u <= t))
    small[0] = pre
    small[1] = step
    small[2] = cum
    small[3] = rate
    copies = copy_all([(small, small_out)], sems)
    remain_step = jnp.exp(cum[:, SPAN - 1 :] - cum) * step
    growth = jnp.exp(cum)
    for b, (x, y, bm, cm) in enumerate(((xo, yo, bo, co), (xp, yp, bp, cp))):
        rows = slice(b * HH, (b + 1) * HH)
        weights = columns(remain_step[rows], growth[rows])
        b_t = bm[...].astype(F32).T.astype(BF)
        c_t = cm[...].astype(F32).T.astype(BF)
        for k in range(W // 256):
            cols = slice(k * 256, (k + 1) * 256)
            w_in = dot(weights, maps[:, cols])
            s_all[b, :, cols] = dot(b_t, (w_in * x[:, cols].astype(F32)).astype(BF))
            w_out = dot(weights, maps[:, W + k * 256 : W + (k + 1) * 256])
            p_all[b, :, cols] = dot(c_t, (w_out * y[:, cols].astype(F32)).astype(BF))
            decay[b, :, cols] = jnp.broadcast_to(w_out[SPAN - 1 :], (8, 256))
    per = N // PIECE
    for k in range(W // 128):
        cols = slice(k * 128, (k + 1) * 128)
        d_first, d_second = decay[first, 0:1, cols], decay[second, 0:1, cols]
        s_f, p_s = s_all[first, :, cols], p_all[second, :, cols]
        forward = d_second * s_f + s_all[second, :, cols]
        backward = p_all[first, :, cols] + d_first * p_s
        keep[0, :, cols] = s_f.astype(BF)
        keep[1, :, cols] = p_s.astype(BF)
        d3 = split3(d_first * d_second) + [jnp.zeros((5, 128), F32)]
        for r in range(per):
            rows = slice(r * PIECE, (r + 1) * PIECE)
            whole = jnp.concatenate([forward[rows], backward[rows]] + d3, 0)
            msg[k * per + r] = whole.astype(BF)
        if k % 2 == 1:
            done = pl.ds((k - 1) * per, 2 * per)
            copies += copy_all([(msg.at[done], msg_out.at[done])], sems, 1 + k // 2)
    copies += copy_all([(keep, keep_out)], sems, 5)
    wait_all(copies)


def fold_kernel(msg, out):
    parts = [msg[k].astype(F32) for k in range(CHIPS)]
    decays = [v[2 * PIECE : 2 * PIECE + 1] + v[2 * PIECE + 1 : 2 * PIECE + 2] + v[2 * PIECE + 2 : 2 * PIECE + 3] for v in parts]
    total = jnp.zeros((PIECE, 128), F32)
    for k in range(CHIPS):
        out[k, 0:PIECE, :] = total.astype(BF)
        total = total * decays[k] + parts[k][:PIECE]
    total = jnp.zeros((PIECE, 128), F32)
    for k in reversed(range(CHIPS)):
        out[k, PIECE : 2 * PIECE, :] = total.astype(BF)
        total = total * decays[k] + parts[k][PIECE : 2 * PIECE]


def intra_kernel(
    small_in, xo, xp, yo, yp, bo, bp, co, cp, gs, gb, gc, sums_out, small, sums_v, sems
):
    wait_all(copy_all([(small_in, small)], sems))
    lane = iota((SPAN, 128), 1)
    low = lane < HD
    later = lane >= iota((SPAN, SPAN), 0)
    step_t = jnp.concatenate([small[1], jnp.zeros((96, 128), F32)], 0).T
    cum_t = jnp.concatenate([small[2], jnp.zeros((96, 128), F32)], 0).T
    sums = jnp.zeros((SPAN, 128), F32)
    zero = jnp.zeros((SPAN, 128), BF)
    for b, (x, y, bm, cm) in enumerate(((xo, yo, bo, co), (xp, yp, bp, cp))):
        scores = dot_nt(bm[...], cm[...])
        grad_scores = jnp.zeros((SPAN, SPAN), F32)
        for pair in range(HH // 2):
            cols = slice(pair * 128, (pair + 1) * 128)
            xs, ys = x[:, cols], y[:, cols]
            halves = []
            for side in range(2):
                h = b * HH + pair * 2 + side
                mine = jnp.where(low if side == 0 else ~low, xs, zero)
                grad_mixing = dot_nt(mine, ys)
                spread = small[2, h : h + 1, :] - cum_t[:, h : h + 1]
                decay = jnp.where(later, jnp.exp(jnp.minimum(spread, 0.0)), 0.0)
                mixing = scores * decay
                halves.append(dot(mixing.astype(BF), ys))
                scaled = grad_mixing * step_t[:, h : h + 1]
                grad_scores = grad_scores + scaled * decay
                sums_v[0, h : h + 1, :] = jnp.sum(scaled * mixing, axis=0, keepdims=True)
                col = jnp.sum(grad_mixing * mixing, axis=1, keepdims=True)
                sums = jnp.where(lane == h, col, sums)
            gs[b, :, cols] = jnp.where(low, halves[0], halves[1])
        gs_bf = grad_scores.astype(BF)
        gb[b] = dot(gs_bf, cm[...])
        gc[b] = dot(grad_scores.T.astype(BF), bm[...])
    sums_v[1] = sums.T[: 2 * HH]
    wait_all(copy_all([(sums_v, sums_out)], sems, 1))


def block_decays(small, decay):
    for b in range(2):
        last = jnp.exp(small[2, b * HH : (b + 1) * HH, SPAN - 1 :])
        spread = jnp.where(iota((HH, W), 1) // HD == iota((HH, W), 0), last, 0.0)
        decay[b] = jnp.broadcast_to(jnp.sum(spread, axis=0, keepdims=True), (8, W))


def assemble(scal, got, keep, decay, start, end, exact):
    first = scal[1]
    second = 1 - first
    for k in range(W // 128):
        cols = slice(k * 128, (k + 1) * 128)
        d_first, d_second = decay[first, 0:1, cols], decay[second, 0:1, cols]
        for r in range(N // PIECE):
            at = k * (N // PIECE) + r
            rows = slice(r * PIECE, (r + 1) * PIECE)
            s_in, e_in = got[at, 0:PIECE, :], got[at, PIECE : 2 * PIECE, :]
            start[first, rows, cols] = s_in
            end[second, rows, cols] = e_in
            s_f, e_f = s_in.astype(F32), e_in.astype(F32)
            s_next = d_first * s_f + keep[0, rows, cols].astype(F32)
            e_next = d_second * e_f + keep[1, rows, cols].astype(F32)
            start[second, rows, cols] = s_next.astype(BF)
            end[first, rows, cols] = e_next.astype(BF)
            if exact is not None:
                one = jnp.sum(s_f * e_next, axis=0, keepdims=True)
                two = jnp.sum(s_next * e_f, axis=0, keepdims=True)
                if r == 0:
                    sum_one, sum_two = one, two
                else:
                    sum_one, sum_two = sum_one + one, sum_two + two
        if exact is not None:
            exact[first, 0:1, cols] = sum_one
            exact[second, 0:1, cols] = sum_two


def head_map(shape, head_dim, chan_dim):
    return jnp.where(iota(shape, chan_dim) // HD == iota(shape, head_dim), 1.0, 0.0).astype(BF)


def pre_kernel(
    scal, got, keep_in, small_in, sums_in,
    xo, xp, yo, yp, bo, bp, co, cp, lo_in, lp_in,
    z0, z1, z2, z3, msg_out,
    start, end, exact, decay, keep, small, sums_v, rows_v, zed, msg, sems,
):
    early = copy_all([(small_in, small), (keep_in, keep)], sems)
    late = copy_all(
        [(sums_in, sums_v), (lo_in, rows_v.at[pl.ds(0, 128)]), (lp_in, rows_v.at[pl.ds(128, 128)])],
        sems,
        2,
    )
    wait_all(early)
    block_decays(small, decay)
    assemble(scal, got, keep, decay, start, end, exact)
    by_head = head_map((W, 128), 1, 0)
    sums = []
    joint = []
    for b, (x, y, bm, cm) in enumerate(((xo, yo, bo, co), (xp, yp, bp, cp))):
        for grad, mat, state in ((x, bm, end), (y, cm, start)):
            total = jnp.zeros((SPAN, 128), F32)
            for k in range(W // 256):
                cols = slice(k * 256, (k + 1) * 256)
                prod = dot(mat[...], state[b, :, cols]) * grad[:, cols].astype(F32)
                total = total + dot(prod.astype(BF), by_head[cols])
            sums.append(total.T[:HH])
        rows8 = jnp.concatenate(split3(exact[b, 0:1, :]) + [jnp.zeros((5, W), F32)], 0).astype(BF)
        joint.append(jnp.sum(dot_nt(head_map((HH, W), 0, 1), rows8), axis=1, keepdims=True))
    x_pulled = jnp.concatenate([sums[0], sums[2]], 0)
    y_state = jnp.concatenate([sums[1], sums[3]], 0)
    joint = jnp.concatenate(joint, 0)
    pre, step, cum = small[0], small[1], small[2]
    last = cum[:, SPAN - 1 :]
    rate = small[3]
    q = jnp.exp(last - cum) * x_pulled
    wait_all(late)
    cols = sums_v[1]
    u = sums_v[0] - step * cols + jnp.exp(cum) * y_state
    grad_log = (
        sum_by(u, triangle(lambda u, t: u >= t))
        + sum_by(step * q, triangle(lambda u, t: u < t))
        + jnp.exp(last) * joint
    )
    grad_step = cols + q - rate * grad_log
    grad_pre = grad_step * jax.nn.sigmoid(pre)
    rolled = pltpu.roll(grad_pre, scal[2], 1)
    for k in range(TP):
        turn = rolled if k == 0 else pltpu.roll(rolled, 128 - 32 * k, 1)
        zed[k] = turn.astype(BF)
    copies = copy_all([(zed.at[k], z) for k, z in enumerate((z0, z1, z2, z3))], sems, 5)
    rolled = jnp.concatenate([rolled[:HH], rolled[HH:]], 1).astype(BF)
    diagonal = iota((HH, 128), 0) == iota((HH, 128), 1)

    def as_row(v):
        v = v[:HH] + v[HH:]
        v = jnp.sum(v, axis=1, keepdims=True)
        return jnp.sum(jnp.where(diagonal, v, 0.0), axis=0, keepdims=True)

    extra = split3(as_row(grad_pre)) + split3(as_row(-grad_log * step))
    extra = jnp.concatenate(extra + [jnp.zeros((10, 128), F32)], 0).astype(BF)
    for k in range(D // 256):
        cols = slice(k * 256, (k + 1) * 256)
        part = dot(rolled, rows_v[:, cols])
        for j in range(2):
            msg[2 * k + j, 0:HH, :] = part[:, j * 128 : (j + 1) * 128].astype(BF)
            msg[2 * k + j, HH : 2 * HH, :] = extra
        if k % 4 == 3:
            done = pl.ds(2 * k - 6, 8)
            copies += copy_all([(msg.at[done], msg_out.at[done])], sems, 9 + k // 4)
    wait_all(copies)


def sum_kernel(msg, out, totals):
    total = jnp.zeros((2 * HH, 128), F32)
    for k in range(CHIPS):
        total = total + msg[k].astype(F32)
    rounded = total[:HH].astype(BF)
    for k in range(CHIPS):
        out[k] = rounded
    e = total[HH:]
    bias = e[0:1] + e[1:2] + e[2:3]
    rate = e[3:4] + e[4:5] + e[5:6]
    totals[...] = jnp.concatenate([bias, rate, jnp.zeros((6, 128), F32)], 0)


def grads_kernel(
    scal, got, keep_in, small_in, gs, gb, gc, maps,
    xo, xp, yo, yp, bo, bp, co, cp,
    gx_own, gx_other, bc_own, bc_other,
    start, end, decay, keep, small, sems,
):
    wait_all(copy_all([(small_in, small), (keep_in, keep)], sems))
    block_decays(small, decay)
    assemble(scal, got, keep, decay, start, end, None)
    step, cum = small[1], small[2]
    remain = jnp.exp(cum[:, SPAN - 1 :] - cum)
    growth = jnp.exp(cum)
    for b, (x, y, bm, cm) in enumerate(((xo, yo, bo, co), (xp, yp, bp, cp))):
        rows = slice(b * HH, (b + 1) * HH)
        w_a = columns(remain[rows], growth[rows])
        w_b = columns(step[rows], step[rows])
        grad_b, grad_c = gb[b], gc[b]
        gx_out, bc_out = ((gx_own, bc_own), (gx_other, bc_other))[b]
        for k in range(W // 256):
            cols = slice(k * 256, (k + 1) * 256)
            wide = slice(W + k * 256, W + (k + 1) * 256)
            remain_w = dot(w_a, maps[:, cols])
            step_w = dot(w_b, maps[:, cols])
            growth_w = dot(w_a, maps[:, wide])
            pulled = dot(bm[...], end[b, :, cols])
            gx_out[:, cols] = (step_w * (gs[b, :, cols] + remain_w * pulled)).astype(BF)
            in_w = (remain_w * (step_w * x[:, cols].astype(F32))).astype(BF)
            out_w = (growth_w * y[:, cols].astype(F32)).astype(BF)
            grad_b = grad_b + dot_nt(in_w, end[b, :, cols])
            grad_c = grad_c + dot_nt(out_w, start[b, :, cols])
        bc_out[0] = grad_b.astype(BF)
        bc_out[1] = grad_c.astype(BF)


def weight_kernel(scal, own, other, out):
    at_zero = scal[1] == 0
    for j in range(CHIPS):
        a, b = own[j].astype(F32), other[j].astype(F32)
        cols = slice(j * 128, (j + 1) * 128)
        out[0:HH, cols] = jnp.where(at_zero, a, b)
        out[HH : 2 * HH, cols] = jnp.where(at_zero, b, a)


def join_kernel(scal, gx_own, gx_other, bc_own, bc_other, gx, gb, gc):
    at_zero = scal[1] == 0

    def join(own, other, out, width):
        out[:, :width] = jnp.where(at_zero, own, other)
        out[:, width:] = jnp.where(at_zero, other, own)

    join(gx_own[...], gx_other[...], gx, W)
    join(bc_own[0], bc_other[0], gb, N)
    join(bc_own[1], bc_other[1], gc, N)


def input_kernel(scal, a0, a1, a2, a3, b0, b1, b2, b3, w0, w1, w2, w3, out):
    first = scal[1]
    mine = pl.ds(pl.multiple_of(HH * first, HH), HH)
    others = pl.ds(pl.multiple_of(HH * (1 - first), HH), HH)
    rows = []
    for a, b in ((a0, b0), (a1, b1), (a2, b2), (a3, b3)):
        rows += [a[:HH], b[HH:]]
    zed = jnp.concatenate(rows, 0).astype(F32).T[:32].astype(BF)
    for k in range(D // 512):
        cols = slice(k * 512, (k + 1) * 512)
        mats = []
        for w in (w0, w1, w2, w3):
            mats += [w[mine, cols], w[others, cols]]
        out[:, cols] = dot(zed, jnp.concatenate(mats, 0)).astype(BF)


def call(kernel, outs, args, scratch=(), sems=0, far_in=(), far_out=(), flops=0, moved=0, limit=16):
    near = pl.BlockSpec(memory_space=pltpu.VMEM)
    far = pl.BlockSpec(memory_space=pltpu.HBM)
    specs = []
    for i, a in enumerate(args):
        if a.dtype == jnp.int32:
            specs.append(pl.BlockSpec(memory_space=pltpu.SMEM))
        else:
            specs.append(far if i in far_in else near)
    shapes = [pltpu.VMEM(s, t) for s, t in scratch]
    if sems:
        shapes.append(pltpu.SemaphoreType.DMA((sems,)))
    return pl.pallas_call(
        kernel,
        out_shape=[jax.ShapeDtypeStruct(s, t) for s, t in outs],
        in_specs=specs,
        out_specs=[far if i in far_out else near for i in range(len(outs))],
        scratch_shapes=shapes,
        compiler_params=pltpu.CompilerParams(vmem_limit_bytes=limit * 2**20),
        cost_estimate=pl.CostEstimate(flops=flops, bytes_accessed=moved, transcendentals=0),
    )(*args)


def swap(v):
    return lax.ppermute(v, "core", [(0, 1), (1, 0)])


def round_tp(v, k):
    return lax.ppermute(v, "tp", [(i, (i + k) % TP) for i in range(TP)])


def local(layer_input, dt_weight, dt_bias, a_log, ssm_input, b_in, c_in, out_grad):
    core = lax.axis_index("core")
    tp = lax.axis_index("tp")
    scal = jnp.stack([32 * tp, core, (128 - 32 * tp) % 128]).astype(jnp.int32)

    def half(v, which, width, axis):
        return lax.dynamic_slice_in_dim(v, which * width, width, axis)

    pieces = [layer_input] + [
        lax.ppermute(layer_input, "tp", [((i + k) % TP, i) for i in range(TP)]) for k in (1, 3, 2)
    ]
    pieces = [pieces[0], pieces[1], pieces[3], pieces[2]]
    weight_t = dt_weight.T
    weight_mine = jnp.concatenate(
        [half(weight_t, core, HH, 0), half(weight_t, 1 - core, HH, 0)], 0
    )
    operands = []
    for v, width in ((ssm_input, W), (out_grad, W), (b_in, N), (c_in, N)):
        operands += [half(v, core, width, 1), swap(half(v, 1 - core, width, 1))]
    maps = spread_maps()
    small_t = ((4, 2 * HH, 128), F32)
    keep_t = ((2, N, W), BF)

    proj_own, proj_other, rows_own = call(
        project_kernel,
        [((HH, 128), F32)] * 2 + [((SPAN, D), BF)],
        [scal, weight_mine, dt_bias[None, :]] + pieces,
        sems=4,
        far_out=(2,),
        flops=2**26,
        moved=2**21,
    )
    proj_other = swap(proj_other)
    msg_t = ((CHIPS, 2 * PIECE + 8, 128), BF)
    msg, keep, small = call(
        state_kernel,
        [msg_t, keep_t, small_t],
        [scal, proj_own, proj_other, a_log[None, :]] + operands + [maps],
        [((2, N, W), F32), ((2, N, W), F32), ((2, 8, W), F32), msg_t, keep_t, small_t],
        sems=6,
        far_out=(0, 1, 2),
        flops=2**28,
        moved=2**22,
    )
    got = lax.all_to_all(msg, "chip", 0, 0, tiled=True)

    weight_t, rows_own = lax.optimization_barrier((weight_t, rows_own))
    weights = [weight_t] + [round_tp(weight_t, k) for k in (1, 2, 3)]
    rows_other = swap(rows_own)
    sums_t = ((2, 2 * HH, 128), F32)
    gs, gb, gc, sums = call(
        intra_kernel,
        [((2, SPAN, W), F32), ((2, SPAN, N), F32), ((2, SPAN, N), F32), sums_t],
        [small] + operands,
        [small_t, sums_t],
        sems=2,
        far_in=(0,),
        far_out=(3,),
    )

    (folded,) = call(
        fold_kernel, [((CHIPS, 2 * PIECE, 128), BF)], [got], flops=2**20, moved=2**20
    )
    states = lax.all_to_all(folded, "chip", 0, 0, tiled=True)

    states, weights = lax.optimization_barrier((states, weights))
    zed_t = ((2 * HH, 128), BF)
    parts_t = ((CHIPS, 2 * HH, 128), BF)
    state_scratch = [((2, N, W), BF), ((2, N, W), BF)]
    kept = [((2, 8, W), F32), keep_t, small_t]
    *zed, parts = call(
        pre_kernel,
        [zed_t] * 4 + [parts_t],
        [scal, states, keep, small, sums] + operands + [rows_own, rows_other],
        state_scratch
        + [((2, 8, W), F32)]
        + kept
        + [sums_t, ((2 * SPAN, D), BF), ((TP, 2 * HH, 128), BF), parts_t],
        sems=13,
        far_in=(2, 3, 4, 13, 14),
        far_out=(0, 1, 2, 3, 4),
        flops=2**29,
        moved=2**23,
    )
    shares = lax.all_to_all(parts, "chip", 0, 0, tiled=True)

    zed = [zed[0]] + [round_tp(zed[k], k) for k in (1, 2, 3)]
    (grad_layer_input,) = call(
        input_kernel, [((32, D), BF)], [scal] + zed + [swap(z) for z in zed] + weights
    )

    total, totals = call(
        sum_kernel, [((CHIPS, HH, 128), BF), ((8, 128), F32)], [shares], flops=2**20, moved=2**20
    )
    weight_own = lax.all_to_all(total, "chip", 0, 0, tiled=True)

    def join(mine, other, axis):
        return jnp.where(
            core == 0,
            jnp.concatenate([mine, other], axis),
            jnp.concatenate([other, mine], axis),
        )

    totals = join(totals[:2, :HH], swap(totals[:2, :HH]), 1)
    grad_dt_bias = totals[0]
    grad_a_log = jnp.exp(a_log) * totals[1]

    gs, total = lax.optimization_barrier((gs, total))
    gx_own, gx_other, bc_own, bc_other = call(
        grads_kernel,
        [((SPAN, W), BF)] * 2 + [((2, SPAN, N), BF)] * 2,
        [scal, states, keep, small, gs, gb, gc, maps] + operands,
        state_scratch + kept,
        sems=2,
        far_in=(2, 3),
    )
    grad_ssm_input, grad_b_in, grad_c_in = call(
        join_kernel,
        [((SPAN, 2 * W), BF), ((SPAN, 2 * N), BF), ((SPAN, 2 * N), BF)],
        [scal, gx_own, swap(gx_other), bc_own, swap(bc_other)],
    )

    (grad_dt_weight,) = call(
        weight_kernel,
        [((2 * HH, D), F32)],
        [scal, weight_own, swap(weight_own)],
        flops=2**20,
        moved=2**22,
    )
    return (
        grad_ssm_input,
        grad_b_in,
        grad_c_in,
        grad_layer_input,
        grad_dt_weight.T,
        grad_dt_bias,
        grad_a_log,
    )


def solution(mesh):
    fine = Mesh(mesh.devices.reshape(CHIPS, CORES, TP), ("chip", "core", "tp"))
    ctx = ("chip", "core")
    everything = ("chip", "core", "tp")
    placed = (
        P(everything, None),
        P(None, "tp"),
        P("tp"),
        P("tp"),
        P(ctx, "tp"),
        P(ctx, "tp"),
        P(ctx, "tp"),
        P(ctx, "tp"),
    )
    return jax.shard_map(
        local,
        mesh=fine,
        in_specs=placed,
        out_specs=(
            P(ctx, "tp"),
            P(ctx, "tp"),
            P(ctx, "tp"),
            P(everything, None),
            P(None, "tp"),
            P("tp"),
            P("tp"),
        ),
        check_vma=False,
    )
```

time: 159 us -> 134 us (0.84)
  waiting for transfers between devices: 42.2 us -> 26.6 us
  between operations: 14.5 us -> 1 us
  starting transfers between devices: 52.5 us -> 61 us
  local copies, waits for them, and re-layouts: 23 us -> 18.1 us
  Pallas kernels: 19 us -> 21.6 us
  matrix products: 2.24 us -> 0 us
    ppermute x3, waiting for transfers between devices: 8.56 us -> 0.02 us  [local(): lax.ppermute(layer_input, 'tp', [((i + k) % TP, i) for i in range(TP)])]
    ppermute x0 -> x6, waiting for transfers between devices: none -> 7.87 us  [round_tp(): return lax.ppermute(v, 'tp', [(i, (i + k) % TP) for i in range(TP)])]
    all_to_all x1, waiting for transfers between devices: 8.54 us -> 2.37 us  [local(): weight_own = lax.all_to_all(total, 'chip', 0, 0, tiled=True)]
    ppermute x0 -> x6, starting transfers between devices: none -> 5.85 us  [round_tp(): return lax.ppermute(v, 'tp', [(i, (i + k) % TP) for i in range(TP)])]
    all_to_all x1, starting transfers between devices: 4.14 us -> 9.63 us  [local(): weight_own = lax.all_to_all(total, 'chip', 0, 0, tiled=True)]
    all_to_all x1 -> x0, waiting for transfers between devices: 4.68 us -> none  [local(): zed = lax.all_to_all(zed, ('core', 'tp'), 0, 0, tiled=True)]
    unnamed x90 -> x62, local copies, waits for them, and re-layouts: 19.2 us -> 14.7 us
    all_to_all x1, starting transfers between devices: 5.01 us -> 9.22 us  [local(): shares = lax.all_to_all(parts, 'chip', 0, 0, tiled=True)]
  transfers between devices with their start and end apart: 20 -> 27, of which waited for: 9 -> 6; matrix products, arithmetic and copies ran while one was open for 8% -> 6% of each run, Pallas kernels for 9% -> 10%
where the time goes in v2:
time: 134 us; the launch traced here: 133 us
  starting transfers between devices  61 us (46%)
  waiting for transfers between devices  26.6 us (20%)
  Pallas kernels  21.6 us (16%)
  local copies, waits for them, and re-layouts  18.1 us (14%)
  other arithmetic  4.61 us (3%)
    pallas_call x10, Pallas kernels, call(): pl.pallas_call(kernel, out_shape=[jax.ShapeDtypeStruct(s, t) for s, t in...  21.6 us
    all_to_all x1, waiting for transfers between devices, local(): got = lax.all_to_all(msg, 'chip', 0, 0, tiled=True)  15.4 us
    unnamed x62, local copies, waits for them, and re-layouts  14.7 us
    ppermute x14, starting transfers between devices, swap(): return lax.ppermute(v, 'core', [(0, 1), (1, 0)])  12.3 us
    all_to_all x1, starting transfers between devices, local(): got = lax.all_to_all(msg, 'chip', 0, 0, tiled=True)  11 us
    all_to_all x1, starting transfers between devices, local(): weight_own = lax.all_to_all(total, 'chip', 0, 0, tiled=True)  9.63 us
    all_to_all x1, starting transfers between devices, local(): shares = lax.all_to_all(parts, 'chip', 0, 0, tiled=True)  9.22 us
    ppermute x6, waiting for transfers between devices, round_tp(): return lax.ppermute(v, 'tp', [(i, (i + k) % TP) for i in range(TP)])  7.87 us
  transfers between devices with their start and end apart: 27, of which 6 were waited for; matrix products, arithmetic and copies ran while one was open for 6% of the time, Pallas kernels for 10%

profile of v2, /device:TPU:1, one launch (start us, length us, event | category | flops | bytes accessed | tf_op | source)
XLA Modules:
  0.0 132.9 jit_solution(14252283117188223582)
XLA Ops:
  0.6 3.8 %collective-permute-start.1 = (bf16[32,4096]{1,0:T(8,128)(2,1)}, bf16[32,4096]{1,0:T(8,128)(2,1)S(1)}, u32[]{:S(2)}, u32[]{:S(2)}) collective-permute-start(bf16[32,4096]{1,0:T(8,128)(2,1)} %l0.1), channel_id=1, source_target_pairs={{2,0},{3,1},{0,2},{1,3},{6,4},{7,5},{4,6},{5,7},{10,8},{11,9},{8,1... | collective-permute-start | bytes 786440 | tf_op jit(solution)/shard_map/ppermute | solution.py:433
  4.5 0.8 collective-permute-start
  5.2 0.7 collective-permute-start.2
  5.9 1.4 %constant_dynamic-slice_fusion.2 = (bf16[128,128]{1,0:T(8,128)(2,1)}, bf16[128,128]{1,0:T(8,128)(2,1)S(1)}) fusion(bf16[128,256]{1,0:T(8,128)(2,1)} %param.13, s32[]{:T(128)S(6)} %select_n.80, s32[]{:T(128)S(6)} %select_n.79), kind=kLoop, calls=%fused_computation.31 | loop fusion | bytes 131080 | tf_op jit(solution)/shard_map/dynamic_slice | solution.py:430
  7.3 1.5 %collective-permute-start.6 = (bf16[128,128]{1,0:T(8,128)(2,1)}, bf16[128,128]{1,0:T(8,128)(2,1)S(1)}, u32[]{:S(2)}, u32[]{:S(2)}) collective-permute-start(bf16[128,128]{1,0:T(8,128)(2,1)} %get-tuple-element.79), channel_id=1, source_target_pairs={{0,4},{4,0},{1,5},{5,1},{2,6},{6,2},{3,7},{7,3},{8,12},{12,8},{9,1... | collective-permute-start | bytes 98312 | tf_op jit(solution)/shard_map/ppermute | solution.py:417
  8.8 1.4 %constant_dynamic-slice_fusion = (bf16[128,128]{1,0:T(8,128)(2,1)}, bf16[128,128]{1,0:T(8,128)(2,1)S(1)}) fusion(bf16[128,256]{1,0:T(8,128)(2,1)} %param.14, s32[]{:T(128)S(6)} %select_n.80, s32[]{:T(128)S(6)} %select_n.79), kind=kLoop, calls=%fused_computation.29 | loop fusion | bytes 131080 | tf_op jit(solution)/shard_map/dynamic_slice | solution.py:430
  10.2 0.6 broadcast_add_fusion.1
  10.8 0.6 iota_divide_fusion
  11.4 0.6 compare_and_fusion
  12.0 0.6 fusion.10
  12.6 0.6 fusion.7
  13.2 0.6 iota_shift-right-logical_fusion
  13.9 0.9 copy-done.19
  14.9 1.0 copy-done.20
  15.9 0.6 collective-permute-start.4
  16.6 1.4 %collective-permute-start.5 = (bf16[128,1024]{1,0:T(8,128)(2,1)S(1)}, bf16[128,1024]{1,0:T(8,128)(2,1)S(1)}, u32[]{:S(2)}, u32[]{:S(2)}) collective-permute-start(bf16[128,1024]{1,0:T(8,128)(2,1)S(1)} %get-tuple-element.71), channel_id=1, source_target_pairs={{0,4},{4,0},{1,5},{5,1},{2,6},{6,2},{3,7},{7,3},{8,12},{12,8},{9,1... | collective-permute-start | bytes 786440 | tf_op jit(solution)/shard_map/ppermute | solution.py:417
  18.1 1.2 shard_map.135
  19.3 1.0 copy-done
  20.3 0.6 collective-permute-start.3
  21.0 0.6 copy-done.22
  21.6 0.4 select_convert_fusion.maps
  22.0 0.6 copy-done.18
  22.7 2.8 %shard_map.136 = (bf16[32,72,128]{2,1,0:T(8,128)(2,1)S(1)}, bf16[2,128,1024]{2,1,0:T(8,128)(2,1)S(1)}, f32[4,32,128]{2,1,0:T(8,128)S(1)}) custom-call(s32[3]{0:T(128)S(1)} %pad_add_fusion.scal, f32[16,128]{1,0:T(8,128)S(1)} %get-tuple-element.39.po, f32[16,128]{1,0:T(8,128)S(1)} %collective-permute-done.3.pp, f32[1,32]{1,0:T(1,128)S(1)} %bitcast.20, ...), custom_call_target="tpu_custom_call" | custom-call | flops 268435456 | bytes 4194304 | tf_op jit(solution)/shard_map/pallas_call | solution.py:405
  25.5 0.8 copy-done.5
  26.3 11.0 %all-to-all-start = ((bf16[32,72,128]{2,1,0:T(8,128)(2,1)}), bf16[32,72,128]{2,1,0:T(8,128)(2,1)S(1)}, u32[]{:S(2)}, u32[]{:S(2)}) async-start(bf16[32,72,128]{2,1,0:T(8,128)(2,1)} %copy-done.5), calls=%async_computation | async-start | bytes 1179648 | tf_op jit(solution)/shard_map/all_to_all | solution.py:468
  37.4 0.4 collective-permute-start.11
  37.8 15.4 %all-to-all-done.msg = bf16[32,72,128]{2,1,0:T(8,128)(2,1)S(1)} async-done(((bf16[32,72,128]{2,1,0:T(8,128)(2,1)}), bf16[32,72,128]{2,1,0:T(8,128)(2,1)S(1)}, u32[]{:S(2)}, u32[]{:S(2)}) %all-to-all-start) | async-done | bytes 589856 | tf_op jit(solution)/shard_map/all_to_all | solution.py:468
  53.2 0.9 shard_map.137
  54.2 7.6 %all-to-all-start.1 = ((bf16[32,64,128]{2,1,0:T(8,128)(2,1)}), bf16[32,64,128]{2,1,0:T(8,128)(2,1)S(1)}, u32[]{:S(2)}, u32[]{:S(2)}) async-start(bf16[32,64,128]{2,1,0:T(8,128)(2,1)} %shard_map.137), calls=%async_computation.1 | async-start | bytes 1048576 | tf_op jit(solution)/shard_map/all_to_all | solution.py:487
  61.8 2.4 %collective-permute-start.10 = (bf16[32,4096]{1,0:T(8,128)(2,1)S(1)}, bf16[32,4096]{1,0:T(8,128)(2,1)S(1)}, u32[]{:S(2)}, u32[]{:S(2)}) collective-permute-start(bf16[32,4096]{1,0:T(8,128)(2,1)S(1)} %bitcast.15), channel_id=1, source_target_pairs={{0,3},{1,0},{2,1},{3,2},{4,7},{5,4},{6,5},{7,6},{8,11},{9,8},{10,9... | collective-permute-start | bytes 786440 | tf_op jit(solution)/shard_map/ppermute | solution.py:421
  64.9 4.5 %shard_map.138 = (f32[2,128,1024]{2,1,0:T(8,128)S(1)}, f32[2,128,128]{2,1,0:T(8,128)S(1)}, f32[2,128,128]{2,1,0:T(8,128)S(1)}, f32[2,32,128]{2,1,0:T(8,128)S(1)}) custom-call(f32[4,32,128]{2,1,0:T(8,128)S(1)} %get-tuple-element.46.small_in, bf16[128,1024]{1,0:T(8,128)(2,1)S(1)} %get-tuple-element.74.xo, bf16[128,1024]{1,0:T(8,128)(2,1)S(1)} %collective-permute-done.4.xp, ...), custom_call_target="tpu_custom_call" | custom-call | tf_op jit(solution)/shard_map/pallas_call | solution.py:405
  69.4 1.0 copy-done.3
  70.4 0.7 copy-done.14
  71.0 1.0 collective-permute-done.9.w2
  72.0 0.7 copy-done.8
  72.7 6.9 %collective-permute-done.8.w1 = bf16[32,4096]{1,0:T(8,128)(2,1)S(1)} collective-permute-done((bf16[32,4096]{1,0:T(8,128)(2,1)S(1)}, bf16[32,4096]{1,0:T(8,128)(2,1)S(1)}, u32[]{:S(2)}, u32[]{:S(2)}) %collective-permute-start.8) | collective-permute-done | bytes 262176 | tf_op jit(solution)/shard_map/ppermute | solution.py:421
  79.6 0.7 copy-done.10
  80.3 1.2 copy-done.1
  81.5 4.4 %shard_map.139 = (bf16[32,128]{1,0:T(8,128)(2,1)S(1)}, bf16[32,128]{1,0:T(8,128)(2,1)}, bf16[32,128]{1,0:T(8,128)(2,1)}, bf16[32,128]{1,0:T(8,128)(2,1)S(1)}, bf16[32,32,128]{2,1,0:T(8,128)(2,1)S(1)}) custom-call(s32[3]{0:T(128)S(1)} %pad_add_fusion.scal, bf16[32,64,128]{2,1,0:T(8,128)(2,1)S(1)} %all-to-all-done.1.got, ...), custom_call_target="tpu_custom_call" | custom-call | flops 536870912 | bytes 8388608 | tf_op jit(solution)/shard_map/pallas_call | solution.py:405
  85.9 0.7 copy-done.12
  86.6 9.2 %all-to-all-start.2 = ((bf16[32,32,128]{2,1,0:T(8,128)(2,1)}), bf16[32,32,128]{2,1,0:T(8,128)(2,1)S(1)}, u32[]{:S(2)}, u32[]{:S(2)}) async-start(bf16[32,32,128]{2,1,0:T(8,128)(2,1)} %copy-done.12), calls=%async_computation.2 | async-start | bytes 524288 | tf_op jit(solution)/shard_map/all_to_all | solution.py:508
  96.0 0.4 collective-permute-start.15
  96.4 2.2 %collective-permute-start.16 = (bf16[32,128]{1,0:T(8,128)(2,1)S(1)}, bf16[32,128]{1,0:T(8,128)(2,1)S(1)}, u32[]{:S(2)}, u32[]{:S(2)}) collective-permute-start(bf16[32,128]{1,0:T(8,128)(2,1)S(1)} %get-tuple-element.65), channel_id=1, source_target_pairs={{0,3},{1,0},{2,1},{3,2},{4,7},{5,4},{6,5},{7,6},{8,11},{9,8},{10,9... | collective-permute-start | bytes 24584 | tf_op jit(solution)/shard_map/ppermute | solution.py:421
  98.6 1.4 %collective-permute-start.17 = (bf16[32,128]{1,0:T(8,128)(2,1)S(1)}, bf16[32,128]{1,0:T(8,128)(2,1)S(1)}, u32[]{:S(2)}, u32[]{:S(2)}) collective-permute-start(bf16[32,128]{1,0:T(8,128)(2,1)S(1)} %get-tuple-element.62.a0), channel_id=1, source_target_pairs={{0,4},{4,0},{1,5},{5,1},{2,6},{6,2},{3,7},{7,3},{8,12},{12,8},{9,1... | collective-permute-start | bytes 24584 | tf_op jit(solution)/shard_map/ppermute | solution.py:417
  100.0 1.8 %collective-permute-start.18 = (bf16[32,128]{1,0:T(8,128)(2,1)S(1)}, bf16[32,128]{1,0:T(8,128)(2,1)S(1)}, u32[]{:S(2)}, u32[]{:S(2)}) collective-permute-start(bf16[32,128]{1,0:T(8,128)(2,1)S(1)} %collective-permute-done.14.a1), channel_id=1, source_target_pairs={{0,4},{4,0},{1,5},{5,1},{2,6},{6,2},{3,7},{7,3},{8,12},{12,8},{9,1... | collective-permute-start | bytes 24584 | tf_op jit(solution)/shard_map/ppermute | solution.py:417
  101.8 0.4 collective-permute-start.19
  102.2 0.5 collective-permute-start.20
  103.0 0.6 collective-permute-done.20.b3
  103.6 0.9 copy-done.7
  104.5 0.9 copy-done.9
  105.5 0.9 copy-done.11
  106.4 1.6 %shard_map.143 = bf16[32,4096]{1,0:T(8,128)(2,1)} custom-call(s32[3]{0:T(128)S(1)} %pad_add_fusion.scal, bf16[32,128]{1,0:T(8,128)(2,1)S(1)} %get-tuple-element.62.a0, bf16[32,128]{1,0:T(8,128)(2,1)S(1)} %collective-permute-done.14.a1, bf16[32,128]{1,0:T(8,128)(2,1)S(1)} %collective-permute-done.15.a2, bf16[32,128]{1,0:T(8,128)(2,1)S(1)} %collective-permute-done.16.a3, ...), custom_call_target="tpu_custom_call" | custom-call | tf_op jit(solution)/shard_map/pallas_call | solution.py:405
  108.1 0.6 copy-done.16
  108.7 9.6 %all-to-all-start.3 = ((bf16[32,16,128]{2,1,0:T(8,128)(2,1)}), bf16[32,16,128]{2,1,0:T(8,128)(2,1)S(1)}, u32[]{:S(2)}, u32[]{:S(2)}) async-start(bf16[32,16,128]{2,1,0:T(8,128)(2,1)} %copy-done.16), calls=%async_computation.3 | async-start | bytes 262144 | tf_op jit(solution)/shard_map/all_to_all | solution.py:518
  118.3 0.9 collective-permute-start.22
  119.3 1.2 copy-done.4
  120.5 3.4 %shard_map.141 = (bf16[128,1024]{1,0:T(8,128)(2,1)S(1)}, bf16[128,1024]{1,0:T(8,128)(2,1)}, bf16[2,128,128]{2,1,0:T(8,128)(2,1)S(1)}, bf16[2,128,128]{2,1,0:T(8,128)(2,1)}) custom-call(s32[3]{0:T(128)S(1)} %pad_add_fusion.scal, bf16[32,64,128]{2,1,0:T(8,128)(2,1)S(1)} %all-to-all-done.1.got, bf16[2,128,1024]{2,1,0:T(8,128)(2,1)S(1)} %get-tuple-element.45.keep_in, ...), custom_call_target="tpu_custom_call" | custom-call | tf_op jit(solution)/shard_map/pallas_call | solution.py:405
  124.0 0.5 collective-permute-start.12
  124.6 0.5 bitcast_multiply_fusion
  125.1 2.4 %all-to-all-done.3.own = bf16[32,16,128]{2,1,0:T(8,128)(2,1)S(1)} async-done(((bf16[32,16,128]{2,1,0:T(8,128)(2,1)}), bf16[32,16,128]{2,1,0:T(8,128)(2,1)S(1)}, u32[]{:S(2)}, u32[]{:S(2)}) %all-to-all-start.3) | async-done | bytes 131104 | tf_op jit(solution)/shard_map/all_to_all | solution.py:518
  127.5 2.1 %collective-permute-start.21 = (bf16[32,16,128]{2,1,0:T(8,128)(2,1)S(1)}, bf16[32,16,128]{2,1,0:T(8,128)(2,1)S(1)}, u32[]{:S(2)}, u32[]{:S(2)}) collective-permute-start(bf16[32,16,128]{2,1,0:T(8,128)(2,1)S(1)} %all-to-all-done.3.own), channel_id=1, source_target_pairs={{0,4},{4,0},{1,5},{5,1},{2,6},{6,2},{3,7},{7,3},{8,12},{12,8},{9,1... | collective-permute-start | bytes 393224 | tf_op jit(solution)/shard_map/ppermute | solution.py:417
  129.6 0.5 slice_bitcast_fusion
  130.1 1.4 %shard_map.142 = (bf16[128,2048]{1,0:T(8,128)(2,1)}, bf16[128,256]{1,0:T(8,128)(2,1)}, bf16[128,256]{1,0:T(8,128)(2,1)}) custom-call(s32[3]{0:T(128)S(1)} %pad_add_fusion.scal, bf16[128,1024]{1,0:T(8,128)(2,1)S(1)} %get-tuple-element.55.gx_own, bf16[128,1024]{1,0:T(8,128)(2,1)S(1)} %collective-permute-done.12.gx_other, ...), custom_call_target="tpu_custom_call" | custom-call | tf_op jit(solution)/shard_map/pallas_call | solution.py:405
  131.5 1.4 %shard_map.144 = f32[32,4096]{1,0:T(8,128)} custom-call(s32[3]{0:T(128)S(1)} %pad_add_fusion.scal, bf16[32,16,128]{2,1,0:T(8,128)(2,1)S(1)} %all-to-all-done.3.own, bf16[32,16,128]{2,1,0:T(8,128)(2,1)S(1)} %collective-permute-done.21.other), custom_call_target="tpu_custom_call" | custom-call | flops 1048576 | bytes 4194304 | tf_op jit(solution)/shard_map/pallas_call | solution.py:405
  (80 shorter events, 1.6 us)
Async XLA Ops:
  0.6 13.2 %copy-start.2 = (bf16[4096,32]{0,1:T(8,128)(2,1)S(1)}, bf16[4096,32]{0,1:T(8,128)(2,1)}, u32[]{:S(2)}) copy-start(bf16[4096,32]{0,1:T(8,128)(2,1)} %param.9) | copy-start | bytes 786436
  0.6 15.3 %collective-permute-start.1 = (bf16[32,4096]{1,0:T(8,128)(2,1)}, bf16[32,4096]{1,0:T(8,128)(2,1)S(1)}, u32[]{:S(2)}, u32[]{:S(2)}) collective-permute-start(bf16[32,4096]{1,0:T(8,128)(2,1)} %l0.1), channel_id=1, source_target_pairs={{2,0},{3,1},{0,2},{1,3},{6,4},{7,5},{4,6},{5,7},{10,8},{11,9},{8,1... | collective-permute-start | bytes 786440 | tf_op jit(solution)/shard_map/ppermute | solution.py:433
  4.5 12.1 %collective-permute-start = (bf16[32,4096]{1,0:T(8,128)(2,1)}, bf16[32,4096]{1,0:T(8,128)(2,1)S(1)}, u32[]{:S(2)}, u32[]{:S(2)}) collective-permute-start(bf16[32,4096]{1,0:T(8,128)(2,1)} %l0.1), channel_id=1, source_target_pairs={{1,0},{2,1},{3,2},{0,3},{5,4},{6,5},{7,6},{4,7},{9,8},{10,9},{11,1... | collective-permute-start | bytes 786440 | tf_op jit(solution)/shard_map/ppermute | solution.py:433
  5.2 12.8 %collective-permute-start.2 = (bf16[32,4096]{1,0:T(8,128)(2,1)}, bf16[32,4096]{1,0:T(8,128)(2,1)S(1)}, u32[]{:S(2)}, u32[]{:S(2)}) collective-permute-start(bf16[32,4096]{1,0:T(8,128)(2,1)} %l0.1), channel_id=1, source_target_pairs={{3,0},{0,1},{1,2},{2,3},{7,4},{4,5},{5,6},{6,7},{11,8},{8,9},{9,10... | collective-permute-start | bytes 786440 | tf_op jit(solution)/shard_map/ppermute | solution.py:433
  7.3 14.6 %collective-permute-start.6 = (bf16[128,128]{1,0:T(8,128)(2,1)}, bf16[128,128]{1,0:T(8,128)(2,1)S(1)}, u32[]{:S(2)}, u32[]{:S(2)}) collective-permute-start(bf16[128,128]{1,0:T(8,128)(2,1)} %get-tuple-element.79), channel_id=1, source_target_pairs={{0,4},{4,0},{1,5},{5,1},{2,6},{6,2},{3,7},{7,3},{8,12},{12,8},{9,1... | collective-permute-start | bytes 98312 | tf_op jit(solution)/shard_map/ppermute | solution.py:417
  10.2 11.7 %collective-permute-start.7 = (bf16[128,128]{1,0:T(8,128)(2,1)}, bf16[128,128]{1,0:T(8,128)(2,1)S(1)}, u32[]{:S(2)}, u32[]{:S(2)}) collective-permute-start(bf16[128,128]{1,0:T(8,128)(2,1)} %get-tuple-element.77), channel_id=1, source_target_pairs={{0,4},{4,0},{1,5},{5,1},{2,6},{6,2},{3,7},{7,3},{8,12},{12,8},{9,1... | collective-permute-start | bytes 98312 | tf_op jit(solution)/shard_map/ppermute | solution.py:417
  13.8 1.0 copy-start.19
  14.8 1.0 copy-start.20
  15.9 2.1 %copy-start.13 = (bf16[32,4096]{1,0:T(8,128)(2,1)S(1)}, bf16[32,4096]{1,0:T(8,128)(2,1)}, u32[]{:S(2)}) copy-start(bf16[32,4096]{1,0:T(8,128)(2,1)} %l0.1) | copy-start | bytes 786436
  15.9 6.0 %collective-permute-start.4 = (bf16[128,1024]{1,0:T(8,128)(2,1)S(1)}, bf16[128,1024]{1,0:T(8,128)(2,1)S(1)}, u32[]{:S(2)}, u32[]{:S(2)}) collective-permute-start(bf16[128,1024]{1,0:T(8,128)(2,1)S(1)} %get-tuple-element.73), channel_id=1, source_target_pairs={{0,4},{4,0},{1,5},{5,1},{2,6},{6,2},{3,7},{7,3},{8,12},{12,8},{9,1... | collective-permute-start | bytes 786440 | tf_op jit(solution)/shard_map/ppermute | solution.py:417
  16.5 1.5 %copy-start.17 = (f32[32]{0:T(128)S(1)}, f32[32]{0:T(128)}, u32[]{:S(2)}) copy-start(f32[32]{0:T(128)} %param.10) | copy-start | bytes 388
  16.6 5.4 %collective-permute-start.5 = (bf16[128,1024]{1,0:T(8,128)(2,1)S(1)}, bf16[128,1024]{1,0:T(8,128)(2,1)S(1)}, u32[]{:S(2)}, u32[]{:S(2)}) collective-permute-start(bf16[128,1024]{1,0:T(8,128)(2,1)S(1)} %get-tuple-element.71), channel_id=1, source_target_pairs={{0,4},{4,0},{1,5},{5,1},{2,6},{6,2},{3,7},{7,3},{8,12},{12,8},{9,1... | collective-permute-start | bytes 786440 | tf_op jit(solution)/shard_map/ppermute | solution.py:417
  18.0 2.9 %copy-start.24 = (pred[2048]{0:T(1024)(128)(4,1)S(1)}, pred[2048]{0:T(1024)(128)(4,1)}, u32[]{:S(2)}) copy-start(pred[2048]{0:T(1024)(128)(4,1)} %get-tuple-element.88) | copy-start | bytes 6148
  18.0 2.9 %copy-start.26 = (s32[128]{0:T(128)S(1)}, s32[128]{0:T(128)}, u32[]{:S(2)}) copy-start(s32[128]{0:T(128)} %get-tuple-element.92) | copy-start | bytes 1540
  18.0 2.9 %copy-start.27 = (s32[128]{0:T(128)S(1)}, s32[128]{0:T(128)}, u32[]{:S(2)}) copy-start(s32[128]{0:T(128)} %get-tuple-element.89) | copy-start | bytes 1540
  18.0 2.9 %copy-start.28 = (s32[128]{0:T(128)S(1)}, s32[128]{0:T(128)}, u32[]{:S(2)}) copy-start(s32[128]{0:T(128)} %get-tuple-element.90) | copy-start | bytes 1540
  18.1 2.9 %copy-start.29 = (pred[128]{0:T(512)(128)(4,1)S(1)}, pred[128]{0:T(512)(128)(4,1)}, u32[]{:S(2)}) copy-start(pred[128]{0:T(512)(128)(4,1)} %get-tuple-element.81) | copy-start | bytes 388
  18.1 2.9 %copy-start.30 = (pred[128]{0:T(512)(128)(4,1)S(1)}, pred[128]{0:T(512)(128)(4,1)}, u32[]{:S(2)}) copy-start(pred[128]{0:T(512)(128)(4,1)} %get-tuple-element.82) | copy-start | bytes 388
  19.3 1.0 copy-start
  20.3 0.7 copy-start.23
  20.3 1.7 %collective-permute-start.3 = (f32[16,128]{1,0:T(8,128)S(1)}, f32[16,128]{1,0:T(8,128)S(1)}, u32[]{:S(2)}, u32[]{:S(2)}) collective-permute-start(f32[16,128]{1,0:T(8,128)S(1)} %get-tuple-element.40), channel_id=1, source_target_pairs={{0,4},{4,0},{1,5},{5,1},{2,6},{6,2},{3,7},{7,3},{8,12},{12,8},{9,1... | collective-permute-start | bytes 24584 | tf_op jit(solution)/shard_map/ppermute | solution.py:417
  20.9 0.7 copy-start.22
  20.9 0.7 copy-start.21
  20.9 0.7 copy-start.25
  22.0 0.7 copy-start.18
  25.5 0.8 copy-start.5
  26.3 26.9 %all-to-all-start = ((bf16[32,72,128]{2,1,0:T(8,128)(2,1)}), bf16[32,72,128]{2,1,0:T(8,128)(2,1)S(1)}, u32[]{:S(2)}, u32[]{:S(2)}) async-start(bf16[32,72,128]{2,1,0:T(8,128)(2,1)} %copy-done.5), calls=%async_computation | async-start | bytes 1179648 | tf_op jit(solution)/shard_map/all_to_all | solution.py:468
  37.4 42.9 %collective-permute-start.11 = (bf16[128,4096]{1,0:T(8,128)(2,1)}, bf16[128,4096]{1,0:T(8,128)(2,1)}, u32[]{:S(2)}, u32[]{:S(2)}) collective-permute-start(bf16[128,4096]{1,0:T(8,128)(2,1)} %copy-done), channel_id=1, source_target_pairs={{0,4},{4,0},{1,5},{5,1},{2,6},{6,2},{3,7},{7,3},{8,12},{12,8},{9,1... | collective-permute-start | bytes 3145736 | tf_op jit(solution)/shard_map/ppermute | solution.py:417
  54.2 26.1 %all-to-all-start.1 = ((bf16[32,64,128]{2,1,0:T(8,128)(2,1)}), bf16[32,64,128]{2,1,0:T(8,128)(2,1)S(1)}, u32[]{:S(2)}, u32[]{:S(2)}) async-start(bf16[32,64,128]{2,1,0:T(8,128)(2,1)} %shard_map.137), calls=%async_computation.1 | async-start | bytes 1048576 | tf_op jit(solution)/shard_map/all_to_all | solution.py:487
  61.8 9.2 %collective-permute-start.10 = (bf16[32,4096]{1,0:T(8,128)(2,1)S(1)}, bf16[32,4096]{1,0:T(8,128)(2,1)S(1)}, u32[]{:S(2)}, u32[]{:S(2)}) collective-permute-start(bf16[32,4096]{1,0:T(8,128)(2,1)S(1)} %bitcast.15), channel_id=1, source_target_pairs={{0,3},{1,0},{2,1},{3,2},{4,7},{5,4},{6,5},{7,6},{8,11},{9,8},{10,9... | collective-permute-start | bytes 786440 | tf_op jit(solution)/shard_map/ppermute | solution.py:421
  64.3 7.8 %collective-permute-start.9 = (bf16[32,4096]{1,0:T(8,128)(2,1)S(1)}, bf16[32,4096]{1,0:T(8,128)(2,1)S(1)}, u32[]{:S(2)}, u32[]{:S(2)}) collective-permute-start(bf16[32,4096]{1,0:T(8,128)(2,1)S(1)} %bitcast.16), channel_id=1, source_target_pairs={{0,2},{1,3},{2,0},{3,1},{4,6},{5,7},{6,4},{7,5},{8,10},{9,11},{10,... | collective-permute-start | bytes 786440 | tf_op jit(solution)/shard_map/ppermute | solution.py:421
  64.6 15.0 %collective-permute-start.8 = (bf16[32,4096]{1,0:T(8,128)(2,1)S(1)}, bf16[32,4096]{1,0:T(8,128)(2,1)S(1)}, u32[]{:S(2)}, u32[]{:S(2)}) collective-permute-start(bf16[32,4096]{1,0:T(8,128)(2,1)S(1)} %bitcast.17), channel_id=1, source_target_pairs={{0,1},{1,2},{2,3},{3,0},{4,5},{5,6},{6,7},{7,4},{8,9},{9,10},{10,1... | collective-permute-start | bytes 786440 | tf_op jit(solution)/shard_map/ppermute | solution.py:421
  69.4 1.0 copy-start.3
  70.4 0.7 copy-start.14
  71.0 14.9 %copy-start.6 = (bf16[32,4096]{1,0:T(8,128)(2,1)}, bf16[32,4096]{1,0:T(8,128)(2,1)S(1)}, u32[]{:S(2)}) copy-start(bf16[32,4096]{1,0:T(8,128)(2,1)S(1)} %collective-permute-done.10.w3) | copy-start | bytes 786436
  72.0 0.7 copy-start.8
  79.6 0.7 copy-start.10
  80.3 1.2 copy-start.1
  85.9 0.7 copy-start.12
  86.6 21.4 %all-to-all-start.2 = ((bf16[32,32,128]{2,1,0:T(8,128)(2,1)}), bf16[32,32,128]{2,1,0:T(8,128)(2,1)S(1)}, u32[]{:S(2)}, u32[]{:S(2)}) async-start(bf16[32,32,128]{2,1,0:T(8,128)(2,1)} %copy-done.12), calls=%async_computation.2 | async-start | bytes 524288 | tf_op jit(solution)/shard_map/all_to_all | solution.py:508
  95.9 4.1 %collective-permute-start.14 = (bf16[32,128]{1,0:T(8,128)(2,1)}, bf16[32,128]{1,0:T(8,128)(2,1)S(1)}, u32[]{:S(2)}, u32[]{:S(2)}) collective-permute-start(bf16[32,128]{1,0:T(8,128)(2,1)} %get-tuple-element.63), channel_id=1, source_target_pairs={{0,1},{1,2},{2,3},{3,0},{4,5},{5,6},{6,7},{7,4},{8,9},{9,10},{10,1... | collective-permute-start | bytes 24584 | tf_op jit(solution)/shard_map/ppermute | solution.py:421
  96.0 5.8 %collective-permute-start.15 = (bf16[32,128]{1,0:T(8,128)(2,1)}, bf16[32,128]{1,0:T(8,128)(2,1)S(1)}, u32[]{:S(2)}, u32[]{:S(2)}) collective-permute-start(bf16[32,128]{1,0:T(8,128)(2,1)} %get-tuple-element.64), channel_id=1, source_target_pairs={{0,2},{1,3},{2,0},{3,1},{4,6},{5,7},{6,4},{7,5},{8,10},{9,11},{10,... | collective-permute-start | bytes 24584 | tf_op jit(solution)/shard_map/ppermute | solution.py:421
  96.4 5.8 %collective-permute-start.16 = (bf16[32,128]{1,0:T(8,128)(2,1)S(1)}, bf16[32,128]{1,0:T(8,128)(2,1)S(1)}, u32[]{:S(2)}, u32[]{:S(2)}) collective-permute-start(bf16[32,128]{1,0:T(8,128)(2,1)S(1)} %get-tuple-element.65), channel_id=1, source_target_pairs={{0,3},{1,0},{2,1},{3,2},{4,7},{5,4},{6,5},{7,6},{8,11},{9,8},{10,9... | collective-permute-start | bytes 24584 | tf_op jit(solution)/shard_map/ppermute | solution.py:421
  98.6 4.1 %collective-permute-start.17 = (bf16[32,128]{1,0:T(8,128)(2,1)S(1)}, bf16[32,128]{1,0:T(8,128)(2,1)S(1)}, u32[]{:S(2)}, u32[]{:S(2)}) collective-permute-start(bf16[32,128]{1,0:T(8,128)(2,1)S(1)} %get-tuple-element.62.a0), channel_id=1, source_target_pairs={{0,4},{4,0},{1,5},{5,1},{2,6},{6,2},{3,7},{7,3},{8,12},{12,8},{9,1... | collective-permute-start | bytes 24584 | tf_op jit(solution)/shard_map/ppermute | solution.py:417
  100.0 2.8 %collective-permute-start.18 = (bf16[32,128]{1,0:T(8,128)(2,1)S(1)}, bf16[32,128]{1,0:T(8,128)(2,1)S(1)}, u32[]{:S(2)}, u32[]{:S(2)}) collective-permute-start(bf16[32,128]{1,0:T(8,128)(2,1)S(1)} %collective-permute-done.14.a1), channel_id=1, source_target_pairs={{0,4},{4,0},{1,5},{5,1},{2,6},{6,2},{3,7},{7,3},{8,12},{12,8},{9,1... | collective-permute-start | bytes 24584 | tf_op jit(solution)/shard_map/ppermute | solution.py:417
  101.8 1.2 collective-permute-start.19
  102.2 1.4 %collective-permute-start.20 = (bf16[32,128]{1,0:T(8,128)(2,1)S(1)}, bf16[32,128]{1,0:T(8,128)(2,1)S(1)}, u32[]{:S(2)}, u32[]{:S(2)}) collective-permute-start(bf16[32,128]{1,0:T(8,128)(2,1)S(1)} %collective-permute-done.16.a3), channel_id=1, source_target_pairs={{0,4},{4,0},{1,5},{5,1},{2,6},{6,2},{3,7},{7,3},{8,12},{12,8},{9,1... | collective-permute-start | bytes 24584 | tf_op jit(solution)/shard_map/ppermute | solution.py:417
  103.6 0.9 copy-start.7
  104.5 0.9 copy-start.9
  105.5 0.9 copy-start.11
  108.0 0.7 copy-start.16
  108.7 10.6 %copy-start.15 = (f32[2,128,128]{2,1,0:T(8,128)S(1)}, f32[2,128,128]{2,1,0:T(8,128)}, u32[]{:S(2)}) copy-start(f32[2,128,128]{2,1,0:T(8,128)} %copy-done.14) | copy-start | bytes 393220
  108.7 18.8 %all-to-all-start.3 = ((bf16[32,16,128]{2,1,0:T(8,128)(2,1)}), bf16[32,16,128]{2,1,0:T(8,128)(2,1)S(1)}, u32[]{:S(2)}, u32[]{:S(2)}) async-start(bf16[32,16,128]{2,1,0:T(8,128)(2,1)} %copy-done.16), calls=%async_computation.3 | async-start | bytes 262144 | tf_op jit(solution)/shard_map/all_to_all | solution.py:518
  118.3 6.2 %collective-permute-start.22 = (f32[2,16]{1,0:T(2,128)S(1)}, f32[2,16]{1,0:T(2,128)S(1)}, u32[]{:S(2)}, u32[]{:S(2)}) collective-permute-start(f32[2,16]{1,0:T(2,128)S(1)} %slice.10), channel_id=1, source_target_pairs={{0,4},{4,0},{1,5},{5,1},{2,6},{6,2},{3,7},{7,3},{8,12},{12,8},{9,1... | collective-permute-start | bytes 392 | tf_op jit(solution)/shard_map/ppermute | solution.py:417
  119.3 1.2 copy-start.4
  123.9 6.2 %collective-permute-start.13 = (bf16[2,128,128]{2,1,0:T(8,128)(2,1)}, bf16[2,128,128]{2,1,0:T(8,128)(2,1)S(1)}, u32[]{:S(2)}, u32[]{:S(2)}) collective-permute-start(bf16[2,128,128]{2,1,0:T(8,128)(2,1)} %get-tuple-element.58), channel_id=1, source_target_pairs={{0,4},{4,0},{1,5},{5,1},{2,6},{6,2},{3,7},{7,3},{8,12},{12,8},{9,1... | collective-permute-start | bytes 196616 | tf_op jit(solution)/shard_map/ppermute | solution.py:417
  124.0 6.1 %collective-permute-start.12 = (bf16[128,1024]{1,0:T(8,128)(2,1)}, bf16[128,1024]{1,0:T(8,128)(2,1)S(1)}, u32[]{:S(2)}, u32[]{:S(2)}) collective-permute-start(bf16[128,1024]{1,0:T(8,128)(2,1)} %get-tuple-element.56), channel_id=1, source_target_pairs={{0,4},{4,0},{1,5},{5,1},{2,6},{6,2},{3,7},{7,3},{8,12},{12,8},{9,1... | collective-permute-start | bytes 786440 | tf_op jit(solution)/shard_map/ppermute | solution.py:417
  127.5 4.0 %collective-permute-start.21 = (bf16[32,16,128]{2,1,0:T(8,128)(2,1)S(1)}, bf16[32,16,128]{2,1,0:T(8,128)(2,1)S(1)}, u32[]{:S(2)}, u32[]{:S(2)}) collective-permute-start(bf16[32,16,128]{2,1,0:T(8,128)(2,1)S(1)} %all-to-all-done.3.own), channel_id=1, source_target_pairs={{0,4},{4,0},{1,5},{5,1},{2,6},{6,2},{3,7},{7,3},{8,12},{12,8},{9,1... | collective-permute-start | bytes 393224 | tf_op jit(solution)/shard_map/ppermute | solution.py:417

commit v3 on v2

--- a/solution.py
+++ b/solution.py
@@ -6,6 +6,8 @@
 from jax.sharding import Mesh
 from jax.sharding import PartitionSpec as P
 
+LIMITS = 16, 16, 16, 16, 60
+STATE_LIMIT, INTRA_LIMIT, PRE_LIMIT, GRADS_LIMIT, INPUT_LIMIT = LIMITS
 BF = jnp.bfloat16
 F32 = jnp.float32
 CHIPS, CORES, TP = 32, 2, 4
@@ -52,12 +54,15 @@
     return jnp.concatenate(stack, 0).T.astype(BF)
 
 
-def spread_maps():
-    row = lax.broadcasted_iota(jnp.int32, (128, 2 * W), 0)
-    col = lax.broadcasted_iota(jnp.int32, (128, 2 * W), 1)
-    part = row // 48
-    same = (row % 16) == (col % W) // HD
-    return jnp.where(same & (part == col // W), 1.0, 0.0).astype(BF)
+def spreader():
+    row = iota((128, 256), 0)
+    off = row % HH - iota((128, 256), 1) // HD
+    offs = [jnp.where(row // 48 == part, off, -99) for part in range(2)]
+
+    def spread(cols, part, k):
+        return dot(cols, jnp.where(offs[part] == 4 * k, 1.0, 0.0).astype(BF))
+
+    return spread
 
 
 def copy_all(pairs, sems, first=0):
@@ -72,53 +77,66 @@
         c.wait()
 
 
-def project_kernel(scal, w, bias, l0, l1, l2, l3, own, other, rows_out, sems):
-    pieces = (l0, l1, l2, l3)
-    copies = copy_all(
-        [(v, rows_out.at[pl.ds(32 * k, 32)]) for k, v in enumerate(pieces)], sems
-    )
+def parts_of(pack):
+    views = []
+    for at, width in ((0, W), (W, W), (2 * W, N), (2 * W + N, N)):
+        views.append(pack.at[:, pl.ds(at, width)])
+    return views
+
+
+def pack_kernel(scal, x, y, bm, cm, mine, theirs):
+    first = scal[1]
+    for out, side in ((mine, first), (theirs, 1 - first)):
+        at = 0
+        for v, width in ((x, W), (y, W), (bm, N), (cm, N)):
+            place = pl.ds(pl.multiple_of(side * width, width), width)
+            out[:, at : at + width] = v[:, place]
+            at += width
+
+
+def project_kernel(scal, w, params, l0, l1, l2, l3, own, other):
     first = scal[1]
     head = iota((2 * HH, 2 * HH), 0)
     head = jnp.where(first == 0, head, lax.rem(head + HH, 2 * HH))
     mine = iota((2 * HH, 2 * HH), 1) == head
-    add = jnp.sum(jnp.where(mine, bias[...], 0.0), axis=1, keepdims=True)
-    rows = jnp.concatenate([v[...] for v in pieces], 0)
+    add = jnp.sum(jnp.where(mine, params[0:1], 0.0), axis=1, keepdims=True)
+    rate = jnp.exp(jnp.sum(jnp.where(mine, params[1:2], 0.0), axis=1, keepdims=True))
+    own[1] = jnp.broadcast_to(rate[:HH], (HH, 128))
+    rows = jnp.concatenate([l0[...], l1[...], l2[...], l3[...]], 0)
     acc = pltpu.roll(dot_nt(w[...], rows), scal[0], 1) + add
-    own[...] = acc[:HH]
+    own[0] = acc[:HH]
     other[...] = acc[HH:]
-    wait_all(copies)
 
 
 def state_kernel(
-    scal, po, pp, alog, xo, xp, yo, yp, bo, bp, co, cp, maps,
-    msg_out, keep_out, small_out,
-    s_all, p_all, decay, msg, keep, small, sems,
+    scal, po, pp, own, other,
+    msg_out, keep, small,
+    s_all, p_all, decay, msg, sems,
 ):
     first = scal[1]
     second = 1 - first
-    pre = jnp.concatenate([po[...], pp[...]], 0)
+    pre = jnp.concatenate([po[0], pp[...]], 0)
     step = jnp.maximum(pre, 0.0) + jnp.log1p(jnp.exp(-jnp.abs(pre)))
-    mine = iota((2 * HH, 2 * HH), 1) == lax.rem(iota((2 * HH, 2 * HH), 0), HH) + HH * first
-    rate = jnp.exp(jnp.sum(jnp.where(mine, alog[...], 0.0), axis=1, keepdims=True))
-    rate = jnp.broadcast_to(rate, (2 * HH, 128))
+    rate = jnp.concatenate([po[1], po[1]], 0)
     cum = sum_by(-rate * step, triangle(lambda u, t: u <= t))
     small[0] = pre
     small[1] = step
     small[2] = cum
     small[3] = rate
-    copies = copy_all([(small, small_out)], sems)
+    copies = []
+    spread = spreader()
     remain_step = jnp.exp(cum[:, SPAN - 1 :] - cum) * step
     growth = jnp.exp(cum)
-    for b, (x, y, bm, cm) in enumerate(((xo, yo, bo, co), (xp, yp, bp, cp))):
+    for b, (x, y, bm, cm) in enumerate((parts_of(own), parts_of(other))):
         rows = slice(b * HH, (b + 1) * HH)
         weights = columns(remain_step[rows], growth[rows])
         b_t = bm[...].astype(F32).T.astype(BF)
         c_t = cm[...].astype(F32).T.astype(BF)
         for k in range(W // 256):
             cols = slice(k * 256, (k + 1) * 256)
-            w_in = dot(weights, maps[:, cols])
+            w_in = spread(weights, 0, k)
             s_all[b, :, cols] = dot(b_t, (w_in * x[:, cols].astype(F32)).astype(BF))
-            w_out = dot(weights, maps[:, W + k * 256 : W + (k + 1) * 256])
+            w_out = spread(weights, 1, k)
             p_all[b, :, cols] = dot(c_t, (w_out * y[:, cols].astype(F32)).astype(BF))
             decay[b, :, cols] = jnp.broadcast_to(w_out[SPAN - 1 :], (8, 256))
     per = N // PIECE
@@ -137,8 +155,7 @@
             msg[k * per + r] = whole.astype(BF)
         if k % 2 == 1:
             done = pl.ds((k - 1) * per, 2 * per)
-            copies += copy_all([(msg.at[done], msg_out.at[done])], sems, 1 + k // 2)
-    copies += copy_all([(keep, keep_out)], sems, 5)
+            copies += copy_all([(msg.at[done], msg_out.at[done])], sems, k // 2)
     wait_all(copies)
 
 
@@ -156,9 +173,14 @@
 
 
 def intra_kernel(
-    small_in, xo, xp, yo, yp, bo, bp, co, cp, gs, gb, gc, sums_out, small, sums_v, sems
+    small, own, other,
+    wide, gb, gc, sums_v,
+    gs,
 ):
-    wait_all(copy_all([(small_in, small)], sems))
+    spread = spreader()
+    step, cum = small[1], small[2]
+    remain = jnp.exp(cum[:, SPAN - 1 :] - cum)
+    growth = jnp.exp(cum)
     lane = iota((SPAN, 128), 1)
     low = lane < HD
     later = lane >= iota((SPAN, SPAN), 0)
@@ -166,7 +188,7 @@
     cum_t = jnp.concatenate([small[2], jnp.zeros((96, 128), F32)], 0).T
     sums = jnp.zeros((SPAN, 128), F32)
     zero = jnp.zeros((SPAN, 128), BF)
-    for b, (x, y, bm, cm) in enumerate(((xo, yo, bo, co), (xp, yp, bp, cp))):
+    for b, (x, y, bm, cm) in enumerate((parts_of(own), parts_of(other))):
         scores = dot_nt(bm[...], cm[...])
         grad_scores = jnp.zeros((SPAN, SPAN), F32)
         for pair in range(HH // 2):
@@ -177,8 +199,8 @@
                 h = b * HH + pair * 2 + side
                 mine = jnp.where(low if side == 0 else ~low, xs, zero)
                 grad_mixing = dot_nt(mine, ys)
-                spread = small[2, h : h + 1, :] - cum_t[:, h : h + 1]
-                decay = jnp.where(later, jnp.exp(jnp.minimum(spread, 0.0)), 0.0)
+                gap = small[2, h : h + 1, :] - cum_t[:, h : h + 1]
+                decay = jnp.where(later, jnp.exp(jnp.minimum(gap, 0.0)), 0.0)
                 mixing = scores * decay
                 halves.append(dot(mixing.astype(BF), ys))
                 scaled = grad_mixing * step_t[:, h : h + 1]
@@ -187,11 +209,20 @@
                 col = jnp.sum(grad_mixing * mixing, axis=1, keepdims=True)
                 sums = jnp.where(lane == h, col, sums)
             gs[b, :, cols] = jnp.where(low, halves[0], halves[1])
+        rows = slice(b * HH, (b + 1) * HH)
+        w_a = columns(remain[rows] * step[rows], growth[rows])
+        w_b = columns(step[rows], step[rows])
+        for k in range(W // 256):
+            cols = slice(k * 256, (k + 1) * 256)
+            remain_w = spread(w_a, 0, k)
+            wide[1, b, :, cols] = remain_w.astype(BF)
+            wide[2, b, :, cols] = (remain_w * x[:, cols].astype(F32)).astype(BF)
+            wide[3, b, :, cols] = (spread(w_a, 1, k) * y[:, cols].astype(F32)).astype(BF)
+            wide[0, b, :, cols] = (gs[b, :, cols] * spread(w_b, 0, k)).astype(BF)
         gs_bf = grad_scores.astype(BF)
         gb[b] = dot(gs_bf, cm[...])
         gc[b] = dot(grad_scores.T.astype(BF), bm[...])
     sums_v[1] = sums.T[: 2 * HH]
-    wait_all(copy_all([(sums_v, sums_out)], sems, 1))
 
 
 def block_decays(small, decay):
@@ -235,24 +266,19 @@
 
 
 def pre_kernel(
-    scal, got, keep_in, small_in, sums_in,
-    xo, xp, yo, yp, bo, bp, co, cp, lo_in, lp_in,
-    z0, z1, z2, z3, msg_out,
-    start, end, exact, decay, keep, small, sums_v, rows_v, zed, msg, sems,
+    scal, got, keep, small, sums_v, own, other, lo_in, lp_in,
+    zed_own, zed_other, msg_out,
+    start, end, exact, decay, rows_v, msg, sems,
 ):
-    early = copy_all([(small_in, small), (keep_in, keep)], sems)
     late = copy_all(
-        [(sums_in, sums_v), (lo_in, rows_v.at[pl.ds(0, 128)]), (lp_in, rows_v.at[pl.ds(128, 128)])],
-        sems,
-        2,
-    )
-    wait_all(early)
+        [(v, rows_v.at[pl.ds(SPAN * k, SPAN)]) for k, v in enumerate((lo_in, lp_in))], sems, 4
+    )
     block_decays(small, decay)
     assemble(scal, got, keep, decay, start, end, exact)
     by_head = head_map((W, 128), 1, 0)
     sums = []
     joint = []
-    for b, (x, y, bm, cm) in enumerate(((xo, yo, bo, co), (xp, yp, bp, cp))):
+    for b, (x, y, bm, cm) in enumerate((parts_of(own), parts_of(other))):
         for grad, mat, state in ((x, bm, end), (y, cm, start)):
             total = jnp.zeros((SPAN, 128), F32)
             for k in range(W // 256):
@@ -269,7 +295,6 @@
     last = cum[:, SPAN - 1 :]
     rate = small[3]
     q = jnp.exp(last - cum) * x_pulled
-    wait_all(late)
     cols = sums_v[1]
     u = sums_v[0] - step * cols + jnp.exp(cum) * y_state
     grad_log = (
@@ -282,8 +307,9 @@
     rolled = pltpu.roll(grad_pre, scal[2], 1)
     for k in range(TP):
         turn = rolled if k == 0 else pltpu.roll(rolled, 128 - 32 * k, 1)
-        zed[k] = turn.astype(BF)
-    copies = copy_all([(zed.at[k], z) for k, z in enumerate((z0, z1, z2, z3))], sems, 5)
+        zed_own[k] = turn[:HH].astype(BF)
+        zed_other[k] = turn[HH:].astype(BF)
+    copies = []
     rolled = jnp.concatenate([rolled[:HH], rolled[HH:]], 1).astype(BF)
     diagonal = iota((HH, 128), 0) == iota((HH, 128), 1)
 
@@ -292,6 +318,7 @@
         v = jnp.sum(v, axis=1, keepdims=True)
         return jnp.sum(jnp.where(diagonal, v, 0.0), axis=0, keepdims=True)
 
+    wait_all(late)
     extra = split3(as_row(grad_pre)) + split3(as_row(-grad_log * step))
     extra = jnp.concatenate(extra + [jnp.zeros((10, 128), F32)], 0).astype(BF)
     for k in range(D // 256):
@@ -302,7 +329,7 @@
             msg[2 * k + j, HH : 2 * HH, :] = extra
         if k % 4 == 3:
             done = pl.ds(2 * k - 6, 8)
-            copies += copy_all([(msg.at[done], msg_out.at[done])], sems, 9 + k // 4)
+            copies += copy_all([(msg.at[done], msg_out.at[done])], sems, k // 4)
     wait_all(copies)
 
 
@@ -320,37 +347,30 @@
 
 
 def grads_kernel(
-    scal, got, keep_in, small_in, gs, gb, gc, maps,
-    xo, xp, yo, yp, bo, bp, co, cp,
-    gx_own, gx_other, bc_own, bc_other,
-    start, end, decay, keep, small, sems,
+    scal, got, keep, small, wide_in, gb, gc, own, other, totals,
+    out_own, out_other,
+    start, end, decay, wide, sems,
 ):
-    wait_all(copy_all([(small_in, small), (keep_in, keep)], sems))
+    loads = copy_all([(wide_in, wide)], sems)
+    gs, remain, in_w, out_w = [wide.at[i] for i in range(4)]
     block_decays(small, decay)
     assemble(scal, got, keep, decay, start, end, None)
-    step, cum = small[1], small[2]
-    remain = jnp.exp(cum[:, SPAN - 1 :] - cum)
-    growth = jnp.exp(cum)
-    for b, (x, y, bm, cm) in enumerate(((xo, yo, bo, co), (xp, yp, bp, cp))):
-        rows = slice(b * HH, (b + 1) * HH)
-        w_a = columns(remain[rows], growth[rows])
-        w_b = columns(step[rows], step[rows])
+    wait_all(loads)
+    for b, bm in enumerate((parts_of(own)[2], parts_of(other)[2])):
         grad_b, grad_c = gb[b], gc[b]
-        gx_out, bc_out = ((gx_own, bc_own), (gx_other, bc_other))[b]
+        out = (out_own, out_other)[b]
         for k in range(W // 256):
             cols = slice(k * 256, (k + 1) * 256)
-            wide = slice(W + k * 256, W + (k + 1) * 256)
-            remain_w = dot(w_a, maps[:, cols])
-            step_w = dot(w_b, maps[:, cols])
-            growth_w = dot(w_a, maps[:, wide])
             pulled = dot(bm[...], end[b, :, cols])
-            gx_out[:, cols] = (step_w * (gs[b, :, cols] + remain_w * pulled)).astype(BF)
-            in_w = (remain_w * (step_w * x[:, cols].astype(F32))).astype(BF)
-            out_w = (growth_w * y[:, cols].astype(F32)).astype(BF)
-            grad_b = grad_b + dot_nt(in_w, end[b, :, cols])
-            grad_c = grad_c + dot_nt(out_w, start[b, :, cols])
-        bc_out[0] = grad_b.astype(BF)
-        bc_out[1] = grad_c.astype(BF)
+            out[:SPAN, cols] = (
+                gs[b, :, cols].astype(F32) + remain[b, :, cols].astype(F32) * pulled
+            ).astype(BF)
+            grad_b = grad_b + dot_nt(in_w[b, :, cols], end[b, :, cols])
+            grad_c = grad_c + dot_nt(out_w[b, :, cols], start[b, :, cols])
+        out[:SPAN, W : W + N] = grad_b.astype(BF)
+        out[:SPAN, W + N :] = grad_c.astype(BF)
+        spare = jnp.concatenate(split3(totals[...]) + [jnp.zeros((8, 128), F32)], 0)
+        out[SPAN:, :128] = spare.astype(BF)
 
 
 def weight_kernel(scal, own, other, out):
@@ -362,32 +382,46 @@
         out[HH : 2 * HH, cols] = jnp.where(at_zero, b, a)
 
 
-def join_kernel(scal, gx_own, gx_other, bc_own, bc_other, gx, gb, gc):
+def join_kernel(scal, own, other, params, gx, gb, gc, g_bias, g_rate):
     at_zero = scal[1] == 0
 
-    def join(own, other, out, width):
-        out[:, :width] = jnp.where(at_zero, own, other)
-        out[:, width:] = jnp.where(at_zero, other, own)
-
-    join(gx_own[...], gx_other[...], gx, W)
-    join(bc_own[0], bc_other[0], gb, N)
-    join(bc_own[1], bc_other[1], gc, N)
-
-
-def input_kernel(scal, a0, a1, a2, a3, b0, b1, b2, b3, w0, w1, w2, w3, out):
+    def join(a, b):
+        return jnp.where(at_zero, a, b), jnp.where(at_zero, b, a)
+
+    for out, at, width in ((gx, 0, W), (gb, W, N), (gc, W + N, N)):
+        cols = slice(at, at + width)
+        out[:, :width], out[:, width:] = join(own[:SPAN, cols], other[:SPAN, cols])
+    sums = []
+    for v in (own, other):
+        v = v[SPAN:, :128].astype(F32)
+        sums.append(v[:8] + v[8:16] + v[16:24])
+    low, high = join(*sums)
+    lane = iota((8, 128), 1)
+    total = jnp.where(lane < HH, low, pltpu.roll(high, HH, 1))
+    g_bias[...] = total[0:1, : 2 * HH]
+    g_rate[...] = total[1:2, : 2 * HH] * jnp.exp(params[1:2])
+
+
+def turn_kernel(own, other, *outs):
+    for k, out in enumerate(outs):
+        out[:HH] = own[k]
+        out[HH:] = other[k]
+
+
+def input_kernel(scal, a0, a1, a2, a3, w0, w1, w2, w3, out, mat, sems):
     first = scal[1]
-    mine = pl.ds(pl.multiple_of(HH * first, HH), HH)
-    others = pl.ds(pl.multiple_of(HH * (1 - first), HH), HH)
-    rows = []
-    for a, b in ((a0, b0), (a1, b1), (a2, b2), (a3, b3)):
-        rows += [a[:HH], b[HH:]]
+    copies = []
+    for k, w in enumerate((w0, w1, w2, w3)):
+        for j, side in enumerate((first, 1 - first)):
+            part = w.at[pl.ds(pl.multiple_of(HH * side, HH), HH)]
+            place = mat.at[pl.ds(2 * HH * k + HH * j, HH)]
+            copies += copy_all([(part, place)], sems, 2 * k + j)
+    rows = [a[...] for a in (a0, a1, a2, a3)]
     zed = jnp.concatenate(rows, 0).astype(F32).T[:32].astype(BF)
+    wait_all(copies)
     for k in range(D // 512):
         cols = slice(k * 512, (k + 1) * 512)
-        mats = []
-        for w in (w0, w1, w2, w3):
-            mats += [w[mine, cols], w[others, cols]]
-        out[:, cols] = dot(zed, jnp.concatenate(mats, 0)).astype(BF)
+        out[:, cols] = dot(zed, mat[:, cols]).astype(BF)
 
 
 def call(kernel, outs, args, scratch=(), sems=0, far_in=(), far_out=(), flops=0, moved=0, limit=16):
@@ -408,7 +442,7 @@
         in_specs=specs,
         out_specs=[far if i in far_out else near for i in range(len(outs))],
         scratch_shapes=shapes,
-        compiler_params=pltpu.CompilerParams(vmem_limit_bytes=limit * 2**20),
+        compiler_params=pltpu.CompilerParams(vmem_limit_bytes=int(limit * 2**20)),
         cost_estimate=pl.CostEstimate(flops=flops, bytes_accessed=moved, transcendentals=0),
     )(*args)
 
@@ -437,19 +471,18 @@
     weight_mine = jnp.concatenate(
         [half(weight_t, core, HH, 0), half(weight_t, 1 - core, HH, 0)], 0
     )
-    operands = []
-    for v, width in ((ssm_input, W), (out_grad, W), (b_in, N), (c_in, N)):
-        operands += [half(v, core, width, 1), swap(half(v, 1 - core, width, 1))]
-    maps = spread_maps()
+    pack_t = ((SPAN, 2 * W + 2 * N), BF)
+    mine, theirs = call(pack_kernel, [pack_t] * 2, [scal, ssm_input, out_grad, b_in, c_in])
+    operands = [mine, swap(theirs)]
+    params = jnp.stack([dt_bias, a_log])
     small_t = ((4, 2 * HH, 128), F32)
     keep_t = ((2, N, W), BF)
 
-    proj_own, proj_other, rows_own = call(
+    proj_own, proj_other = call(
         project_kernel,
-        [((HH, 128), F32)] * 2 + [((SPAN, D), BF)],
-        [scal, weight_mine, dt_bias[None, :]] + pieces,
-        sems=4,
-        far_out=(2,),
+        [((2, HH, 128), F32), ((HH, 128), F32)],
+        [scal, weight_mine, params] + pieces,
+        limit=16,
         flops=2**26,
         moved=2**21,
     )
@@ -458,90 +491,94 @@
     msg, keep, small = call(
         state_kernel,
         [msg_t, keep_t, small_t],
-        [scal, proj_own, proj_other, a_log[None, :]] + operands + [maps],
-        [((2, N, W), F32), ((2, N, W), F32), ((2, 8, W), F32), msg_t, keep_t, small_t],
-        sems=6,
-        far_out=(0, 1, 2),
+        [scal, proj_own, proj_other] + operands,
+        [((2, N, W), F32), ((2, N, W), F32), ((2, 8, W), F32), msg_t],
+        sems=4,
+        far_out=(0,),
+        limit=STATE_LIMIT,
         flops=2**28,
         moved=2**22,
     )
     got = lax.all_to_all(msg, "chip", 0, 0, tiled=True)
 
-    weight_t, rows_own = lax.optimization_barrier((weight_t, rows_own))
-    weights = [weight_t] + [round_tp(weight_t, k) for k in (1, 2, 3)]
+    weight_t, small = lax.optimization_barrier((weight_t, small))
+    near = [round_tp(weight_t, k) for k in (1, 3)]
+    far = round_tp(weight_t, 2)
+    rows_own = jnp.concatenate(pieces, 0)
     rows_other = swap(rows_own)
     sums_t = ((2, 2 * HH, 128), F32)
-    gs, gb, gc, sums = call(
+    wide_t = ((4, 2, SPAN, W), BF)
+    wide, gb, gc, sums = call(
         intra_kernel,
-        [((2, SPAN, W), F32), ((2, SPAN, N), F32), ((2, SPAN, N), F32), sums_t],
+        [wide_t, ((2, SPAN, N), F32), ((2, SPAN, N), F32), sums_t],
         [small] + operands,
-        [small_t, sums_t],
-        sems=2,
-        far_in=(0,),
-        far_out=(3,),
-    )
-
+        [((2, SPAN, W), F32)],
+        limit=INTRA_LIMIT,
+    )
+
+    got, near = lax.optimization_barrier((got, near))
     (folded,) = call(
-        fold_kernel, [((CHIPS, 2 * PIECE, 128), BF)], [got], flops=2**20, moved=2**20
+        fold_kernel, [((CHIPS, 2 * PIECE, 128), BF)], [got], flops=2**20, moved=2**20, limit=16
     )
     states = lax.all_to_all(folded, "chip", 0, 0, tiled=True)
-
-    states, weights = lax.optimization_barrier((states, weights))
-    zed_t = ((2 * HH, 128), BF)
+    states, far = lax.optimization_barrier((states, far))
+    weights = [weight_t, near[0], far, near[1]]
+
     parts_t = ((CHIPS, 2 * HH, 128), BF)
     state_scratch = [((2, N, W), BF), ((2, N, W), BF)]
-    kept = [((2, 8, W), F32), keep_t, small_t]
-    *zed, parts = call(
+    zed_own, zed_other, parts = call(
         pre_kernel,
-        [zed_t] * 4 + [parts_t],
+        [((TP, HH, 128), BF)] * 2 + [parts_t],
         [scal, states, keep, small, sums] + operands + [rows_own, rows_other],
         state_scratch
-        + [((2, 8, W), F32)]
-        + kept
-        + [sums_t, ((2 * SPAN, D), BF), ((TP, 2 * HH, 128), BF), parts_t],
-        sems=13,
-        far_in=(2, 3, 4, 13, 14),
-        far_out=(0, 1, 2, 3, 4),
+        + [((2, 8, W), F32), ((2, 8, W), F32), ((2 * SPAN, D), BF), parts_t],
+        sems=6,
+        far_in=(7, 8),
+        far_out=(2,),
         flops=2**29,
         moved=2**23,
+        limit=PRE_LIMIT,
     )
     shares = lax.all_to_all(parts, "chip", 0, 0, tiled=True)
 
+    zed = call(turn_kernel, [((2 * HH, 128), BF)] * TP, [zed_own, swap(zed_other)])
     zed = [zed[0]] + [round_tp(zed[k], k) for k in (1, 2, 3)]
+    shares, zed = lax.optimization_barrier((shares, zed))
+    total, totals = call(
+        sum_kernel, [((CHIPS, HH, 128), BF), ((8, 128), F32)], [shares], flops=2**20, moved=2**20, limit=16
+    )
+    weight_own = lax.all_to_all(total, "chip", 0, 0, tiled=True)
+
+    wide, zed, total = lax.optimization_barrier((wide, zed, total))
     (grad_layer_input,) = call(
-        input_kernel, [((32, D), BF)], [scal] + zed + [swap(z) for z in zed] + weights
-    )
-
-    total, totals = call(
-        sum_kernel, [((CHIPS, HH, 128), BF), ((8, 128), F32)], [shares], flops=2**20, moved=2**20
-    )
-    weight_own = lax.all_to_all(total, "chip", 0, 0, tiled=True)
-
-    def join(mine, other, axis):
-        return jnp.where(
-            core == 0,
-            jnp.concatenate([mine, other], axis),
-            jnp.concatenate([other, mine], axis),
-        )
-
-    totals = join(totals[:2, :HH], swap(totals[:2, :HH]), 1)
-    grad_dt_bias = totals[0]
-    grad_a_log = jnp.exp(a_log) * totals[1]
-
-    gs, total = lax.optimization_barrier((gs, total))
-    gx_own, gx_other, bc_own, bc_other = call(
+        input_kernel,
+        [((32, D), BF)],
+        [scal] + zed + weights,
+        [((TP * 2 * HH, D), BF)],
+        sems=8,
+        far_in=(5, 6, 7, 8),
+        limit=INPUT_LIMIT,
+    )
+
+    out_t = ((SPAN + 32, W + 2 * N), BF)
+    out_own, out_other = call(
         grads_kernel,
-        [((SPAN, W), BF)] * 2 + [((2, SPAN, N), BF)] * 2,
-        [scal, states, keep, small, gs, gb, gc, maps] + operands,
-        state_scratch + kept,
-        sems=2,
-        far_in=(2, 3),
-    )
-    grad_ssm_input, grad_b_in, grad_c_in = call(
+        [out_t] * 2,
+        [scal, states, keep, small, wide, gb, gc] + operands + [totals],
+        state_scratch + [((2, 8, W), F32), wide_t],
+        sems=1,
+        far_in=(4,),
+        limit=GRADS_LIMIT,
+    )
+    weight_own, out_own, out_other, grad_layer_input = lax.optimization_barrier(
+        (weight_own, out_own, out_other, grad_layer_input)
+    )
+    joined = call(
         join_kernel,
-        [((SPAN, 2 * W), BF), ((SPAN, 2 * N), BF), ((SPAN, 2 * N), BF)],
-        [scal, gx_own, swap(gx_other), bc_own, swap(bc_other)],
-    )
+        [((SPAN, 2 * W), BF), ((SPAN, 2 * N), BF), ((SPAN, 2 * N), BF)] + [((1, 2 * HH), F32)] * 2,
+        [scal, out_own, swap(out_other), params],
+    )
+    grad_ssm_input, grad_b_in, grad_c_in, grad_dt_bias, grad_a_log = joined
 
     (grad_dt_weight,) = call(
         weight_kernel,
@@ -556,8 +593,8 @@
         grad_c_in,
         grad_layer_input,
         grad_dt_weight.T,
-        grad_dt_bias,
-        grad_a_log,
+        grad_dt_bias[0],
+        grad_a_log[0],
     )
 
 

time: 134 us -> 124 us (0.925)
  other arithmetic: 4.61 us -> 0.1 us
  local copies, waits for them, and re-layouts: 18.1 us -> 14.3 us
  Pallas kernels: 21.6 us -> 24.1 us
  waiting for transfers between devices: 26.6 us -> 24.4 us
  starting transfers between devices: 61 us -> 58.9 us
    all_to_all x1, waiting for transfers between devices: 15.4 us -> 3.23 us  [local(): got = lax.all_to_all(msg, 'chip', 0, 0, tiled=True)]
    all_to_all x1, waiting for transfers between devices: 0.01 us -> 4.97 us  [local(): states = lax.all_to_all(folded, 'chip', 0, 0, tiled=True)]
    ppermute x14 -> x6, starting transfers between devices: 12.3 us -> 8.94 us  [swap(): return lax.ppermute(v, 'core', [(0, 1), (1, 0)])]
    ppermute x6, starting transfers between devices: 5.85 us -> 8.83 us  [round_tp(): return lax.ppermute(v, 'tp', [(i, (i + k) % TP) for i in range(TP)])]
    ppermute x3, waiting for transfers between devices: 0.02 us -> 2.55 us  [local(): lax.ppermute(layer_input, 'tp', [((i + k) % TP, i) for i in range(TP)])]
    pallas_call x10 -> x12, Pallas kernels: 21.6 us -> 24.1 us  [call(): pl.pallas_call(kernel, out_shape=[jax.ShapeDtypeStruct(s, t) for s, t in...]
    unnamed x62 -> x51, local copies, waits for them, and re-layouts: 14.7 us -> 12.3 us
    ppermute x14 -> x6, waiting for transfers between devices: 0.85 us -> 3.08 us  [swap(): return lax.ppermute(v, 'core', [(0, 1), (1, 0)])]
  transfers between devices with their start and end apart: 27 -> 19, of which waited for: 6 -> 12; matrix products, arithmetic and copies ran while one was open for 6% -> 3% of each run, Pallas kernels for 10% -> 12%
where the time goes in v3:
time: 124 us; the launch traced here: 123 us
  starting transfers between devices  58.9 us (48%)
  waiting for transfers between devices  24.4 us (20%)
  Pallas kernels  24.1 us (19%)
  local copies, waits for them, and re-layouts  14.3 us (12%)
    pallas_call x12, Pallas kernels, call(): pl.pallas_call(kernel, out_shape=[jax.ShapeDtypeStruct(s, t) for s, t in...  24.1 us
    unnamed x51, local copies, waits for them, and re-layouts  12.3 us
    all_to_all x1, starting transfers between devices, local(): got = lax.all_to_all(msg, 'chip', 0, 0, tiled=True)  11 us
    ppermute x6, starting transfers between devices, swap(): return lax.ppermute(v, 'core', [(0, 1), (1, 0)])  8.94 us
    ppermute x6, starting transfers between devices, round_tp(): return lax.ppermute(v, 'tp', [(i, (i + k) % TP) for i in range(TP)])  8.83 us
    all_to_all x1, starting transfers between devices, local(): weight_own = lax.all_to_all(total, 'chip', 0, 0, tiled=True)  8.12 us
    all_to_all x1, starting transfers between devices, local(): states = lax.all_to_all(folded, 'chip', 0, 0, tiled=True)  8.07 us
    all_to_all x1, starting transfers between devices, local(): shares = lax.all_to_all(parts, 'chip', 0, 0, tiled=True)  7.98 us
  transfers between devices with their start and end apart: 19, of which 12 were waited for; matrix products, arithmetic and copies ran while one was open for 3% of the time, Pallas kernels for 12%

profile of v3, /device:TPU:1, one launch (start us, length us, event | category | flops | bytes accessed | tf_op | source)
XLA Modules:
  0.0 122.7 jit_solution(1684421018883830994)
XLA Ops:
  0.6 2.2 %collective-permute-start.2 = (bf16[32,4096]{1,0:T(8,128)(2,1)}, bf16[32,4096]{1,0:T(8,128)(2,1)S(1)}, u32[]{:S(2)}, u32[]{:S(2)}) collective-permute-start(bf16[32,4096]{1,0:T(8,128)(2,1)} %l0.1), channel_id=1, source_target_pairs={{3,0},{0,1},{1,2},{2,3},{7,4},{4,5},{5,6},{6,7},{11,8},{8,9},{9,10... | collective-permute-start | bytes 786440 | tf_op jit(solution)/shard_map/ppermute | solution.py:467
  2.8 2.6 %collective-permute-start.1 = (bf16[32,4096]{1,0:T(8,128)(2,1)}, bf16[32,4096]{1,0:T(8,128)(2,1)S(1)}, u32[]{:S(2)}, u32[]{:S(2)}) collective-permute-start(bf16[32,4096]{1,0:T(8,128)(2,1)} %l0.1), channel_id=1, source_target_pairs={{2,0},{3,1},{0,2},{1,3},{6,4},{7,5},{4,6},{5,7},{10,8},{11,9},{8,1... | collective-permute-start | bytes 786440 | tf_op jit(solution)/shard_map/ppermute | solution.py:467
  5.5 1.1 collective-permute-start
  6.5 0.1 pad_add_fusion.scal
  6.6 1.0 copy-done.7
  7.7 1.0 copy-done.8
  8.7 0.8 copy-done.12
  9.5 0.8 copy-done.13
  10.4 1.5 %shard_map.136 = (bf16[128,2304]{1,0:T(8,128)(2,1)S(1)}, bf16[128,2304]{1,0:T(8,128)(2,1)}) custom-call(s32[3]{0:T(128)S(1)} %pad_add_fusion.scal, bf16[128,2048]{1,0:T(8,128)(2,1)S(1)} %copy-done.7, bf16[128,2048]{1,0:T(8,128)(2,1)S(1)} %copy-done.8, bf16[128,256]{1,0:T(8,128)(2,1)S(1)} %copy-done.12, bf16[128,256]{1,0:T(8,128)(2,1)S(1)} %copy-done.13), custom_call_target="tpu_custom_call" | custom-call | tf_op jit(solution)/shard_map/pallas_call | solution.py:439
  11.9 1.5 %collective-permute-start.4 = (bf16[128,2304]{1,0:T(8,128)(2,1)}, bf16[128,2304]{1,0:T(8,128)(2,1)S(1)}, u32[]{:S(2)}, u32[]{:S(2)}) collective-permute-start(bf16[128,2304]{1,0:T(8,128)(2,1)} %get-tuple-element.58), channel_id=1, source_target_pairs={{0,4},{4,0},{1,5},{5,1},{2,6},{6,2},{3,7},{7,3},{8,12},{12,8},{9,1... | collective-permute-start | bytes 1769480 | tf_op jit(solution)/shard_map/ppermute | solution.py:451
  13.4 1.0 dynamic-slice_bitcast_fusion.1
  14.4 0.0 collective-permute-done.2.l3
  14.4 0.0 copy-start.3
  14.5 2.5 %collective-permute-done.1.l2 = bf16[32,4096]{1,0:T(8,128)(2,1)S(1)} collective-permute-done((bf16[32,4096]{1,0:T(8,128)(2,1)}, bf16[32,4096]{1,0:T(8,128)(2,1)S(1)}, u32[]{:S(2)}, u32[]{:S(2)}) %collective-permute-start.1) | collective-permute-done | bytes 262176 | tf_op jit(solution)/shard_map/ppermute | solution.py:467
  17.0 0.0 copy-start.5
  17.0 1.1 shard_map.135
  18.1 1.6 %collective-permute-start.3 = (f32[16,128]{1,0:T(8,128)S(1)}, f32[16,128]{1,0:T(8,128)S(1)}, u32[]{:S(2)}, u32[]{:S(2)}) collective-permute-start(f32[16,128]{1,0:T(8,128)S(1)} %get-tuple-element.56), channel_id=1, source_target_pairs={{0,4},{4,0},{1,5},{5,1},{2,6},{6,2},{3,7},{7,3},{8,12},{12,8},{9,1... | collective-permute-start | bytes 24584 | tf_op jit(solution)/shard_map/ppermute | solution.py:451
  19.7 0.8 collective-permute-done.3.pp
  20.5 2.7 %shard_map.137 = (bf16[32,72,128]{2,1,0:T(8,128)(2,1)S(1)}, bf16[2,128,1024]{2,1,0:T(8,128)(2,1)S(1)}, f32[4,32,128]{2,1,0:T(8,128)S(1)}) custom-call(s32[3]{0:T(128)S(1)} %pad_add_fusion.scal, f32[2,16,128]{2,1,0:T(8,128)S(1)} %get-tuple-element.55.po, f32[16,128]{1,0:T(8,128)S(1)} %collective-permute-done.3.pp, ...), custom_call_target="tpu_custom_call" | custom-call | flops 268435456 | bytes 4194304 | tf_op jit(solution)/shard_map/pallas_call | solution.py:439
  23.2 0.8 copy-done.6
  24.1 11.0 %all-to-all-start = ((bf16[32,72,128]{2,1,0:T(8,128)(2,1)}), bf16[32,72,128]{2,1,0:T(8,128)(2,1)S(1)}, u32[]{:S(2)}, u32[]{:S(2)}) async-start(bf16[32,72,128]{2,1,0:T(8,128)(2,1)} %copy-done.6), calls=%async_computation | async-start | bytes 1179648 | tf_op jit(solution)/shard_map/all_to_all | solution.py:502
  35.1 1.0 constant_dynamic-update-slice_fusion.2
  36.1 1.0 constant_dynamic-update-slice_fusion.1
  37.0 1.9 %collective-permute-start.6 = (bf16[32,4096]{1,0:T(8,128)(2,1)}, bf16[32,4096]{1,0:T(8,128)(2,1)S(1)}, u32[]{:S(2)}, u32[]{:S(2)}) collective-permute-start(bf16[32,4096]{1,0:T(8,128)(2,1)} %bitcast.13), channel_id=1, source_target_pairs={{0,3},{1,0},{2,1},{3,2},{4,7},{5,4},{6,5},{7,6},{8,11},{9,8},{10,9... | collective-permute-start | bytes 786440 | tf_op jit(solution)/shard_map/ppermute | solution.py:455
  39.0 1.0 constant_dynamic-update-slice_fusion.lo_in
  40.0 1.0 collective-permute-start.8
  41.0 3.7 %collective-permute-done.6.w3 = bf16[32,4096]{1,0:T(8,128)(2,1)S(1)} collective-permute-done((bf16[32,4096]{1,0:T(8,128)(2,1)}, bf16[32,4096]{1,0:T(8,128)(2,1)S(1)}, u32[]{:S(2)}, u32[]{:S(2)}) %collective-permute-start.6) | collective-permute-done | bytes 262176 | tf_op jit(solution)/shard_map/ppermute | solution.py:455
  44.7 0.7 copy-done.18
  45.4 2.1 %collective-permute-done.5.w1 = bf16[32,4096]{1,0:T(8,128)(2,1)} collective-permute-done((bf16[32,4096]{1,0:T(8,128)(2,1)}, bf16[32,4096]{1,0:T(8,128)(2,1)}, u32[]{:S(2)}, u32[]{:S(2)}) %collective-permute-start.5) | collective-permute-done | bytes 262176 | tf_op jit(solution)/shard_map/ppermute | solution.py:455
  47.4 3.2 %all-to-all-done.msg = bf16[32,72,128]{2,1,0:T(8,128)(2,1)S(1)} async-done(((bf16[32,72,128]{2,1,0:T(8,128)(2,1)}), bf16[32,72,128]{2,1,0:T(8,128)(2,1)S(1)}, u32[]{:S(2)}, u32[]{:S(2)}) %all-to-all-start) | async-done | bytes 589856 | tf_op jit(solution)/shard_map/all_to_all | solution.py:502
  50.7 0.9 shard_map.138
  51.6 8.1 %all-to-all-start.1 = ((bf16[32,64,128]{2,1,0:T(8,128)(2,1)}), bf16[32,64,128]{2,1,0:T(8,128)(2,1)S(1)}, u32[]{:S(2)}, u32[]{:S(2)}) async-start(bf16[32,64,128]{2,1,0:T(8,128)(2,1)} %shard_map.138), calls=%async_computation.1 | async-start | bytes 1048576 | tf_op jit(solution)/shard_map/all_to_all | solution.py:523
  59.7 2.5 %collective-permute-start.7 = (bf16[32,4096]{1,0:T(8,128)(2,1)}, bf16[32,4096]{1,0:T(8,128)(2,1)}, u32[]{:S(2)}, u32[]{:S(2)}) collective-permute-start(bf16[32,4096]{1,0:T(8,128)(2,1)} %bitcast.15), channel_id=1, source_target_pairs={{0,2},{1,3},{2,0},{3,1},{4,6},{5,7},{6,4},{7,5},{8,10},{9,11},{10,... | collective-permute-start | bytes 786440 | tf_op jit(solution)/shard_map/ppermute | solution.py:455
  62.2 4.6 %shard_map.139 = (bf16[4,2,128,1024]{3,2,1,0:T(8,128)(2,1)S(1)}, f32[2,128,128]{2,1,0:T(8,128)S(1)}, f32[2,128,128]{2,1,0:T(8,128)S(1)}, f32[2,32,128]{2,1,0:T(8,128)S(1)}) custom-call(f32[4,32,128]{2,1,0:T(8,128)S(1)} %get-tuple-element.65.small, bf16[128,2304]{1,0:T(8,128)(2,1)S(1)} %get-tuple-element.57.own, ...), custom_call_target="tpu_custom_call" | custom-call | tf_op jit(solution)/shard_map/pallas_call | solution.py:439
  66.8 1.3 %copy-done = bf16[4,2,128,1024]{3,2,1,0:T(8,128)(2,1)} copy-done((bf16[4,2,128,1024]{3,2,1,0:T(8,128)(2,1)}, bf16[4,2,128,1024]{3,2,1,0:T(8,128)(2,1)S(1)}, u32[]{:S(2)}) %copy-start) | copy-done | bytes 2097176
  68.2 0.7 copy-done.10
  68.8 0.0 collective-permute-done.7.w2
  68.8 5.0 %all-to-all-done.1.got = bf16[32,64,128]{2,1,0:T(8,128)(2,1)S(1)} async-done(((bf16[32,64,128]{2,1,0:T(8,128)(2,1)}), bf16[32,64,128]{2,1,0:T(8,128)(2,1)S(1)}, u32[]{:S(2)}, u32[]{:S(2)}) %all-to-all-start.1) | async-done | bytes 524320 | tf_op jit(solution)/shard_map/all_to_all | solution.py:523
  73.8 5.0 %shard_map.140 = (bf16[4,16,128]{2,1,0:T(8,128)(2,1)S(1)}, bf16[4,16,128]{2,1,0:T(8,128)(2,1)S(1)}, bf16[32,32,128]{2,1,0:T(8,128)(2,1)S(1)}) custom-call(s32[3]{0:T(128)S(1)} %pad_add_fusion.scal, bf16[32,64,128]{2,1,0:T(8,128)(2,1)S(1)} %all-to-all-done.1.got, bf16[2,128,1024]{2,1,0:T(8,128)(2,1)S(1)} %get-tuple-element.64.keep, ...), custom_call_target="tpu_custom_call" | custom-call | flops 536870912 | bytes 8388608 | tf_op jit(solution)/shard_map/pallas_call | solution.py:439
  78.8 0.0 copy-start.9
  78.8 0.7 copy-done.9
  79.5 8.0 %all-to-all-start.2 = ((bf16[32,32,128]{2,1,0:T(8,128)(2,1)}), bf16[32,32,128]{2,1,0:T(8,128)(2,1)S(1)}, u32[]{:S(2)}, u32[]{:S(2)}) async-start(bf16[32,32,128]{2,1,0:T(8,128)(2,1)} %copy-done.9), calls=%async_computation.2 | async-start | bytes 524288 | tf_op jit(solution)/shard_map/all_to_all | solution.py:542
  87.5 1.6 %collective-permute-start.9 = (bf16[4,16,128]{2,1,0:T(8,128)(2,1)S(1)}, bf16[4,16,128]{2,1,0:T(8,128)(2,1)S(1)}, u32[]{:S(2)}, u32[]{:S(2)}) collective-permute-start(bf16[4,16,128]{2,1,0:T(8,128)(2,1)S(1)} %get-tuple-element.69), channel_id=1, source_target_pairs={{0,4},{4,0},{1,5},{5,1},{2,6},{6,2},{3,7},{7,3},{8,12},{12,8},{9,1... | collective-permute-start | bytes 49160 | tf_op jit(solution)/shard_map/ppermute | solution.py:451
  89.1 0.8 collective-permute-done.9.other
  89.9 0.9 collective-permute-start.10
  90.9 2.1 %collective-permute-start.11 = (bf16[32,128]{1,0:T(8,128)(2,1)S(1)}, bf16[32,128]{1,0:T(8,128)(2,1)S(1)}, u32[]{:S(2)}, u32[]{:S(2)}) collective-permute-start(bf16[32,128]{1,0:T(8,128)(2,1)S(1)} %get-tuple-element.72), channel_id=1, source_target_pairs={{0,2},{1,3},{2,0},{3,1},{4,6},{5,7},{6,4},{7,5},{8,10},{9,11},{10,... | collective-permute-start | bytes 24584 | tf_op jit(solution)/shard_map/ppermute | solution.py:455
  93.0 1.3 %collective-permute-start.12 = (bf16[32,128]{1,0:T(8,128)(2,1)S(1)}, bf16[32,128]{1,0:T(8,128)(2,1)S(1)}, u32[]{:S(2)}, u32[]{:S(2)}) collective-permute-start(bf16[32,128]{1,0:T(8,128)(2,1)S(1)} %get-tuple-element.73), channel_id=1, source_target_pairs={{0,3},{1,0},{2,1},{3,2},{4,7},{5,4},{6,5},{7,6},{8,11},{9,8},{10,9... | collective-permute-start | bytes 24584 | tf_op jit(solution)/shard_map/ppermute | solution.py:455
  94.3 0.0 collective-permute-done.10.a1
  94.3 0.9 collective-permute-done.11.a2
  95.2 0.6 collective-permute-done.12.a3
  95.8 1.4 %all-to-all-done.2.msg = bf16[32,32,128]{2,1,0:T(8,128)(2,1)S(1)} async-done(((bf16[32,32,128]{2,1,0:T(8,128)(2,1)}), bf16[32,32,128]{2,1,0:T(8,128)(2,1)S(1)}, u32[]{:S(2)}, u32[]{:S(2)}) %all-to-all-start.2) | async-done | bytes 262176 | tf_op jit(solution)/shard_map/all_to_all | solution.py:542
  97.2 0.7 shard_map.142
  97.9 8.1 %all-to-all-start.3 = ((bf16[32,16,128]{2,1,0:T(8,128)(2,1)}), bf16[32,16,128]{2,1,0:T(8,128)(2,1)S(1)}, u32[]{:S(2)}, u32[]{:S(2)}) async-start(bf16[32,16,128]{2,1,0:T(8,128)(2,1)} %get-tuple-element.75), calls=%async_computation.3 | async-start | bytes 262144 | tf_op jit(solution)/shard_map/all_to_all | solution.py:550
  106.0 3.1 %shard_map.144 = bf16[32,4096]{1,0:T(8,128)(2,1)} custom-call(s32[3]{0:T(128)} %copy-done.14, bf16[32,128]{1,0:T(8,128)(2,1)} %copy-done.16, bf16[32,128]{1,0:T(8,128)(2,1)} %copy-done.19, bf16[32,128]{1,0:T(8,128)(2,1)} %copy-done.20, bf16[32,128]{1,0:T(8,128)(2,1)} %copy-done.21, bf16[32,4096]{1,0:T(8,128)(2,1)} %bitcast.16, ...), custom_call_target="tpu_custom_call" | custom-call | tf_op jit(solution)/shard_map/pallas_call | solution.py:439
  109.2 1.6 %copy-done.1 = bf16[4,2,128,1024]{3,2,1,0:T(8,128)(2,1)S(1)} copy-done((bf16[4,2,128,1024]{3,2,1,0:T(8,128)(2,1)S(1)}, bf16[4,2,128,1024]{3,2,1,0:T(8,128)(2,1)}, u32[]{:S(2)}) %copy-start.1) | copy-done | bytes 2097176
  110.8 1.6 %shard_map.143 = (bf16[160,1280]{1,0:T(8,128)(2,1)S(1)}, bf16[160,1280]{1,0:T(8,128)(2,1)S(1)}) custom-call(s32[3]{0:T(128)S(1)} %copy-done.15, bf16[32,64,128]{2,1,0:T(8,128)(2,1)S(1)} %all-to-all-done.1.got, bf16[2,128,1024]{2,1,0:T(8,128)(2,1)S(1)} %get-tuple-element.64.keep, f32[4,32,128]{2,1,0:T(8,128)S(1)} %get-tuple-element.65.small, ...), custom_call_target="tpu_custom_call" | custom-call | tf_op jit(solution)/shard_map/pallas_call | solution.py:439
  112.5 0.0 copy-start.17
  112.5 0.7 copy-done.17
  113.2 1.9 %all-to-all-done.3.own = bf16[32,16,128]{2,1,0:T(8,128)(2,1)S(1)} async-done(((bf16[32,16,128]{2,1,0:T(8,128)(2,1)}), bf16[32,16,128]{2,1,0:T(8,128)(2,1)S(1)}, u32[]{:S(2)}, u32[]{:S(2)}) %all-to-all-start.3) | async-done | bytes 131104 | tf_op jit(solution)/shard_map/all_to_all | solution.py:550
  115.2 3.3 %collective-permute-start.13 = (bf16[160,1280]{1,0:T(8,128)(2,1)}, bf16[160,1280]{1,0:T(8,128)(2,1)S(1)}, u32[]{:S(2)}, u32[]{:S(2)}) collective-permute-start(bf16[160,1280]{1,0:T(8,128)(2,1)} %copy-done.17), channel_id=1, source_target_pairs={{0,4},{4,0},{1,5},{5,1},{2,6},{6,2},{3,7},{7,3},{8,12},{12,8},{9,1... | collective-permute-start | bytes 1228808 | tf_op jit(solution)/shard_map/ppermute | solution.py:451
  118.4 0.0 collective-permute-start.14
  118.4 1.4 %collective-permute-done.14.other = bf16[32,16,128]{2,1,0:T(8,128)(2,1)S(1)} collective-permute-done((bf16[32,16,128]{2,1,0:T(8,128)(2,1)S(1)}, bf16[32,16,128]{2,1,0:T(8,128)(2,1)S(1)}, u32[]{:S(2)}, u32[]{:S(2)}) %collective-permute-start.14) | collective-permute-done | bytes 131104 | tf_op jit(solution)/shard_map/ppermute | solution.py:451
  119.8 1.4 %shard_map.146 = f32[32,4096]{1,0:T(8,128)} custom-call(s32[3]{0:T(128)S(1)} %copy-done.15, bf16[32,16,128]{2,1,0:T(8,128)(2,1)S(1)} %all-to-all-done.3.own, bf16[32,16,128]{2,1,0:T(8,128)(2,1)S(1)} %collective-permute-done.14.other), custom_call_target="tpu_custom_call" | custom-call | flops 1048576 | bytes 4194304 | tf_op jit(solution)/shard_map/pallas_call | solution.py:439
  121.2 1.4 %shard_map.145 = (bf16[128,2048]{1,0:T(8,128)(2,1)}, bf16[128,256]{1,0:T(8,128)(2,1)}, bf16[128,256]{1,0:T(8,128)(2,1)}, f32[1,32]{1,0:T(1,128)}, f32[1,32]{1,0:T(1,128)}) custom-call(s32[3]{0:T(128)S(1)} %copy-done.15, bf16[160,1280]{1,0:T(8,128)(2,1)S(1)} %get-tuple-element.94.own, bf16[160,1280]{1,0:T(8,128)(2,1)S(1)} %collective-permute-done.13.other, ...), custom_call_target="tpu_custom_call" | custom-call | tf_op jit(solution)/shard_map/pallas_call | solution.py:439
  (42 shorter events, 0.1 us)
Async XLA Ops:
  0.6 16.4 %copy-start.2 = (bf16[32,4096]{1,0:T(8,128)(2,1)S(1)}, bf16[32,4096]{1,0:T(8,128)(2,1)}, u32[]{:S(2)}) copy-start(bf16[32,4096]{1,0:T(8,128)(2,1)} %l0.1) | copy-start | bytes 786436
  0.6 13.8 %collective-permute-start.2 = (bf16[32,4096]{1,0:T(8,128)(2,1)}, bf16[32,4096]{1,0:T(8,128)(2,1)S(1)}, u32[]{:S(2)}, u32[]{:S(2)}) collective-permute-start(bf16[32,4096]{1,0:T(8,128)(2,1)} %l0.1), channel_id=1, source_target_pairs={{3,0},{0,1},{1,2},{2,3},{7,4},{4,5},{5,6},{6,7},{11,8},{8,9},{9,10... | collective-permute-start | bytes 786440 | tf_op jit(solution)/shard_map/ppermute | solution.py:467
  2.8 14.2 %collective-permute-start.1 = (bf16[32,4096]{1,0:T(8,128)(2,1)}, bf16[32,4096]{1,0:T(8,128)(2,1)S(1)}, u32[]{:S(2)}, u32[]{:S(2)}) collective-permute-start(bf16[32,4096]{1,0:T(8,128)(2,1)} %l0.1), channel_id=1, source_target_pairs={{2,0},{3,1},{0,2},{1,3},{6,4},{7,5},{4,6},{5,7},{10,8},{11,9},{8,1... | collective-permute-start | bytes 786440 | tf_op jit(solution)/shard_map/ppermute | solution.py:467
  5.5 11.5 %collective-permute-start = (bf16[32,4096]{1,0:T(8,128)(2,1)}, bf16[32,4096]{1,0:T(8,128)(2,1)S(1)}, u32[]{:S(2)}, u32[]{:S(2)}) collective-permute-start(bf16[32,4096]{1,0:T(8,128)(2,1)} %l0.1), channel_id=1, source_target_pairs={{1,0},{2,1},{3,2},{0,3},{5,4},{6,5},{7,6},{4,7},{9,8},{10,9},{11,1... | collective-permute-start | bytes 786440 | tf_op jit(solution)/shard_map/ppermute | solution.py:467
  6.6 1.0 copy-start.7
  7.7 1.0 copy-start.8
  8.7 0.8 copy-start.12
  9.5 0.8 copy-start.13
  10.4 63.4 %copy-start.14 = (s32[3]{0:T(128)}, s32[3]{0:T(128)S(1)}, u32[]{:S(2)}) copy-start(s32[3]{0:T(128)S(1)} %pad_add_fusion.scal) | copy-start | bytes 40
  10.4 4.0 %copy-start.22 = (f32[32]{0:T(128)S(1)}, f32[32]{0:T(128)}, u32[]{:S(2)}) copy-start(f32[32]{0:T(128)} %param.11) | copy-start | bytes 388
  10.4 4.0 %copy-start.23 = (f32[32]{0:T(128)S(1)}, f32[32]{0:T(128)}, u32[]{:S(2)}) copy-start(f32[32]{0:T(128)} %param.10) | copy-start | bytes 388
  11.9 8.6 %collective-permute-start.4 = (bf16[128,2304]{1,0:T(8,128)(2,1)}, bf16[128,2304]{1,0:T(8,128)(2,1)S(1)}, u32[]{:S(2)}, u32[]{:S(2)}) collective-permute-start(bf16[128,2304]{1,0:T(8,128)(2,1)} %get-tuple-element.58), channel_id=1, source_target_pairs={{0,4},{4,0},{1,5},{5,1},{2,6},{6,2},{3,7},{7,3},{8,12},{12,8},{9,1... | collective-permute-start | bytes 1769480 | tf_op jit(solution)/shard_map/ppermute | solution.py:451
  14.4 9.6 %copy-start.3 = (bf16[32,4096]{1,0:T(8,128)(2,1)}, bf16[32,4096]{1,0:T(8,128)(2,1)S(1)}, u32[]{:S(2)}) copy-start(bf16[32,4096]{1,0:T(8,128)(2,1)S(1)} %collective-permute-done.2.l3) | copy-start | bytes 786436
  17.0 3.5 %copy-start.4 = (bf16[32,4096]{1,0:T(8,128)(2,1)}, bf16[32,4096]{1,0:T(8,128)(2,1)S(1)}, u32[]{:S(2)}) copy-start(bf16[32,4096]{1,0:T(8,128)(2,1)S(1)} %collective-permute-done.1.l2) | copy-start | bytes 786436
  17.0 3.5 %copy-start.5 = (bf16[32,4096]{1,0:T(8,128)(2,1)}, bf16[32,4096]{1,0:T(8,128)(2,1)S(1)}, u32[]{:S(2)}) copy-start(bf16[32,4096]{1,0:T(8,128)(2,1)S(1)} %collective-permute-done.l1) | copy-start | bytes 786436
  18.1 2.4 %collective-permute-start.3 = (f32[16,128]{1,0:T(8,128)S(1)}, f32[16,128]{1,0:T(8,128)S(1)}, u32[]{:S(2)}, u32[]{:S(2)}) collective-permute-start(f32[16,128]{1,0:T(8,128)S(1)} %get-tuple-element.56), channel_id=1, source_target_pairs={{0,4},{4,0},{1,5},{5,1},{2,6},{6,2},{3,7},{7,3},{8,12},{12,8},{9,1... | collective-permute-start | bytes 24584 | tf_op jit(solution)/shard_map/ppermute | solution.py:451
  23.2 0.8 copy-start.6
  24.1 26.6 %all-to-all-start = ((bf16[32,72,128]{2,1,0:T(8,128)(2,1)}), bf16[32,72,128]{2,1,0:T(8,128)(2,1)S(1)}, u32[]{:S(2)}, u32[]{:S(2)}) async-start(bf16[32,72,128]{2,1,0:T(8,128)(2,1)} %copy-done.6), calls=%async_computation | async-start | bytes 1179648 | tf_op jit(solution)/shard_map/all_to_all | solution.py:502
  37.0 7.6 %collective-permute-start.6 = (bf16[32,4096]{1,0:T(8,128)(2,1)}, bf16[32,4096]{1,0:T(8,128)(2,1)S(1)}, u32[]{:S(2)}, u32[]{:S(2)}) collective-permute-start(bf16[32,4096]{1,0:T(8,128)(2,1)} %bitcast.13), channel_id=1, source_target_pairs={{0,3},{1,0},{2,1},{3,2},{4,7},{5,4},{6,5},{7,6},{8,11},{9,8},{10,9... | collective-permute-start | bytes 786440 | tf_op jit(solution)/shard_map/ppermute | solution.py:455
  39.0 8.4 %collective-permute-start.5 = (bf16[32,4096]{1,0:T(8,128)(2,1)}, bf16[32,4096]{1,0:T(8,128)(2,1)}, u32[]{:S(2)}, u32[]{:S(2)}) collective-permute-start(bf16[32,4096]{1,0:T(8,128)(2,1)} %bitcast.14), channel_id=1, source_target_pairs={{0,1},{1,2},{2,3},{3,0},{4,5},{5,6},{6,7},{7,4},{8,9},{9,10},{10,1... | collective-permute-start | bytes 786440 | tf_op jit(solution)/shard_map/ppermute | solution.py:455
  40.0 33.8 %collective-permute-start.8 = (bf16[128,4096]{1,0:T(8,128)(2,1)S(1)}, bf16[128,4096]{1,0:T(8,128)(2,1)}, u32[]{:S(2)}, u32[]{:S(2)}) collective-permute-start(bf16[128,4096]{1,0:T(8,128)(2,1)S(1)} %constant_dynamic-update-slice_fusion.lo_in), channel_id=1, source_target_pairs={{0,4},{4,0},{1,5},{5,1},{2,6},{6,2},{3,7},{7,3},{8,12},{12,8},{9,1... | collective-permute-start | bytes 3145736 | tf_op jit(solution)/shard_map/ppermute | solution.py:451
  44.7 0.7 copy-start.18
  51.6 22.2 %all-to-all-start.1 = ((bf16[32,64,128]{2,1,0:T(8,128)(2,1)}), bf16[32,64,128]{2,1,0:T(8,128)(2,1)S(1)}, u32[]{:S(2)}, u32[]{:S(2)}) async-start(bf16[32,64,128]{2,1,0:T(8,128)(2,1)} %shard_map.138), calls=%async_computation.1 | async-start | bytes 1048576 | tf_op jit(solution)/shard_map/all_to_all | solution.py:523
  59.7 9.1 %collective-permute-start.7 = (bf16[32,4096]{1,0:T(8,128)(2,1)}, bf16[32,4096]{1,0:T(8,128)(2,1)}, u32[]{:S(2)}, u32[]{:S(2)}) collective-permute-start(bf16[32,4096]{1,0:T(8,128)(2,1)} %bitcast.15), channel_id=1, source_target_pairs={{0,2},{1,3},{2,0},{3,1},{4,6},{5,7},{6,4},{7,5},{8,10},{9,11},{10,... | collective-permute-start | bytes 786440 | tf_op jit(solution)/shard_map/ppermute | solution.py:455
  66.8 1.4 %copy-start = (bf16[4,2,128,1024]{3,2,1,0:T(8,128)(2,1)}, bf16[4,2,128,1024]{3,2,1,0:T(8,128)(2,1)S(1)}, u32[]{:S(2)}) copy-start(bf16[4,2,128,1024]{3,2,1,0:T(8,128)(2,1)S(1)} %get-tuple-element.81.wide_in) | copy-start | bytes 6291460
  68.1 0.7 copy-start.10
  78.8 0.7 copy-start.9
  79.5 29.7 %copy-start.11 = (f32[2,128,128]{2,1,0:T(8,128)S(1)}, f32[2,128,128]{2,1,0:T(8,128)}, u32[]{:S(2)}) copy-start(f32[2,128,128]{2,1,0:T(8,128)} %copy-done.10) | copy-start | bytes 393220
  79.5 29.7 %copy-start.15 = (s32[3]{0:T(128)S(1)}, s32[3]{0:T(128)}, u32[]{:S(2)}) copy-start(s32[3]{0:T(128)} %copy-done.14) | copy-start | bytes 40
  79.5 17.6 %all-to-all-start.2 = ((bf16[32,32,128]{2,1,0:T(8,128)(2,1)}), bf16[32,32,128]{2,1,0:T(8,128)(2,1)S(1)}, u32[]{:S(2)}, u32[]{:S(2)}) async-start(bf16[32,32,128]{2,1,0:T(8,128)(2,1)} %copy-done.9), calls=%async_computation.2 | async-start | bytes 524288 | tf_op jit(solution)/shard_map/all_to_all | solution.py:542
  87.5 2.4 %collective-permute-start.9 = (bf16[4,16,128]{2,1,0:T(8,128)(2,1)S(1)}, bf16[4,16,128]{2,1,0:T(8,128)(2,1)S(1)}, u32[]{:S(2)}, u32[]{:S(2)}) collective-permute-start(bf16[4,16,128]{2,1,0:T(8,128)(2,1)S(1)} %get-tuple-element.69), channel_id=1, source_target_pairs={{0,4},{4,0},{1,5},{5,1},{2,6},{6,2},{3,7},{7,3},{8,12},{12,8},{9,1... | collective-permute-start | bytes 49160 | tf_op jit(solution)/shard_map/ppermute | solution.py:451
  89.9 16.1 %copy-start.16 = (bf16[32,128]{1,0:T(8,128)(2,1)}, bf16[32,128]{1,0:T(8,128)(2,1)S(1)}, u32[]{:S(2)}) copy-start(bf16[32,128]{1,0:T(8,128)(2,1)S(1)} %get-tuple-element.87.a0) | copy-start | bytes 24580
  89.9 4.3 %collective-permute-start.10 = (bf16[32,128]{1,0:T(8,128)(2,1)S(1)}, bf16[32,128]{1,0:T(8,128)(2,1)S(1)}, u32[]{:S(2)}, u32[]{:S(2)}) collective-permute-start(bf16[32,128]{1,0:T(8,128)(2,1)S(1)} %get-tuple-element.71), channel_id=1, source_target_pairs={{0,1},{1,2},{2,3},{3,0},{4,5},{5,6},{6,7},{7,4},{8,9},{9,10},{10,1... | collective-permute-start | bytes 24584 | tf_op jit(solution)/shard_map/ppermute | solution.py:455
  90.9 4.3 %collective-permute-start.11 = (bf16[32,128]{1,0:T(8,128)(2,1)S(1)}, bf16[32,128]{1,0:T(8,128)(2,1)S(1)}, u32[]{:S(2)}, u32[]{:S(2)}) collective-permute-start(bf16[32,128]{1,0:T(8,128)(2,1)S(1)} %get-tuple-element.72), channel_id=1, source_target_pairs={{0,2},{1,3},{2,0},{3,1},{4,6},{5,7},{6,4},{7,5},{8,10},{9,11},{10,... | collective-permute-start | bytes 24584 | tf_op jit(solution)/shard_map/ppermute | solution.py:455
  93.0 2.8 %collective-permute-start.12 = (bf16[32,128]{1,0:T(8,128)(2,1)S(1)}, bf16[32,128]{1,0:T(8,128)(2,1)S(1)}, u32[]{:S(2)}, u32[]{:S(2)}) collective-permute-start(bf16[32,128]{1,0:T(8,128)(2,1)S(1)} %get-tuple-element.73), channel_id=1, source_target_pairs={{0,3},{1,0},{2,1},{3,2},{4,7},{5,4},{6,5},{7,6},{8,11},{9,8},{10,9... | collective-permute-start | bytes 24584 | tf_op jit(solution)/shard_map/ppermute | solution.py:455
  94.3 11.7 %copy-start.19 = (bf16[32,128]{1,0:T(8,128)(2,1)}, bf16[32,128]{1,0:T(8,128)(2,1)S(1)}, u32[]{:S(2)}) copy-start(bf16[32,128]{1,0:T(8,128)(2,1)S(1)} %collective-permute-done.10.a1) | copy-start | bytes 24580
  95.2 10.8 %copy-start.20 = (bf16[32,128]{1,0:T(8,128)(2,1)}, bf16[32,128]{1,0:T(8,128)(2,1)S(1)}, u32[]{:S(2)}) copy-start(bf16[32,128]{1,0:T(8,128)(2,1)S(1)} %collective-permute-done.11.a2) | copy-start | bytes 24580
  95.8 10.2 %copy-start.21 = (bf16[32,128]{1,0:T(8,128)(2,1)}, bf16[32,128]{1,0:T(8,128)(2,1)S(1)}, u32[]{:S(2)}) copy-start(bf16[32,128]{1,0:T(8,128)(2,1)S(1)} %collective-permute-done.12.a3) | copy-start | bytes 24580
  97.9 17.3 %all-to-all-start.3 = ((bf16[32,16,128]{2,1,0:T(8,128)(2,1)}), bf16[32,16,128]{2,1,0:T(8,128)(2,1)S(1)}, u32[]{:S(2)}, u32[]{:S(2)}) async-start(bf16[32,16,128]{2,1,0:T(8,128)(2,1)} %get-tuple-element.75), calls=%async_computation.3 | async-start | bytes 262144 | tf_op jit(solution)/shard_map/all_to_all | solution.py:550
  109.2 1.6 %copy-start.1 = (bf16[4,2,128,1024]{3,2,1,0:T(8,128)(2,1)S(1)}, bf16[4,2,128,1024]{3,2,1,0:T(8,128)(2,1)}, u32[]{:S(2)}) copy-start(bf16[4,2,128,1024]{3,2,1,0:T(8,128)(2,1)} %copy-done) | copy-start | bytes 6291460
  112.5 0.8 copy-start.17
  115.2 6.1 %collective-permute-start.13 = (bf16[160,1280]{1,0:T(8,128)(2,1)}, bf16[160,1280]{1,0:T(8,128)(2,1)S(1)}, u32[]{:S(2)}, u32[]{:S(2)}) collective-permute-start(bf16[160,1280]{1,0:T(8,128)(2,1)} %copy-done.17), channel_id=1, source_target_pairs={{0,4},{4,0},{1,5},{5,1},{2,6},{6,2},{3,7},{7,3},{8,12},{12,8},{9,1... | collective-permute-start | bytes 1228808 | tf_op jit(solution)/shard_map/ppermute | solution.py:451
  118.4 1.4 %collective-permute-start.14 = (bf16[32,16,128]{2,1,0:T(8,128)(2,1)S(1)}, bf16[32,16,128]{2,1,0:T(8,128)(2,1)S(1)}, u32[]{:S(2)}, u32[]{:S(2)}) collective-permute-start(bf16[32,16,128]{2,1,0:T(8,128)(2,1)S(1)} %all-to-all-done.3.own), channel_id=1, source_target_pairs={{0,4},{4,0},{1,5},{5,1},{2,6},{6,2},{3,7},{7,3},{8,12},{12,8},{9,1... | collective-permute-start | bytes 393224 | tf_op jit(solution)/shard_map/ppermute | solution.py:451

commit v4 on v3

--- a/solution.py
+++ b/solution.py
@@ -94,7 +94,7 @@
             at += width
 
 
-def project_kernel(scal, w, params, l0, l1, l2, l3, own, other):
+def project_kernel(scal, w, params, l3, l2, l1, l0, own, other):
     first = scal[1]
     head = iota((2 * HH, 2 * HH), 0)
     head = jnp.where(first == 0, head, lax.rem(head + HH, 2 * HH))
@@ -110,8 +110,8 @@
 
 def state_kernel(
     scal, po, pp, own, other,
-    msg_out, keep, small,
-    s_all, p_all, decay, msg, sems,
+    msg, keep, small,
+    s_all, p_all, decay,
 ):
     first = scal[1]
     second = 1 - first
@@ -123,22 +123,24 @@
     small[1] = step
     small[2] = cum
     small[3] = rate
-    copies = []
     spread = spreader()
     remain_step = jnp.exp(cum[:, SPAN - 1 :] - cum) * step
     growth = jnp.exp(cum)
-    for b, (x, y, bm, cm) in enumerate((parts_of(own), parts_of(other))):
-        rows = slice(b * HH, (b + 1) * HH)
-        weights = columns(remain_step[rows], growth[rows])
-        b_t = bm[...].astype(F32).T.astype(BF)
-        c_t = cm[...].astype(F32).T.astype(BF)
-        for k in range(W // 256):
-            cols = slice(k * 256, (k + 1) * 256)
-            w_in = spread(weights, 0, k)
-            s_all[b, :, cols] = dot(b_t, (w_in * x[:, cols].astype(F32)).astype(BF))
-            w_out = spread(weights, 1, k)
-            p_all[b, :, cols] = dot(c_t, (w_out * y[:, cols].astype(F32)).astype(BF))
-            decay[b, :, cols] = jnp.broadcast_to(w_out[SPAN - 1 :], (8, 256))
+    weights = [columns(remain_step[i : i + HH], growth[i : i + HH]) for i in (0, HH)]
+    weights = jnp.concatenate(weights, 0)
+    blocks = (parts_of(own), parts_of(other))
+    mats = [[v[...].astype(F32).T.astype(BF) for v in block[2:]] for block in blocks]
+    for k in range(W // 256):
+        cols = slice(k * 256, (k + 1) * 256)
+        w_in, w_out = spread(weights, 0, k), spread(weights, 1, k)
+        for b, (x, y, _, _) in enumerate(blocks):
+            rows = slice(b * SPAN, (b + 1) * SPAN)
+            x_w = (w_in[rows] * x[:, cols].astype(F32)).astype(BF)
+            y_w = (w_out[rows] * y[:, cols].astype(F32)).astype(BF)
+            s_all[b, :, cols] = dot(mats[b][0], x_w)
+            p_all[b, :, cols] = dot(mats[b][1], y_w)
+            last = (b + 1) * SPAN - 1
+            decay[b, :, cols] = jnp.broadcast_to(w_out[last : last + 1], (8, 256))
     per = N // PIECE
     for k in range(W // 128):
         cols = slice(k * 128, (k + 1) * 128)
@@ -153,10 +155,6 @@
             rows = slice(r * PIECE, (r + 1) * PIECE)
             whole = jnp.concatenate([forward[rows], backward[rows]] + d3, 0)
             msg[k * per + r] = whole.astype(BF)
-        if k % 2 == 1:
-            done = pl.ds((k - 1) * per, 2 * per)
-            copies += copy_all([(msg.at[done], msg_out.at[done])], sems, k // 2)
-    wait_all(copies)
 
 
 def fold_kernel(msg, out):
@@ -267,25 +265,28 @@
 
 def pre_kernel(
     scal, got, keep, small, sums_v, own, other, lo_in, lp_in,
-    zed_own, zed_other, msg_out,
-    start, end, exact, decay, rows_v, msg, sems,
+    zed_own, zed_other, msg,
+    start, end, exact, decay, rows_v, sems,
 ):
     late = copy_all(
-        [(v, rows_v.at[pl.ds(SPAN * k, SPAN)]) for k, v in enumerate((lo_in, lp_in))], sems, 4
+        [(v, rows_v.at[pl.ds(SPAN * k, SPAN)]) for k, v in enumerate((lo_in, lp_in))], sems
     )
     block_decays(small, decay)
     assemble(scal, got, keep, decay, start, end, exact)
     by_head = head_map((W, 128), 1, 0)
-    sums = []
     joint = []
-    for b, (x, y, bm, cm) in enumerate((parts_of(own), parts_of(other))):
-        for grad, mat, state in ((x, bm, end), (y, cm, start)):
-            total = jnp.zeros((SPAN, 128), F32)
-            for k in range(W // 256):
-                cols = slice(k * 256, (k + 1) * 256)
+    total = jnp.zeros((4 * SPAN, 128), F32)
+    blocks = (parts_of(own), parts_of(other))
+    for k in range(W // 256):
+        cols = slice(k * 256, (k + 1) * 256)
+        prods = []
+        for b, (x, y, bm, cm) in enumerate(blocks):
+            for grad, mat, state in ((x, bm, end), (y, cm, start)):
                 prod = dot(mat[...], state[b, :, cols]) * grad[:, cols].astype(F32)
-                total = total + dot(prod.astype(BF), by_head[cols])
-            sums.append(total.T[:HH])
+                prods.append(prod.astype(BF))
+        total = total + dot(jnp.concatenate(prods, 0), by_head[cols])
+    sums = [total[i * SPAN : (i + 1) * SPAN].T[:HH] for i in range(4)]
+    for b in range(2):
         rows8 = jnp.concatenate(split3(exact[b, 0:1, :]) + [jnp.zeros((5, W), F32)], 0).astype(BF)
         joint.append(jnp.sum(dot_nt(head_map((HH, W), 0, 1), rows8), axis=1, keepdims=True))
     x_pulled = jnp.concatenate([sums[0], sums[2]], 0)
@@ -309,7 +310,6 @@
         turn = rolled if k == 0 else pltpu.roll(rolled, 128 - 32 * k, 1)
         zed_own[k] = turn[:HH].astype(BF)
         zed_other[k] = turn[HH:].astype(BF)
-    copies = []
     rolled = jnp.concatenate([rolled[:HH], rolled[HH:]], 1).astype(BF)
     diagonal = iota((HH, 128), 0) == iota((HH, 128), 1)
 
@@ -320,21 +320,17 @@
 
     wait_all(late)
     extra = split3(as_row(grad_pre)) + split3(as_row(-grad_log * step))
-    extra = jnp.concatenate(extra + [jnp.zeros((10, 128), F32)], 0).astype(BF)
+    extra = jnp.concatenate(extra + [jnp.zeros((2, 128), F32)], 0)
     for k in range(D // 256):
         cols = slice(k * 256, (k + 1) * 256)
         part = dot(rolled, rows_v[:, cols])
         for j in range(2):
-            msg[2 * k + j, 0:HH, :] = part[:, j * 128 : (j + 1) * 128].astype(BF)
-            msg[2 * k + j, HH : 2 * HH, :] = extra
-        if k % 4 == 3:
-            done = pl.ds(2 * k - 6, 8)
-            copies += copy_all([(msg.at[done], msg_out.at[done])], sems, k // 4)
-    wait_all(copies)
+            whole = jnp.concatenate([part[:, j * 128 : (j + 1) * 128], extra], 0)
+            msg[2 * k + j] = whole.astype(BF)
 
 
 def sum_kernel(msg, out, totals):
-    total = jnp.zeros((2 * HH, 128), F32)
+    total = jnp.zeros((HH + 8, 128), F32)
     for k in range(CHIPS):
         total = total + msg[k].astype(F32)
     rounded = total[:HH].astype(BF)
@@ -347,7 +343,7 @@
 
 
 def grads_kernel(
-    scal, got, keep, small, wide_in, gb, gc, own, other, totals,
+    scal, got, keep, small, wide_in, gb, gc, own, other,
     out_own, out_other,
     start, end, decay, wide, sems,
 ):
@@ -362,44 +358,36 @@
         for k in range(W // 256):
             cols = slice(k * 256, (k + 1) * 256)
             pulled = dot(bm[...], end[b, :, cols])
-            out[:SPAN, cols] = (
+            out[:, cols] = (
                 gs[b, :, cols].astype(F32) + remain[b, :, cols].astype(F32) * pulled
             ).astype(BF)
             grad_b = grad_b + dot_nt(in_w[b, :, cols], end[b, :, cols])
             grad_c = grad_c + dot_nt(out_w[b, :, cols], start[b, :, cols])
-        out[:SPAN, W : W + N] = grad_b.astype(BF)
-        out[:SPAN, W + N :] = grad_c.astype(BF)
-        spare = jnp.concatenate(split3(totals[...]) + [jnp.zeros((8, 128), F32)], 0)
-        out[SPAN:, :128] = spare.astype(BF)
-
-
-def weight_kernel(scal, own, other, out):
-    at_zero = scal[1] == 0
-    for j in range(CHIPS):
-        a, b = own[j].astype(F32), other[j].astype(F32)
-        cols = slice(j * 128, (j + 1) * 128)
-        out[0:HH, cols] = jnp.where(at_zero, a, b)
-        out[HH : 2 * HH, cols] = jnp.where(at_zero, b, a)
-
-
-def join_kernel(scal, own, other, params, gx, gb, gc, g_bias, g_rate):
-    at_zero = scal[1] == 0
+        out[:, W : W + N] = grad_b.astype(BF)
+        out[:, W + N :] = grad_c.astype(BF)
+
+
+def final_kernel(
+    own, other, params, t_own, t_other, w_own, w_other, gx, gb, gc, g_bias, g_rate, g_weight
+):
+    at_zero = lax.axis_index("core") == 0
 
     def join(a, b):
         return jnp.where(at_zero, a, b), jnp.where(at_zero, b, a)
 
     for out, at, width in ((gx, 0, W), (gb, W, N), (gc, W + N, N)):
         cols = slice(at, at + width)
-        out[:, :width], out[:, width:] = join(own[:SPAN, cols], other[:SPAN, cols])
-    sums = []
-    for v in (own, other):
-        v = v[SPAN:, :128].astype(F32)
-        sums.append(v[:8] + v[8:16] + v[16:24])
-    low, high = join(*sums)
+        out[:, :width], out[:, width:] = join(own[:, cols], other[:, cols])
+    low, high = join(t_own[...], t_other[...])
     lane = iota((8, 128), 1)
     total = jnp.where(lane < HH, low, pltpu.roll(high, HH, 1))
     g_bias[...] = total[0:1, : 2 * HH]
     g_rate[...] = total[1:2, : 2 * HH] * jnp.exp(params[1:2])
+    for j in range(CHIPS):
+        cols = slice(j * 128, (j + 1) * 128)
+        g_weight[0:HH, cols], g_weight[HH:, cols] = join(
+            w_own[j].astype(F32), w_other[j].astype(F32)
+        )
 
 
 def turn_kernel(own, other, *outs):
@@ -481,7 +469,7 @@
     proj_own, proj_other = call(
         project_kernel,
         [((2, HH, 128), F32), ((HH, 128), F32)],
-        [scal, weight_mine, params] + pieces,
+        [scal, weight_mine, params] + pieces[::-1],
         limit=16,
         flops=2**26,
         moved=2**21,
@@ -492,9 +480,7 @@
         state_kernel,
         [msg_t, keep_t, small_t],
         [scal, proj_own, proj_other] + operands,
-        [((2, N, W), F32), ((2, N, W), F32), ((2, 8, W), F32), msg_t],
-        sems=4,
-        far_out=(0,),
+        [((2, N, W), F32), ((2, N, W), F32), ((2, 8, W), F32)],
         limit=STATE_LIMIT,
         flops=2**28,
         moved=2**22,
@@ -524,32 +510,42 @@
     states, far = lax.optimization_barrier((states, far))
     weights = [weight_t, near[0], far, near[1]]
 
-    parts_t = ((CHIPS, 2 * HH, 128), BF)
+    parts_t = ((CHIPS, HH + 8, 128), BF)
     state_scratch = [((2, N, W), BF), ((2, N, W), BF)]
     zed_own, zed_other, parts = call(
         pre_kernel,
         [((TP, HH, 128), BF)] * 2 + [parts_t],
         [scal, states, keep, small, sums] + operands + [rows_own, rows_other],
         state_scratch
-        + [((2, 8, W), F32), ((2, 8, W), F32), ((2 * SPAN, D), BF), parts_t],
-        sems=6,
+        + [((2, 8, W), F32), ((2, 8, W), F32), ((2 * SPAN, D), BF)],
+        sems=2,
         far_in=(7, 8),
-        far_out=(2,),
         flops=2**29,
         moved=2**23,
         limit=PRE_LIMIT,
     )
     shares = lax.all_to_all(parts, "chip", 0, 0, tiled=True)
 
+    out_t = ((SPAN, W + 2 * N), BF)
+    out_own, out_other = call(
+        grads_kernel,
+        [out_t] * 2,
+        [scal, states, keep, small, wide, gb, gc] + operands,
+        state_scratch + [((2, 8, W), F32), wide_t],
+        sems=1,
+        far_in=(4,),
+        limit=GRADS_LIMIT,
+    )
+    out_other = swap(out_other)
     zed = call(turn_kernel, [((2 * HH, 128), BF)] * TP, [zed_own, swap(zed_other)])
-    zed = [zed[0]] + [round_tp(zed[k], k) for k in (1, 2, 3)]
-    shares, zed = lax.optimization_barrier((shares, zed))
+    shares, zed, out_own, out_other = lax.optimization_barrier((shares, zed, out_own, out_other))
     total, totals = call(
         sum_kernel, [((CHIPS, HH, 128), BF), ((8, 128), F32)], [shares], flops=2**20, moved=2**20, limit=16
     )
     weight_own = lax.all_to_all(total, "chip", 0, 0, tiled=True)
 
-    wide, zed, total = lax.optimization_barrier((wide, zed, total))
+    zed, total = lax.optimization_barrier((zed, total))
+    zed = [zed[0]] + [round_tp(zed[k], k) for k in (1, 2, 3)]
     (grad_layer_input,) = call(
         input_kernel,
         [((32, D), BF)],
@@ -560,32 +556,15 @@
         limit=INPUT_LIMIT,
     )
 
-    out_t = ((SPAN + 32, W + 2 * N), BF)
-    out_own, out_other = call(
-        grads_kernel,
-        [out_t] * 2,
-        [scal, states, keep, small, wide, gb, gc] + operands + [totals],
-        state_scratch + [((2, 8, W), F32), wide_t],
-        sems=1,
-        far_in=(4,),
-        limit=GRADS_LIMIT,
-    )
-    weight_own, out_own, out_other, grad_layer_input = lax.optimization_barrier(
-        (weight_own, out_own, out_other, grad_layer_input)
-    )
-    joined = call(
-        join_kernel,
-        [((SPAN, 2 * W), BF), ((SPAN, 2 * N), BF), ((SPAN, 2 * N), BF)] + [((1, 2 * HH), F32)] * 2,
-        [scal, out_own, swap(out_other), params],
-    )
-    grad_ssm_input, grad_b_in, grad_c_in, grad_dt_bias, grad_a_log = joined
-
-    (grad_dt_weight,) = call(
-        weight_kernel,
-        [((2 * HH, D), F32)],
-        [scal, weight_own, swap(weight_own)],
-        flops=2**20,
-        moved=2**22,
+    weight_own, grad_layer_input, totals_other = lax.optimization_barrier(
+        (weight_own, grad_layer_input, swap(totals))
+    )
+    grad_ssm_input, grad_b_in, grad_c_in, grad_dt_bias, grad_a_log, grad_dt_weight = call(
+        final_kernel,
+        [((SPAN, 2 * W), BF), ((SPAN, 2 * N), BF), ((SPAN, 2 * N), BF)]
+        + [((1, 2 * HH), F32)] * 2
+        + [((2 * HH, D), F32)],
+        [out_own, out_other, params, totals, totals_other, weight_own, swap(weight_own)],
     )
     return (
         grad_ssm_input,

time: 124 us -> 118 us (0.952)
  Pallas kernels: 24.1 us -> 20.5 us
  waiting for transfers between devices: 24.4 us -> 21 us
    pallas_call x12 -> x11, Pallas kernels: 24.1 us -> 20.5 us  [call(): pl.pallas_call(kernel, out_shape=[jax.ShapeDtypeStruct(s, t) for s, t in...]
    ppermute x6, waiting for transfers between devices: 7.26 us -> 3.75 us  [round_tp(): return lax.ppermute(v, 'tp', [(i, (i + k) % TP) for i in range(TP)])]
    all_to_all x1, waiting for transfers between devices: 1.95 us -> 0.01 us  [local(): weight_own = lax.all_to_all(total, 'chip', 0, 0, tiled=True)]
    unnamed x51 -> x45, local copies, waits for them, and re-layouts: 12.3 us -> 13.5 us
    ppermute x6 -> x7, starting transfers between devices: 8.94 us -> 9.23 us  [swap(): return lax.ppermute(v, 'core', [(0, 1), (1, 0)])]
    ppermute x6 -> x7, waiting for transfers between devices: 3.08 us -> 2.98 us  [swap(): return lax.ppermute(v, 'core', [(0, 1), (1, 0)])]
  transfers between devices with their start and end apart: 19 -> 20, of which waited for: 12 -> 8; matrix products, arithmetic and copies ran while one was open for 3% -> 3% of each run, Pallas kernels for 12% -> 10%
where the time goes in v4:
time: 118 us
  starting transfers between devices  59.5 us (50%)
  waiting for transfers between devices  21 us (18%)
  Pallas kernels  20.5 us (17%)
  local copies, waits for them, and re-layouts  15.5 us (13%)
    pallas_call x11, Pallas kernels, call(): pl.pallas_call(kernel, out_shape=[jax.ShapeDtypeStruct(s, t) for s, t in...  20.5 us
    unnamed x45, local copies, waits for them, and re-layouts  13.5 us
    all_to_all x1, starting transfers between devices, local(): got = lax.all_to_all(msg, 'chip', 0, 0, tiled=True)  11 us
    ppermute x6, starting transfers between devices, round_tp(): return lax.ppermute(v, 'tp', [(i, (i + k) % TP) for i in range(TP)])  9.71 us
    ppermute x7, starting transfers between devices, swap(): return lax.ppermute(v, 'core', [(0, 1), (1, 0)])  9.23 us
    all_to_all x1, starting transfers between devices, local(): states = lax.all_to_all(folded, 'chip', 0, 0, tiled=True)  8.06 us
    all_to_all x1, starting transfers between devices, local(): shares = lax.all_to_all(parts, 'chip', 0, 0, tiled=True)  7.86 us
    all_to_all x1, starting transfers between devices, local(): weight_own = lax.all_to_all(total, 'chip', 0, 0, tiled=True)  7.73 us
  transfers between devices with their start and end apart: 20, of which 8 were waited for; matrix products, arithmetic and copies ran while one was open for 3% of the time, Pallas kernels for 10%

profile of v4, /device:TPU:1, one launch (start us, length us, event | category | flops | bytes accessed | tf_op | source)
XLA Modules:
  0.0 117.5 jit_solution(11469448250877564307)
XLA Ops:
  0.6 2.2 %collective-permute-start = (bf16[32,4096]{1,0:T(8,128)(2,1)}, bf16[32,4096]{1,0:T(8,128)(2,1)S(1)}, u32[]{:S(2)}, u32[]{:S(2)}) collective-permute-start(bf16[32,4096]{1,0:T(8,128)(2,1)} %l0.1), channel_id=1, source_target_pairs={{3,0},{0,1},{1,2},{2,3},{7,4},{4,5},{5,6},{6,7},{11,8},{8,9},{9,10... | collective-permute-start | bytes 786440 | tf_op jit(solution)/shard_map/ppermute | solution.py:455
  2.8 2.6 %collective-permute-start.1 = (bf16[32,4096]{1,0:T(8,128)(2,1)}, bf16[32,4096]{1,0:T(8,128)(2,1)S(1)}, u32[]{:S(2)}, u32[]{:S(2)}) collective-permute-start(bf16[32,4096]{1,0:T(8,128)(2,1)} %l0.1), channel_id=1, source_target_pairs={{2,0},{3,1},{0,2},{1,3},{6,4},{7,5},{4,6},{5,7},{10,8},{11,9},{8,1... | collective-permute-start | bytes 786440 | tf_op jit(solution)/shard_map/ppermute | solution.py:455
  5.5 1.1 collective-permute-start.2
  6.5 0.1 pad_add_fusion.scal
  6.6 1.0 copy-done.7
  7.7 1.0 copy-done.8
  8.7 0.8 copy-done.11
  9.5 0.8 copy-done.12
  10.4 0.6 shard_map.136
  11.0 1.6 %collective-permute-start.4 = (bf16[128,2304]{1,0:T(8,128)(2,1)S(1)}, bf16[128,2304]{1,0:T(8,128)(2,1)S(1)}, u32[]{:S(2)}, u32[]{:S(2)}) collective-permute-start(bf16[128,2304]{1,0:T(8,128)(2,1)S(1)} %get-tuple-element.59), channel_id=1, source_target_pairs={{0,4},{4,0},{1,5},{5,1},{2,6},{6,2},{3,7},{7,3},{8,12},{12,8},{9,1... | collective-permute-start | bytes 1769480 | tf_op jit(solution)/shard_map/ppermute | solution.py:439
  12.6 1.0 dynamic-slice_bitcast_fusion.1
  13.7 0.0 collective-permute-done.l3
  13.7 0.0 copy-start.3
  13.7 3.3 %collective-permute-done.1.l2 = bf16[32,4096]{1,0:T(8,128)(2,1)S(1)} collective-permute-done((bf16[32,4096]{1,0:T(8,128)(2,1)}, bf16[32,4096]{1,0:T(8,128)(2,1)S(1)}, u32[]{:S(2)}, u32[]{:S(2)}) %collective-permute-start.1) | collective-permute-done | bytes 262176 | tf_op jit(solution)/shard_map/ppermute | solution.py:455
  17.0 0.0 copy-start.5
  17.0 1.0 shard_map.135
  18.1 0.0 copy-done.5
  18.1 1.6 %collective-permute-start.3 = (f32[16,128]{1,0:T(8,128)S(1)}, f32[16,128]{1,0:T(8,128)S(1)}, u32[]{:S(2)}, u32[]{:S(2)}) collective-permute-start(f32[16,128]{1,0:T(8,128)S(1)} %get-tuple-element.57), channel_id=1, source_target_pairs={{0,4},{4,0},{1,5},{5,1},{2,6},{6,2},{3,7},{7,3},{8,12},{12,8},{9,1... | collective-permute-start | bytes 24584 | tf_op jit(solution)/shard_map/ppermute | solution.py:439
  19.8 0.8 collective-permute-done.3.pp
  20.6 0.0 collective-permute-done.4.other
  20.6 2.2 %shard_map.137 = (bf16[32,72,128]{2,1,0:T(8,128)(2,1)S(1)}, bf16[2,128,1024]{2,1,0:T(8,128)(2,1)S(1)}, f32[4,32,128]{2,1,0:T(8,128)S(1)}) custom-call(s32[3]{0:T(128)S(1)} %pad_add_fusion.scal, f32[2,16,128]{2,1,0:T(8,128)S(1)} %get-tuple-element.56.po, f32[16,128]{1,0:T(8,128)S(1)} %collective-permute-done.3.pp, ...), custom_call_target="tpu_custom_call" | custom-call | flops 268435456 | bytes 4194304 | tf_op jit(solution)/shard_map/pallas_call | solution.py:427
  22.8 0.8 copy-done.6
  23.6 11.0 %all-to-all-start = ((bf16[32,72,128]{2,1,0:T(8,128)(2,1)}), bf16[32,72,128]{2,1,0:T(8,128)(2,1)S(1)}, u32[]{:S(2)}, u32[]{:S(2)}) async-start(bf16[32,72,128]{2,1,0:T(8,128)(2,1)} %copy-done.6), calls=%async_computation | async-start | bytes 1179648 | tf_op jit(solution)/shard_map/all_to_all | solution.py:488
  34.6 1.0 constant_dynamic-update-slice_fusion.2
  35.6 1.0 constant_dynamic-update-slice_fusion.1
  36.6 1.0 collective-permute-start.5
  37.6 1.7 %collective-permute-start.6 = (bf16[32,4096]{1,0:T(8,128)(2,1)}, bf16[32,4096]{1,0:T(8,128)(2,1)}, u32[]{:S(2)}, u32[]{:S(2)}) collective-permute-start(bf16[32,4096]{1,0:T(8,128)(2,1)} %bitcast.14), channel_id=1, source_target_pairs={{0,3},{1,0},{2,1},{3,2},{4,7},{5,4},{6,5},{7,6},{8,11},{9,8},{10,9... | collective-permute-start | bytes 786440 | tf_op jit(solution)/shard_map/ppermute | solution.py:443
  39.3 1.0 constant_dynamic-update-slice_fusion.lo_in
  40.3 1.3 %collective-permute-start.8 = (bf16[128,4096]{1,0:T(8,128)(2,1)S(1)}, bf16[128,4096]{1,0:T(8,128)(2,1)}, u32[]{:S(2)}, u32[]{:S(2)}) collective-permute-start(bf16[128,4096]{1,0:T(8,128)(2,1)S(1)} %constant_dynamic-update-slice_fusion.lo_in), channel_id=1, source_target_pairs={{0,4},{4,0},{1,5},{5,1},{2,6},{6,2},{3,7},{7,3},{8,12},{12,8},{9,1... | collective-permute-start | bytes 3145736 | tf_op jit(solution)/shard_map/ppermute | solution.py:439
  41.6 3.7 %collective-permute-done.5.w1 = bf16[32,4096]{1,0:T(8,128)(2,1)S(1)} collective-permute-done((bf16[32,4096]{1,0:T(8,128)(2,1)}, bf16[32,4096]{1,0:T(8,128)(2,1)S(1)}, u32[]{:S(2)}, u32[]{:S(2)}) %collective-permute-start.5) | collective-permute-done | bytes 262176 | tf_op jit(solution)/shard_map/ppermute | solution.py:443
  45.3 0.7 copy-done.15
  46.0 4.2 %all-to-all-done.msg = bf16[32,72,128]{2,1,0:T(8,128)(2,1)S(1)} async-done(((bf16[32,72,128]{2,1,0:T(8,128)(2,1)}), bf16[32,72,128]{2,1,0:T(8,128)(2,1)S(1)}, u32[]{:S(2)}, u32[]{:S(2)}) %all-to-all-start) | async-done | bytes 589856 | tf_op jit(solution)/shard_map/all_to_all | solution.py:488
  50.2 0.9 shard_map.138
  51.1 8.1 %all-to-all-start.1 = ((bf16[32,64,128]{2,1,0:T(8,128)(2,1)}), bf16[32,64,128]{2,1,0:T(8,128)(2,1)S(1)}, u32[]{:S(2)}, u32[]{:S(2)}) async-start(bf16[32,64,128]{2,1,0:T(8,128)(2,1)} %shard_map.138), calls=%async_computation.1 | async-start | bytes 1048576 | tf_op jit(solution)/shard_map/all_to_all | solution.py:509
  59.2 2.5 %collective-permute-start.7 = (bf16[32,4096]{1,0:T(8,128)(2,1)}, bf16[32,4096]{1,0:T(8,128)(2,1)}, u32[]{:S(2)}, u32[]{:S(2)}) collective-permute-start(bf16[32,4096]{1,0:T(8,128)(2,1)} %bitcast.15), channel_id=1, source_target_pairs={{0,2},{1,3},{2,0},{3,1},{4,6},{5,7},{6,4},{7,5},{8,10},{9,11},{10,... | collective-permute-start | bytes 786440 | tf_op jit(solution)/shard_map/ppermute | solution.py:443
  61.7 4.6 %shard_map.139 = (bf16[4,2,128,1024]{3,2,1,0:T(8,128)(2,1)S(1)}, f32[2,128,128]{2,1,0:T(8,128)S(1)}, f32[2,128,128]{2,1,0:T(8,128)S(1)}, f32[2,32,128]{2,1,0:T(8,128)S(1)}) custom-call(f32[4,32,128]{2,1,0:T(8,128)S(1)} %get-tuple-element.66.small, bf16[128,2304]{1,0:T(8,128)(2,1)S(1)} %get-tuple-element.58.own, ...), custom_call_target="tpu_custom_call" | custom-call | tf_op jit(solution)/shard_map/pallas_call | solution.py:427
  66.3 1.3 %copy-done = bf16[4,2,128,1024]{3,2,1,0:T(8,128)(2,1)} copy-done((bf16[4,2,128,1024]{3,2,1,0:T(8,128)(2,1)}, bf16[4,2,128,1024]{3,2,1,0:T(8,128)(2,1)S(1)}, u32[]{:S(2)}) %copy-start) | copy-done | bytes 2097176
  67.7 0.7 copy-done.9
  68.3 0.0 collective-permute-done.7.w2
  68.3 5.0 %all-to-all-done.1.got = bf16[32,64,128]{2,1,0:T(8,128)(2,1)S(1)} async-done(((bf16[32,64,128]{2,1,0:T(8,128)(2,1)}), bf16[32,64,128]{2,1,0:T(8,128)(2,1)S(1)}, u32[]{:S(2)}, u32[]{:S(2)}) %all-to-all-start.1) | async-done | bytes 524320 | tf_op jit(solution)/shard_map/all_to_all | solution.py:509
  73.3 4.6 %shard_map.140 = (bf16[4,16,128]{2,1,0:T(8,128)(2,1)S(1)}, bf16[4,16,128]{2,1,0:T(8,128)(2,1)S(1)}, bf16[32,24,128]{2,1,0:T(8,128)(2,1)}) custom-call(s32[3]{0:T(128)S(1)} %pad_add_fusion.scal, bf16[32,64,128]{2,1,0:T(8,128)(2,1)S(1)} %all-to-all-done.1.got, bf16[2,128,1024]{2,1,0:T(8,128)(2,1)S(1)} %get-tuple-element.65.keep, ...), custom_call_target="tpu_custom_call" | custom-call | flops 536870912 | bytes 8388608 | tf_op jit(solution)/shard_map/pallas_call | solution.py:427
  77.9 7.9 %all-to-all-start.2 = ((bf16[32,24,128]{2,1,0:T(8,128)(2,1)}), bf16[32,24,128]{2,1,0:T(8,128)(2,1)S(1)}, u32[]{:S(2)}, u32[]{:S(2)}) async-start(bf16[32,24,128]{2,1,0:T(8,128)(2,1)} %get-tuple-element.68), calls=%async_computation.2 | async-start | bytes 393216 | tf_op jit(solution)/shard_map/all_to_all | solution.py:527
  85.8 1.6 %copy-done.1 = bf16[4,2,128,1024]{3,2,1,0:T(8,128)(2,1)S(1)} copy-done((bf16[4,2,128,1024]{3,2,1,0:T(8,128)(2,1)S(1)}, bf16[4,2,128,1024]{3,2,1,0:T(8,128)(2,1)}, u32[]{:S(2)}) %copy-start.1) | copy-done | bytes 2097176
  87.4 0.9 copy-done.10
  88.3 1.6 %shard_map.142 = (bf16[128,1280]{1,0:T(8,128)(2,1)S(1)}, bf16[128,1280]{1,0:T(8,128)(2,1)S(1)}) custom-call(s32[3]{0:T(128)S(1)} %pad_add_fusion.scal, bf16[32,64,128]{2,1,0:T(8,128)(2,1)S(1)} %all-to-all-done.1.got, bf16[2,128,1024]{2,1,0:T(8,128)(2,1)S(1)} %get-tuple-element.65.keep, f32[4,32,128]{2,1,0:T(8,128)S(1)} %get-tuple-element.66.small, ...), custom_call_target="tpu_custom_call" | custom-call | tf_op jit(solution)/shard_map/pallas_call | solution.py:427
  89.9 1.6 %collective-permute-start.10 = (bf16[128,1280]{1,0:T(8,128)(2,1)S(1)}, bf16[128,1280]{1,0:T(8,128)(2,1)S(1)}, u32[]{:S(2)}, u32[]{:S(2)}) collective-permute-start(bf16[128,1280]{1,0:T(8,128)(2,1)S(1)} %get-tuple-element.79), channel_id=1, source_target_pairs={{0,4},{4,0},{1,5},{5,1},{2,6},{6,2},{3,7},{7,3},{8,12},{12,8},{9,1... | collective-permute-start | bytes 983048 | tf_op jit(solution)/shard_map/ppermute | solution.py:439
  91.5 0.1 collective-permute-start.9
  91.6 1.2 %collective-permute-done.9.other = bf16[4,16,128]{2,1,0:T(8,128)(2,1)S(1)} collective-permute-done((bf16[4,16,128]{2,1,0:T(8,128)(2,1)S(1)}, bf16[4,16,128]{2,1,0:T(8,128)(2,1)S(1)}, u32[]{:S(2)}, u32[]{:S(2)}) %collective-permute-start.9) | collective-permute-done | bytes 16416 | tf_op jit(solution)/shard_map/ppermute | solution.py:439
  92.8 0.6 copy-done.14
  93.4 1.8 %all-to-all-done.2.msg = bf16[32,24,128]{2,1,0:T(8,128)(2,1)S(1)} async-done(((bf16[32,24,128]{2,1,0:T(8,128)(2,1)}), bf16[32,24,128]{2,1,0:T(8,128)(2,1)S(1)}, u32[]{:S(2)}, u32[]{:S(2)}) %all-to-all-start.2) | async-done | bytes 196640 | tf_op jit(solution)/shard_map/all_to_all | solution.py:527
  95.2 0.7 shard_map.143
  95.9 7.7 %all-to-all-start.3 = ((bf16[32,16,128]{2,1,0:T(8,128)(2,1)}), bf16[32,16,128]{2,1,0:T(8,128)(2,1)S(1)}, u32[]{:S(2)}, u32[]{:S(2)}) async-start(bf16[32,16,128]{2,1,0:T(8,128)(2,1)} %get-tuple-element.84), calls=%async_computation.3 | async-start | bytes 262144 | tf_op jit(solution)/shard_map/all_to_all | solution.py:545
  103.6 1.0 collective-permute-start.11
  104.6 2.1 %collective-permute-start.12 = (bf16[32,128]{1,0:T(8,128)(2,1)S(1)}, bf16[32,128]{1,0:T(8,128)(2,1)S(1)}, u32[]{:S(2)}, u32[]{:S(2)}) collective-permute-start(bf16[32,128]{1,0:T(8,128)(2,1)S(1)} %get-tuple-element.91), channel_id=1, source_target_pairs={{0,2},{1,3},{2,0},{3,1},{4,6},{5,7},{6,4},{7,5},{8,10},{9,11},{10,... | collective-permute-start | bytes 24584 | tf_op jit(solution)/shard_map/ppermute | solution.py:443
  106.8 1.3 %collective-permute-start.13 = (bf16[32,128]{1,0:T(8,128)(2,1)S(1)}, bf16[32,128]{1,0:T(8,128)(2,1)S(1)}, u32[]{:S(2)}, u32[]{:S(2)}) collective-permute-start(bf16[32,128]{1,0:T(8,128)(2,1)S(1)} %get-tuple-element.92), channel_id=1, source_target_pairs={{0,3},{1,0},{2,1},{3,2},{4,7},{5,4},{6,5},{7,6},{8,11},{9,8},{10,9... | collective-permute-start | bytes 24584 | tf_op jit(solution)/shard_map/ppermute | solution.py:443
  108.0 1.5 %collective-permute-start.14 = (f32[8,128]{1,0:T(8,128)S(1)}, f32[8,128]{1,0:T(8,128)S(1)}, u32[]{:S(2)}, u32[]{:S(2)}) collective-permute-start(f32[8,128]{1,0:T(8,128)S(1)} %get-tuple-element.83.t_own), channel_id=1, source_target_pairs={{0,4},{4,0},{1,5},{5,1},{2,6},{6,2},{3,7},{7,3},{8,12},{12,8},{9,1... | collective-permute-start | bytes 12296 | tf_op jit(solution)/shard_map/ppermute | solution.py:439
  109.5 0.0 collective-permute-done.11.a1
  109.5 0.0 collective-permute-done.12.a2
  109.6 0.6 copy-done.16
  110.1 0.6 copy-done.18
  110.7 3.1 %shard_map.144 = bf16[32,4096]{1,0:T(8,128)(2,1)} custom-call(s32[3]{0:T(128)} %copy-done.13, bf16[32,128]{1,0:T(8,128)(2,1)} %copy-done.14, bf16[32,128]{1,0:T(8,128)(2,1)} %copy-done.16, bf16[32,128]{1,0:T(8,128)(2,1)} %copy-done.17, bf16[32,128]{1,0:T(8,128)(2,1)} %copy-done.18, bf16[32,4096]{1,0:T(8,128)(2,1)} %bitcast.16, bf16[32,4096]{1,0:T(8,128)(2,1)} %copy-done.15, ...), custom_call_target="tpu_custom_call" | custom-call | tf_op jit(solution)/shard_map/pallas_call | solution.py:427
  113.9 1.6 %collective-permute-start.15 = (bf16[32,16,128]{2,1,0:T(8,128)(2,1)S(1)}, bf16[32,16,128]{2,1,0:T(8,128)(2,1)S(1)}, u32[]{:S(2)}, u32[]{:S(2)}) collective-permute-start(bf16[32,16,128]{2,1,0:T(8,128)(2,1)S(1)} %all-to-all-done.3.w_own), channel_id=1, source_target_pairs={{0,4},{4,0},{1,5},{5,1},{2,6},{6,2},{3,7},{7,3},{8,12},{12,8},{9,1... | collective-permute-start | bytes 393224 | tf_op jit(solution)/shard_map/ppermute | solution.py:439
  115.5 1.0 collective-permute-done.15.w_other
  116.4 1.1 shard_map.145
  (37 shorter events, 0.1 us)
Async XLA Ops:
  0.6 16.4 %copy-start.2 = (bf16[32,4096]{1,0:T(8,128)(2,1)S(1)}, bf16[32,4096]{1,0:T(8,128)(2,1)}, u32[]{:S(2)}) copy-start(bf16[32,4096]{1,0:T(8,128)(2,1)} %l0.1) | copy-start | bytes 786436
  0.6 13.0 %collective-permute-start = (bf16[32,4096]{1,0:T(8,128)(2,1)}, bf16[32,4096]{1,0:T(8,128)(2,1)S(1)}, u32[]{:S(2)}, u32[]{:S(2)}) collective-permute-start(bf16[32,4096]{1,0:T(8,128)(2,1)} %l0.1), channel_id=1, source_target_pairs={{3,0},{0,1},{1,2},{2,3},{7,4},{4,5},{5,6},{6,7},{11,8},{8,9},{9,10... | collective-permute-start | bytes 786440 | tf_op jit(solution)/shard_map/ppermute | solution.py:455
  2.8 14.2 %collective-permute-start.1 = (bf16[32,4096]{1,0:T(8,128)(2,1)}, bf16[32,4096]{1,0:T(8,128)(2,1)S(1)}, u32[]{:S(2)}, u32[]{:S(2)}) collective-permute-start(bf16[32,4096]{1,0:T(8,128)(2,1)} %l0.1), channel_id=1, source_target_pairs={{2,0},{3,1},{0,2},{1,3},{6,4},{7,5},{4,6},{5,7},{10,8},{11,9},{8,1... | collective-permute-start | bytes 786440 | tf_op jit(solution)/shard_map/ppermute | solution.py:455
  5.5 11.5 %collective-permute-start.2 = (bf16[32,4096]{1,0:T(8,128)(2,1)}, bf16[32,4096]{1,0:T(8,128)(2,1)S(1)}, u32[]{:S(2)}, u32[]{:S(2)}) collective-permute-start(bf16[32,4096]{1,0:T(8,128)(2,1)} %l0.1), channel_id=1, source_target_pairs={{1,0},{2,1},{3,2},{0,3},{5,4},{6,5},{7,6},{4,7},{9,8},{10,9},{11,1... | collective-permute-start | bytes 786440 | tf_op jit(solution)/shard_map/ppermute | solution.py:455
  6.6 1.0 copy-start.7
  7.7 1.0 copy-start.8
  8.7 0.8 copy-start.11
  9.5 0.8 copy-start.12
  10.4 75.4 %copy-start.13 = (s32[3]{0:T(128)}, s32[3]{0:T(128)S(1)}, u32[]{:S(2)}) copy-start(s32[3]{0:T(128)S(1)} %pad_add_fusion.scal) | copy-start | bytes 40
  10.4 3.3 %copy-start.19 = (f32[32]{0:T(128)S(1)}, f32[32]{0:T(128)}, u32[]{:S(2)}) copy-start(f32[32]{0:T(128)} %param.11) | copy-start | bytes 388
  10.4 3.3 %copy-start.20 = (f32[32]{0:T(128)S(1)}, f32[32]{0:T(128)}, u32[]{:S(2)}) copy-start(f32[32]{0:T(128)} %param.10) | copy-start | bytes 388
  11.0 9.5 %collective-permute-start.4 = (bf16[128,2304]{1,0:T(8,128)(2,1)S(1)}, bf16[128,2304]{1,0:T(8,128)(2,1)S(1)}, u32[]{:S(2)}, u32[]{:S(2)}) collective-permute-start(bf16[128,2304]{1,0:T(8,128)(2,1)S(1)} %get-tuple-element.59), channel_id=1, source_target_pairs={{0,4},{4,0},{1,5},{5,1},{2,6},{6,2},{3,7},{7,3},{8,12},{12,8},{9,1... | collective-permute-start | bytes 1769480 | tf_op jit(solution)/shard_map/ppermute | solution.py:439
  13.7 6.9 %copy-start.3 = (bf16[32,4096]{1,0:T(8,128)(2,1)}, bf16[32,4096]{1,0:T(8,128)(2,1)S(1)}, u32[]{:S(2)}) copy-start(bf16[32,4096]{1,0:T(8,128)(2,1)S(1)} %collective-permute-done.l3) | copy-start | bytes 786436
  17.0 1.1 copy-start.4
  17.0 1.1 copy-start.5
  18.1 2.5 %collective-permute-start.3 = (f32[16,128]{1,0:T(8,128)S(1)}, f32[16,128]{1,0:T(8,128)S(1)}, u32[]{:S(2)}, u32[]{:S(2)}) collective-permute-start(f32[16,128]{1,0:T(8,128)S(1)} %get-tuple-element.57), channel_id=1, source_target_pairs={{0,4},{4,0},{1,5},{5,1},{2,6},{6,2},{3,7},{7,3},{8,12},{12,8},{9,1... | collective-permute-start | bytes 24584 | tf_op jit(solution)/shard_map/ppermute | solution.py:439
  22.8 0.8 copy-start.6
  23.6 26.6 %all-to-all-start = ((bf16[32,72,128]{2,1,0:T(8,128)(2,1)}), bf16[32,72,128]{2,1,0:T(8,128)(2,1)S(1)}, u32[]{:S(2)}, u32[]{:S(2)}) async-start(bf16[32,72,128]{2,1,0:T(8,128)(2,1)} %copy-done.6), calls=%async_computation | async-start | bytes 1179648 | tf_op jit(solution)/shard_map/all_to_all | solution.py:488
  36.6 8.7 %collective-permute-start.5 = (bf16[32,4096]{1,0:T(8,128)(2,1)}, bf16[32,4096]{1,0:T(8,128)(2,1)S(1)}, u32[]{:S(2)}, u32[]{:S(2)}) collective-permute-start(bf16[32,4096]{1,0:T(8,128)(2,1)} %bitcast.13), channel_id=1, source_target_pairs={{0,1},{1,2},{2,3},{3,0},{4,5},{5,6},{6,7},{7,4},{8,9},{9,10},{10,1... | collective-permute-start | bytes 786440 | tf_op jit(solution)/shard_map/ppermute | solution.py:443
  37.6 8.4 %collective-permute-start.6 = (bf16[32,4096]{1,0:T(8,128)(2,1)}, bf16[32,4096]{1,0:T(8,128)(2,1)}, u32[]{:S(2)}, u32[]{:S(2)}) collective-permute-start(bf16[32,4096]{1,0:T(8,128)(2,1)} %bitcast.14), channel_id=1, source_target_pairs={{0,3},{1,0},{2,1},{3,2},{4,7},{5,4},{6,5},{7,6},{8,11},{9,8},{10,9... | collective-permute-start | bytes 786440 | tf_op jit(solution)/shard_map/ppermute | solution.py:443
  40.3 33.0 %collective-permute-start.8 = (bf16[128,4096]{1,0:T(8,128)(2,1)S(1)}, bf16[128,4096]{1,0:T(8,128)(2,1)}, u32[]{:S(2)}, u32[]{:S(2)}) collective-permute-start(bf16[128,4096]{1,0:T(8,128)(2,1)S(1)} %constant_dynamic-update-slice_fusion.lo_in), channel_id=1, source_target_pairs={{0,4},{4,0},{1,5},{5,1},{2,6},{6,2},{3,7},{7,3},{8,12},{12,8},{9,1... | collective-permute-start | bytes 3145736 | tf_op jit(solution)/shard_map/ppermute | solution.py:439
  45.3 0.7 copy-start.15
  51.1 22.2 %all-to-all-start.1 = ((bf16[32,64,128]{2,1,0:T(8,128)(2,1)}), bf16[32,64,128]{2,1,0:T(8,128)(2,1)S(1)}, u32[]{:S(2)}, u32[]{:S(2)}) async-start(bf16[32,64,128]{2,1,0:T(8,128)(2,1)} %shard_map.138), calls=%async_computation.1 | async-start | bytes 1048576 | tf_op jit(solution)/shard_map/all_to_all | solution.py:509
  59.2 9.1 %collective-permute-start.7 = (bf16[32,4096]{1,0:T(8,128)(2,1)}, bf16[32,4096]{1,0:T(8,128)(2,1)}, u32[]{:S(2)}, u32[]{:S(2)}) collective-permute-start(bf16[32,4096]{1,0:T(8,128)(2,1)} %bitcast.15), channel_id=1, source_target_pairs={{0,2},{1,3},{2,0},{3,1},{4,6},{5,7},{6,4},{7,5},{8,10},{9,11},{10,... | collective-permute-start | bytes 786440 | tf_op jit(solution)/shard_map/ppermute | solution.py:443
  66.3 1.3 %copy-start = (bf16[4,2,128,1024]{3,2,1,0:T(8,128)(2,1)}, bf16[4,2,128,1024]{3,2,1,0:T(8,128)(2,1)S(1)}, u32[]{:S(2)}) copy-start(bf16[4,2,128,1024]{3,2,1,0:T(8,128)(2,1)S(1)} %get-tuple-element.75.wide_in) | copy-start | bytes 6291460
  67.7 0.7 copy-start.9
  77.9 17.3 %all-to-all-start.2 = ((bf16[32,24,128]{2,1,0:T(8,128)(2,1)}), bf16[32,24,128]{2,1,0:T(8,128)(2,1)S(1)}, u32[]{:S(2)}, u32[]{:S(2)}) async-start(bf16[32,24,128]{2,1,0:T(8,128)(2,1)} %get-tuple-element.68), calls=%async_computation.2 | async-start | bytes 393216 | tf_op jit(solution)/shard_map/all_to_all | solution.py:527
  85.8 1.6 %copy-start.1 = (bf16[4,2,128,1024]{3,2,1,0:T(8,128)(2,1)S(1)}, bf16[4,2,128,1024]{3,2,1,0:T(8,128)(2,1)}, u32[]{:S(2)}) copy-start(bf16[4,2,128,1024]{3,2,1,0:T(8,128)(2,1)} %copy-done) | copy-start | bytes 6291460
  87.4 0.9 copy-start.10
  89.9 3.5 %collective-permute-start.10 = (bf16[128,1280]{1,0:T(8,128)(2,1)S(1)}, bf16[128,1280]{1,0:T(8,128)(2,1)S(1)}, u32[]{:S(2)}, u32[]{:S(2)}) collective-permute-start(bf16[128,1280]{1,0:T(8,128)(2,1)S(1)} %get-tuple-element.79), channel_id=1, source_target_pairs={{0,4},{4,0},{1,5},{5,1},{2,6},{6,2},{3,7},{7,3},{8,12},{12,8},{9,1... | collective-permute-start | bytes 983048 | tf_op jit(solution)/shard_map/ppermute | solution.py:439
  91.5 1.3 %collective-permute-start.9 = (bf16[4,16,128]{2,1,0:T(8,128)(2,1)S(1)}, bf16[4,16,128]{2,1,0:T(8,128)(2,1)S(1)}, u32[]{:S(2)}, u32[]{:S(2)}) collective-permute-start(bf16[4,16,128]{2,1,0:T(8,128)(2,1)S(1)} %get-tuple-element.70), channel_id=1, source_target_pairs={{0,4},{4,0},{1,5},{5,1},{2,6},{6,2},{3,7},{7,3},{8,12},{12,8},{9,1... | collective-permute-start | bytes 49160 | tf_op jit(solution)/shard_map/ppermute | solution.py:439
  92.8 0.6 copy-start.14
  95.9 18.0 %all-to-all-start.3 = ((bf16[32,16,128]{2,1,0:T(8,128)(2,1)}), bf16[32,16,128]{2,1,0:T(8,128)(2,1)S(1)}, u32[]{:S(2)}, u32[]{:S(2)}) async-start(bf16[32,16,128]{2,1,0:T(8,128)(2,1)} %get-tuple-element.84), calls=%async_computation.3 | async-start | bytes 262144 | tf_op jit(solution)/shard_map/all_to_all | solution.py:545
  103.6 5.9 %collective-permute-start.11 = (bf16[32,128]{1,0:T(8,128)(2,1)S(1)}, bf16[32,128]{1,0:T(8,128)(2,1)S(1)}, u32[]{:S(2)}, u32[]{:S(2)}) collective-permute-start(bf16[32,128]{1,0:T(8,128)(2,1)S(1)} %get-tuple-element.90), channel_id=1, source_target_pairs={{0,1},{1,2},{2,3},{3,0},{4,5},{5,6},{6,7},{7,4},{8,9},{9,10},{10,1... | collective-permute-start | bytes 24584 | tf_op jit(solution)/shard_map/ppermute | solution.py:443
  104.6 4.9 %collective-permute-start.12 = (bf16[32,128]{1,0:T(8,128)(2,1)S(1)}, bf16[32,128]{1,0:T(8,128)(2,1)S(1)}, u32[]{:S(2)}, u32[]{:S(2)}) collective-permute-start(bf16[32,128]{1,0:T(8,128)(2,1)S(1)} %get-tuple-element.91), channel_id=1, source_target_pairs={{0,2},{1,3},{2,0},{3,1},{4,6},{5,7},{6,4},{7,5},{8,10},{9,11},{10,... | collective-permute-start | bytes 24584 | tf_op jit(solution)/shard_map/ppermute | solution.py:443
  106.8 2.8 %collective-permute-start.13 = (bf16[32,128]{1,0:T(8,128)(2,1)S(1)}, bf16[32,128]{1,0:T(8,128)(2,1)S(1)}, u32[]{:S(2)}, u32[]{:S(2)}) collective-permute-start(bf16[32,128]{1,0:T(8,128)(2,1)S(1)} %get-tuple-element.92), channel_id=1, source_target_pairs={{0,3},{1,0},{2,1},{3,2},{4,7},{5,4},{6,5},{7,6},{8,11},{9,8},{10,9... | collective-permute-start | bytes 24584 | tf_op jit(solution)/shard_map/ppermute | solution.py:443
  108.0 5.8 %collective-permute-start.14 = (f32[8,128]{1,0:T(8,128)S(1)}, f32[8,128]{1,0:T(8,128)S(1)}, u32[]{:S(2)}, u32[]{:S(2)}) collective-permute-start(f32[8,128]{1,0:T(8,128)S(1)} %get-tuple-element.83.t_own), channel_id=1, source_target_pairs={{0,4},{4,0},{1,5},{5,1},{2,6},{6,2},{3,7},{7,3},{8,12},{12,8},{9,1... | collective-permute-start | bytes 12296 | tf_op jit(solution)/shard_map/ppermute | solution.py:439
  109.5 0.6 copy-start.16
  109.6 0.6 copy-start.17
  110.1 0.6 copy-start.18
  113.9 2.5 %collective-permute-start.15 = (bf16[32,16,128]{2,1,0:T(8,128)(2,1)S(1)}, bf16[32,16,128]{2,1,0:T(8,128)(2,1)S(1)}, u32[]{:S(2)}, u32[]{:S(2)}) collective-permute-start(bf16[32,16,128]{2,1,0:T(8,128)(2,1)S(1)} %all-to-all-done.3.w_own), channel_id=1, source_target_pairs={{0,4},{4,0},{1,5},{5,1},{2,6},{6,2},{3,7},{7,3},{8,12},{12,8},{9,1... | collective-permute-start | bytes 393224 | tf_op jit(solution)/shard_map/ppermute | solution.py:439

commit v5 on v4

--- a/solution.py
+++ b/solution.py
@@ -94,7 +94,7 @@
             at += width
 
 
-def project_kernel(scal, w, params, l3, l2, l1, l0, own, other):
+def project_kernel(scal, w, params, l2, l3, l1, l0, own, other):
     first = scal[1]
     head = iota((2 * HH, 2 * HH), 0)
     head = jnp.where(first == 0, head, lax.rem(head + HH, 2 * HH))
@@ -396,20 +396,15 @@
         out[HH:] = other[k]
 
 
-def input_kernel(scal, a0, a1, a2, a3, w0, w1, w2, w3, out, mat, sems):
+def input_kernel(scal, a0, a1, a2, a3, w0, w1, w2, w3, out):
     first = scal[1]
-    copies = []
-    for k, w in enumerate((w0, w1, w2, w3)):
-        for j, side in enumerate((first, 1 - first)):
-            part = w.at[pl.ds(pl.multiple_of(HH * side, HH), HH)]
-            place = mat.at[pl.ds(2 * HH * k + HH * j, HH)]
-            copies += copy_all([(part, place)], sems, 2 * k + j)
+    sides = [pl.ds(pl.multiple_of(HH * side, HH), HH) for side in (first, 1 - first)]
     rows = [a[...] for a in (a0, a1, a2, a3)]
     zed = jnp.concatenate(rows, 0).astype(F32).T[:32].astype(BF)
-    wait_all(copies)
     for k in range(D // 512):
         cols = slice(k * 512, (k + 1) * 512)
-        out[:, cols] = dot(zed, mat[:, cols]).astype(BF)
+        mat = [w[side, cols] for w in (w0, w1, w2, w3) for side in sides]
+        out[:, cols] = dot(zed, jnp.concatenate(mat, 0)).astype(BF)
 
 
 def call(kernel, outs, args, scratch=(), sems=0, far_in=(), far_out=(), flops=0, moved=0, limit=16):
@@ -469,7 +464,7 @@
     proj_own, proj_other = call(
         project_kernel,
         [((2, HH, 128), F32), ((HH, 128), F32)],
-        [scal, weight_mine, params] + pieces[::-1],
+        [scal, weight_mine, params] + [pieces[i] for i in (2, 3, 1, 0)],
         limit=16,
         flops=2**26,
         moved=2**21,
@@ -550,9 +545,6 @@
         input_kernel,
         [((32, D), BF)],
         [scal] + zed + weights,
-        [((TP * 2 * HH, D), BF)],
-        sems=8,
-        far_in=(5, 6, 7, 8),
         limit=INPUT_LIMIT,
     )
 

time: 118 us -> 117 us (level)
  transfers between devices with their start and end apart: 20 -> 20, of which waited for: 8 -> 10; matrix products, arithmetic and copies ran while one was open for 3% -> 3% of each run, Pallas kernels for 10% -> 10%
where the time goes in v5:
time: 117 us
  starting transfers between devices  59.7 us (51%)
  waiting for transfers between devices  21.3 us (18%)
  Pallas kernels  19.7 us (17%)
  local copies, waits for them, and re-layouts  14.9 us (13%)
    pallas_call x11, Pallas kernels, call(): pl.pallas_call(kernel, out_shape=[jax.ShapeDtypeStruct(s, t) for s, t in...  19.7 us
    unnamed x45, local copies, waits for them, and re-layouts  13 us
    all_to_all x1, starting transfers between devices, local(): got = lax.all_to_all(msg, 'chip', 0, 0, tiled=True)  11 us
    ppermute x7, starting transfers between devices, swap(): return lax.ppermute(v, 'core', [(0, 1), (1, 0)])  9.73 us
    ppermute x6, starting transfers between devices, round_tp(): return lax.ppermute(v, 'tp', [(i, (i + k) % TP) for i in range(TP)])  8.77 us
    all_to_all x1, starting transfers between devices, local(): states = lax.all_to_all(folded, 'chip', 0, 0, tiled=True)  8.06 us
    all_to_all x1, starting transfers between devices, local(): shares = lax.all_to_all(parts, 'chip', 0, 0, tiled=True)  7.86 us
    all_to_all x1, starting transfers between devices, local(): weight_own = lax.all_to_all(total, 'chip', 0, 0, tiled=True)  7.73 us
  transfers between devices with their start and end apart: 20, of which 10 were waited for; matrix products, arithmetic and copies ran while one was open for 3% of the time, Pallas kernels for 10%

profile of v5, /device:TPU:1, one launch (start us, length us, event | category | flops | bytes accessed | tf_op | source)
XLA Modules:
  0.0 116.6 jit_solution(5075074071836885743)
XLA Ops:
  0.6 3.8 %collective-permute-start = (bf16[32,4096]{1,0:T(8,128)(2,1)}, bf16[32,4096]{1,0:T(8,128)(2,1)S(1)}, u32[]{:S(2)}, u32[]{:S(2)}) collective-permute-start(bf16[32,4096]{1,0:T(8,128)(2,1)} %l0.1), channel_id=1, source_target_pairs={{2,0},{3,1},{0,2},{1,3},{6,4},{7,5},{4,6},{5,7},{10,8},{11,9},{8,1... | collective-permute-start | bytes 786440 | tf_op jit(solution)/shard_map/ppermute | solution.py:450
  4.5 0.4 collective-permute-start.1
  4.9 2.3 %collective-permute-start.2 = (bf16[32,4096]{1,0:T(8,128)(2,1)}, bf16[32,4096]{1,0:T(8,128)(2,1)S(1)}, u32[]{:S(2)}, u32[]{:S(2)}) collective-permute-start(bf16[32,4096]{1,0:T(8,128)(2,1)} %l0.1), channel_id=1, source_target_pairs={{1,0},{2,1},{3,2},{0,3},{5,4},{6,5},{7,6},{4,7},{9,8},{10,9},{11,1... | collective-permute-start | bytes 786440 | tf_op jit(solution)/shard_map/ppermute | solution.py:450
  7.1 0.1 pad_add_fusion.scal
  7.2 1.0 copy-done.7
  8.3 1.0 copy-done.8
  9.3 0.8 copy-done.11
  10.2 0.8 copy-done.12
  11.0 0.6 shard_map.136
  11.6 1.6 %collective-permute-start.4 = (bf16[128,2304]{1,0:T(8,128)(2,1)S(1)}, bf16[128,2304]{1,0:T(8,128)(2,1)S(1)}, u32[]{:S(2)}, u32[]{:S(2)}) collective-permute-start(bf16[128,2304]{1,0:T(8,128)(2,1)S(1)} %get-tuple-element.59), channel_id=1, source_target_pairs={{0,4},{4,0},{1,5},{5,1},{2,6},{6,2},{3,7},{7,3},{8,12},{12,8},{9,1... | collective-permute-start | bytes 1769480 | tf_op jit(solution)/shard_map/ppermute | solution.py:434
  13.2 1.0 dynamic-slice_bitcast_fusion.1
  14.3 0.0 collective-permute-done.l2
  14.3 0.0 copy-start.4
  14.3 2.1 %collective-permute-done.1.l3 = bf16[32,4096]{1,0:T(8,128)(2,1)S(1)} collective-permute-done((bf16[32,4096]{1,0:T(8,128)(2,1)}, bf16[32,4096]{1,0:T(8,128)(2,1)S(1)}, u32[]{:S(2)}, u32[]{:S(2)}) %collective-permute-start.1) | collective-permute-done | bytes 262176 | tf_op jit(solution)/shard_map/ppermute | solution.py:450
  16.4 0.2 collective-permute-done.2.l1
  16.6 1.0 shard_map.135
  17.6 0.0 copy-done.5
  17.6 1.5 %collective-permute-start.3 = (f32[16,128]{1,0:T(8,128)S(1)}, f32[16,128]{1,0:T(8,128)S(1)}, u32[]{:S(2)}, u32[]{:S(2)}) collective-permute-start(f32[16,128]{1,0:T(8,128)S(1)} %get-tuple-element.57), channel_id=1, source_target_pairs={{0,4},{4,0},{1,5},{5,1},{2,6},{6,2},{3,7},{7,3},{8,12},{12,8},{9,1... | collective-permute-start | bytes 24584 | tf_op jit(solution)/shard_map/ppermute | solution.py:434
  19.2 0.8 collective-permute-done.3.pp
  20.0 0.0 collective-permute-done.4.other
  20.0 2.2 %shard_map.137 = (bf16[32,72,128]{2,1,0:T(8,128)(2,1)S(1)}, bf16[2,128,1024]{2,1,0:T(8,128)(2,1)S(1)}, f32[4,32,128]{2,1,0:T(8,128)S(1)}) custom-call(s32[3]{0:T(128)S(1)} %pad_add_fusion.scal, f32[2,16,128]{2,1,0:T(8,128)S(1)} %get-tuple-element.56.po, f32[16,128]{1,0:T(8,128)S(1)} %collective-permute-done.3.pp, ...), custom_call_target="tpu_custom_call" | custom-call | flops 268435456 | bytes 4194304 | tf_op jit(solution)/shard_map/pallas_call | solution.py:422
  22.2 0.8 copy-done.6
  23.0 11.0 %all-to-all-start = ((bf16[32,72,128]{2,1,0:T(8,128)(2,1)}), bf16[32,72,128]{2,1,0:T(8,128)(2,1)S(1)}, u32[]{:S(2)}, u32[]{:S(2)}) async-start(bf16[32,72,128]{2,1,0:T(8,128)(2,1)} %copy-done.6), calls=%async_computation | async-start | bytes 1179648 | tf_op jit(solution)/shard_map/all_to_all | solution.py:483
  34.0 1.0 constant_dynamic-update-slice_fusion.2
  35.0 1.0 constant_dynamic-update-slice_fusion.1
  36.0 1.2 %collective-permute-start.5 = (bf16[32,4096]{1,0:T(8,128)(2,1)}, bf16[32,4096]{1,0:T(8,128)(2,1)S(1)}, u32[]{:S(2)}, u32[]{:S(2)}) collective-permute-start(bf16[32,4096]{1,0:T(8,128)(2,1)} %bitcast.13), channel_id=1, source_target_pairs={{0,1},{1,2},{2,3},{3,0},{4,5},{5,6},{6,7},{7,4},{8,9},{9,10},{10,1... | collective-permute-start | bytes 786440 | tf_op jit(solution)/shard_map/ppermute | solution.py:438
  37.2 1.6 %collective-permute-start.6 = (bf16[32,4096]{1,0:T(8,128)(2,1)}, bf16[32,4096]{1,0:T(8,128)(2,1)}, u32[]{:S(2)}, u32[]{:S(2)}) collective-permute-start(bf16[32,4096]{1,0:T(8,128)(2,1)} %bitcast.14), channel_id=1, source_target_pairs={{0,3},{1,0},{2,1},{3,2},{4,7},{5,4},{6,5},{7,6},{8,11},{9,8},{10,9... | collective-permute-start | bytes 786440 | tf_op jit(solution)/shard_map/ppermute | solution.py:438
  38.7 1.0 constant_dynamic-update-slice_fusion.lo_in
  39.7 1.3 %collective-permute-start.8 = (bf16[128,4096]{1,0:T(8,128)(2,1)S(1)}, bf16[128,4096]{1,0:T(8,128)(2,1)}, u32[]{:S(2)}, u32[]{:S(2)}) collective-permute-start(bf16[128,4096]{1,0:T(8,128)(2,1)S(1)} %constant_dynamic-update-slice_fusion.lo_in), channel_id=1, source_target_pairs={{0,4},{4,0},{1,5},{5,1},{2,6},{6,2},{3,7},{7,3},{8,12},{12,8},{9,1... | collective-permute-start | bytes 3145736 | tf_op jit(solution)/shard_map/ppermute | solution.py:434
  41.0 3.7 %collective-permute-done.5.w1 = bf16[32,4096]{1,0:T(8,128)(2,1)S(1)} collective-permute-done((bf16[32,4096]{1,0:T(8,128)(2,1)}, bf16[32,4096]{1,0:T(8,128)(2,1)S(1)}, u32[]{:S(2)}, u32[]{:S(2)}) %collective-permute-start.5) | collective-permute-done | bytes 262176 | tf_op jit(solution)/shard_map/ppermute | solution.py:438
  44.7 0.7 copy-done.15
  45.4 4.2 %all-to-all-done.msg = bf16[32,72,128]{2,1,0:T(8,128)(2,1)S(1)} async-done(((bf16[32,72,128]{2,1,0:T(8,128)(2,1)}), bf16[32,72,128]{2,1,0:T(8,128)(2,1)S(1)}, u32[]{:S(2)}, u32[]{:S(2)}) %all-to-all-start) | async-done | bytes 589856 | tf_op jit(solution)/shard_map/all_to_all | solution.py:483
  49.6 0.9 shard_map.138
  50.6 8.1 %all-to-all-start.1 = ((bf16[32,64,128]{2,1,0:T(8,128)(2,1)}), bf16[32,64,128]{2,1,0:T(8,128)(2,1)S(1)}, u32[]{:S(2)}, u32[]{:S(2)}) async-start(bf16[32,64,128]{2,1,0:T(8,128)(2,1)} %shard_map.138), calls=%async_computation.1 | async-start | bytes 1048576 | tf_op jit(solution)/shard_map/all_to_all | solution.py:504
  58.6 2.1 %collective-permute-start.7 = (bf16[32,4096]{1,0:T(8,128)(2,1)}, bf16[32,4096]{1,0:T(8,128)(2,1)}, u32[]{:S(2)}, u32[]{:S(2)}) collective-permute-start(bf16[32,4096]{1,0:T(8,128)(2,1)} %bitcast.15), channel_id=1, source_target_pairs={{0,2},{1,3},{2,0},{3,1},{4,6},{5,7},{6,4},{7,5},{8,10},{9,11},{10,... | collective-permute-start | bytes 786440 | tf_op jit(solution)/shard_map/ppermute | solution.py:438
  60.7 4.6 %shard_map.139 = (bf16[4,2,128,1024]{3,2,1,0:T(8,128)(2,1)S(1)}, f32[2,128,128]{2,1,0:T(8,128)S(1)}, f32[2,128,128]{2,1,0:T(8,128)S(1)}, f32[2,32,128]{2,1,0:T(8,128)S(1)}) custom-call(f32[4,32,128]{2,1,0:T(8,128)S(1)} %get-tuple-element.66.small, bf16[128,2304]{1,0:T(8,128)(2,1)S(1)} %get-tuple-element.58.own, ...), custom_call_target="tpu_custom_call" | custom-call | tf_op jit(solution)/shard_map/pallas_call | solution.py:422
  65.3 1.3 %copy-done = bf16[4,2,128,1024]{3,2,1,0:T(8,128)(2,1)} copy-done((bf16[4,2,128,1024]{3,2,1,0:T(8,128)(2,1)}, bf16[4,2,128,1024]{3,2,1,0:T(8,128)(2,1)S(1)}, u32[]{:S(2)}) %copy-start) | copy-done | bytes 2097176
  66.6 0.7 copy-done.9
  67.3 0.0 collective-permute-done.7.w2
  67.3 5.4 %all-to-all-done.1.got = bf16[32,64,128]{2,1,0:T(8,128)(2,1)S(1)} async-done(((bf16[32,64,128]{2,1,0:T(8,128)(2,1)}), bf16[32,64,128]{2,1,0:T(8,128)(2,1)S(1)}, u32[]{:S(2)}, u32[]{:S(2)}) %all-to-all-start.1) | async-done | bytes 524320 | tf_op jit(solution)/shard_map/all_to_all | solution.py:504
  72.7 4.6 %shard_map.140 = (bf16[4,16,128]{2,1,0:T(8,128)(2,1)S(1)}, bf16[4,16,128]{2,1,0:T(8,128)(2,1)S(1)}, bf16[32,24,128]{2,1,0:T(8,128)(2,1)}) custom-call(s32[3]{0:T(128)S(1)} %pad_add_fusion.scal, bf16[32,64,128]{2,1,0:T(8,128)(2,1)S(1)} %all-to-all-done.1.got, bf16[2,128,1024]{2,1,0:T(8,128)(2,1)S(1)} %get-tuple-element.65.keep, ...), custom_call_target="tpu_custom_call" | custom-call | flops 536870912 | bytes 8388608 | tf_op jit(solution)/shard_map/pallas_call | solution.py:422
  77.4 7.9 %all-to-all-start.2 = ((bf16[32,24,128]{2,1,0:T(8,128)(2,1)}), bf16[32,24,128]{2,1,0:T(8,128)(2,1)S(1)}, u32[]{:S(2)}, u32[]{:S(2)}) async-start(bf16[32,24,128]{2,1,0:T(8,128)(2,1)} %get-tuple-element.68), calls=%async_computation.2 | async-start | bytes 393216 | tf_op jit(solution)/shard_map/all_to_all | solution.py:522
  85.2 1.6 %copy-done.1 = bf16[4,2,128,1024]{3,2,1,0:T(8,128)(2,1)S(1)} copy-done((bf16[4,2,128,1024]{3,2,1,0:T(8,128)(2,1)S(1)}, bf16[4,2,128,1024]{3,2,1,0:T(8,128)(2,1)}, u32[]{:S(2)}) %copy-start.1) | copy-done | bytes 2097176
  86.8 0.9 copy-done.10
  87.7 1.6 %shard_map.142 = (bf16[128,1280]{1,0:T(8,128)(2,1)S(1)}, bf16[128,1280]{1,0:T(8,128)(2,1)S(1)}) custom-call(s32[3]{0:T(128)S(1)} %pad_add_fusion.scal, bf16[32,64,128]{2,1,0:T(8,128)(2,1)S(1)} %all-to-all-done.1.got, bf16[2,128,1024]{2,1,0:T(8,128)(2,1)S(1)} %get-tuple-element.65.keep, f32[4,32,128]{2,1,0:T(8,128)S(1)} %get-tuple-element.66.small, ...), custom_call_target="tpu_custom_call" | custom-call | tf_op jit(solution)/shard_map/pallas_call | solution.py:422
  89.4 1.6 %collective-permute-start.10 = (bf16[128,1280]{1,0:T(8,128)(2,1)S(1)}, bf16[128,1280]{1,0:T(8,128)(2,1)S(1)}, u32[]{:S(2)}, u32[]{:S(2)}) collective-permute-start(bf16[128,1280]{1,0:T(8,128)(2,1)S(1)} %get-tuple-element.79), channel_id=1, source_target_pairs={{0,4},{4,0},{1,5},{5,1},{2,6},{6,2},{3,7},{7,3},{8,12},{12,8},{9,1... | collective-permute-start | bytes 983048 | tf_op jit(solution)/shard_map/ppermute | solution.py:434
  91.0 0.1 collective-permute-start.9
  91.1 1.2 %collective-permute-done.9.other = bf16[4,16,128]{2,1,0:T(8,128)(2,1)S(1)} collective-permute-done((bf16[4,16,128]{2,1,0:T(8,128)(2,1)S(1)}, bf16[4,16,128]{2,1,0:T(8,128)(2,1)S(1)}, u32[]{:S(2)}, u32[]{:S(2)}) %collective-permute-start.9) | collective-permute-done | bytes 16416 | tf_op jit(solution)/shard_map/ppermute | solution.py:434
  92.2 0.6 copy-done.14
  92.8 1.8 %all-to-all-done.2.msg = bf16[32,24,128]{2,1,0:T(8,128)(2,1)S(1)} async-done(((bf16[32,24,128]{2,1,0:T(8,128)(2,1)}), bf16[32,24,128]{2,1,0:T(8,128)(2,1)S(1)}, u32[]{:S(2)}, u32[]{:S(2)}) %all-to-all-start.2) | async-done | bytes 196640 | tf_op jit(solution)/shard_map/all_to_all | solution.py:522
  94.6 0.7 shard_map.143
  95.3 7.7 %all-to-all-start.3 = ((bf16[32,16,128]{2,1,0:T(8,128)(2,1)}), bf16[32,16,128]{2,1,0:T(8,128)(2,1)S(1)}, u32[]{:S(2)}, u32[]{:S(2)}) async-start(bf16[32,16,128]{2,1,0:T(8,128)(2,1)} %get-tuple-element.84), calls=%async_computation.3 | async-start | bytes 262144 | tf_op jit(solution)/shard_map/all_to_all | solution.py:540
  103.1 1.2 %collective-permute-start.11 = (bf16[32,128]{1,0:T(8,128)(2,1)S(1)}, bf16[32,128]{1,0:T(8,128)(2,1)S(1)}, u32[]{:S(2)}, u32[]{:S(2)}) collective-permute-start(bf16[32,128]{1,0:T(8,128)(2,1)S(1)} %get-tuple-element.90), channel_id=1, source_target_pairs={{0,1},{1,2},{2,3},{3,0},{4,5},{5,6},{6,7},{7,4},{8,9},{9,10},{10,1... | collective-permute-start | bytes 24584 | tf_op jit(solution)/shard_map/ppermute | solution.py:438
  104.2 2.4 %collective-permute-start.12 = (bf16[32,128]{1,0:T(8,128)(2,1)S(1)}, bf16[32,128]{1,0:T(8,128)(2,1)S(1)}, u32[]{:S(2)}, u32[]{:S(2)}) collective-permute-start(bf16[32,128]{1,0:T(8,128)(2,1)S(1)} %get-tuple-element.91), channel_id=1, source_target_pairs={{0,2},{1,3},{2,0},{3,1},{4,6},{5,7},{6,4},{7,5},{8,10},{9,11},{10,... | collective-permute-start | bytes 24584 | tf_op jit(solution)/shard_map/ppermute | solution.py:438
  106.7 0.3 collective-permute-start.13
  107.0 1.5 %collective-permute-start.14 = (f32[8,128]{1,0:T(8,128)S(1)}, f32[8,128]{1,0:T(8,128)S(1)}, u32[]{:S(2)}, u32[]{:S(2)}) collective-permute-start(f32[8,128]{1,0:T(8,128)S(1)} %get-tuple-element.83.t_own), channel_id=1, source_target_pairs={{0,4},{4,0},{1,5},{5,1},{2,6},{6,2},{3,7},{7,3},{8,12},{12,8},{9,1... | collective-permute-start | bytes 12296 | tf_op jit(solution)/shard_map/ppermute | solution.py:434
  108.5 0.0 collective-permute-done.11.a1
  108.5 0.0 collective-permute-done.12.a2
  108.5 0.9 collective-permute-done.13.a3
  109.5 0.6 copy-done.18
  110.1 2.3 %shard_map.144 = bf16[32,4096]{1,0:T(8,128)(2,1)} custom-call(s32[3]{0:T(128)} %copy-done.13, bf16[32,128]{1,0:T(8,128)(2,1)} %copy-done.14, bf16[32,128]{1,0:T(8,128)(2,1)} %copy-done.16, bf16[32,128]{1,0:T(8,128)(2,1)} %copy-done.17, bf16[32,128]{1,0:T(8,128)(2,1)} %copy-done.18, bf16[32,4096]{1,0:T(8,128)(2,1)} %bitcast.16, bf16[32,4096]{1,0:T(8,128)(2,1)} %copy-done.15, ...), custom_call_target="tpu_custom_call" | custom-call | tf_op jit(solution)/shard_map/pallas_call | solution.py:422
  112.4 2.2 %collective-permute-start.15 = (bf16[32,16,128]{2,1,0:T(8,128)(2,1)S(1)}, bf16[32,16,128]{2,1,0:T(8,128)(2,1)S(1)}, u32[]{:S(2)}, u32[]{:S(2)}) collective-permute-start(bf16[32,16,128]{2,1,0:T(8,128)(2,1)S(1)} %all-to-all-done.3.w_own), channel_id=1, source_target_pairs={{0,4},{4,0},{1,5},{5,1},{2,6},{6,2},{3,7},{7,3},{8,12},{12,8},{9,1... | collective-permute-start | bytes 393224 | tf_op jit(solution)/shard_map/ppermute | solution.py:434
  114.5 1.0 collective-permute-done.15.w_other
  115.5 1.1 shard_map.145
  (37 shorter events, 0.1 us)
Async XLA Ops:
  0.6 15.9 %copy-start.2 = (bf16[32,4096]{1,0:T(8,128)(2,1)S(1)}, bf16[32,4096]{1,0:T(8,128)(2,1)}, u32[]{:S(2)}) copy-start(bf16[32,4096]{1,0:T(8,128)(2,1)} %l0.1) | copy-start | bytes 786436
  0.6 13.7 %collective-permute-start = (bf16[32,4096]{1,0:T(8,128)(2,1)}, bf16[32,4096]{1,0:T(8,128)(2,1)S(1)}, u32[]{:S(2)}, u32[]{:S(2)}) collective-permute-start(bf16[32,4096]{1,0:T(8,128)(2,1)} %l0.1), channel_id=1, source_target_pairs={{2,0},{3,1},{0,2},{1,3},{6,4},{7,5},{4,6},{5,7},{10,8},{11,9},{8,1... | collective-permute-start | bytes 786440 | tf_op jit(solution)/shard_map/ppermute | solution.py:450
  4.5 11.9 %collective-permute-start.1 = (bf16[32,4096]{1,0:T(8,128)(2,1)}, bf16[32,4096]{1,0:T(8,128)(2,1)S(1)}, u32[]{:S(2)}, u32[]{:S(2)}) collective-permute-start(bf16[32,4096]{1,0:T(8,128)(2,1)} %l0.1), channel_id=1, source_target_pairs={{3,0},{0,1},{1,2},{2,3},{7,4},{4,5},{5,6},{6,7},{11,8},{8,9},{9,10... | collective-permute-start | bytes 786440 | tf_op jit(solution)/shard_map/ppermute | solution.py:450
  4.9 11.7 %collective-permute-start.2 = (bf16[32,4096]{1,0:T(8,128)(2,1)}, bf16[32,4096]{1,0:T(8,128)(2,1)S(1)}, u32[]{:S(2)}, u32[]{:S(2)}) collective-permute-start(bf16[32,4096]{1,0:T(8,128)(2,1)} %l0.1), channel_id=1, source_target_pairs={{1,0},{2,1},{3,2},{0,3},{5,4},{6,5},{7,6},{4,7},{9,8},{10,9},{11,1... | collective-permute-start | bytes 786440 | tf_op jit(solution)/shard_map/ppermute | solution.py:450
  7.2 1.0 copy-start.7
  8.3 1.0 copy-start.8
  9.3 0.8 copy-start.11
  10.2 0.8 copy-start.12
  11.0 74.2 %copy-start.13 = (s32[3]{0:T(128)}, s32[3]{0:T(128)S(1)}, u32[]{:S(2)}) copy-start(s32[3]{0:T(128)S(1)} %pad_add_fusion.scal) | copy-start | bytes 40
  11.0 3.3 %copy-start.19 = (f32[32]{0:T(128)S(1)}, f32[32]{0:T(128)}, u32[]{:S(2)}) copy-start(f32[32]{0:T(128)} %param.11) | copy-start | bytes 388
  11.0 3.3 %copy-start.20 = (f32[32]{0:T(128)S(1)}, f32[32]{0:T(128)}, u32[]{:S(2)}) copy-start(f32[32]{0:T(128)} %param.10) | copy-start | bytes 388
  11.6 8.4 %collective-permute-start.4 = (bf16[128,2304]{1,0:T(8,128)(2,1)S(1)}, bf16[128,2304]{1,0:T(8,128)(2,1)S(1)}, u32[]{:S(2)}, u32[]{:S(2)}) collective-permute-start(bf16[128,2304]{1,0:T(8,128)(2,1)S(1)} %get-tuple-element.59), channel_id=1, source_target_pairs={{0,4},{4,0},{1,5},{5,1},{2,6},{6,2},{3,7},{7,3},{8,12},{12,8},{9,1... | collective-permute-start | bytes 1769480 | tf_op jit(solution)/shard_map/ppermute | solution.py:434
  14.3 3.3 %copy-start.4 = (bf16[32,4096]{1,0:T(8,128)(2,1)}, bf16[32,4096]{1,0:T(8,128)(2,1)S(1)}, u32[]{:S(2)}) copy-start(bf16[32,4096]{1,0:T(8,128)(2,1)S(1)} %collective-permute-done.l2) | copy-start | bytes 786436
  16.4 3.6 %copy-start.3 = (bf16[32,4096]{1,0:T(8,128)(2,1)}, bf16[32,4096]{1,0:T(8,128)(2,1)S(1)}, u32[]{:S(2)}) copy-start(bf16[32,4096]{1,0:T(8,128)(2,1)S(1)} %collective-permute-done.1.l3) | copy-start | bytes 786436
  16.5 1.1 copy-start.5
  17.6 2.4 %collective-permute-start.3 = (f32[16,128]{1,0:T(8,128)S(1)}, f32[16,128]{1,0:T(8,128)S(1)}, u32[]{:S(2)}, u32[]{:S(2)}) collective-permute-start(f32[16,128]{1,0:T(8,128)S(1)} %get-tuple-element.57), channel_id=1, source_target_pairs={{0,4},{4,0},{1,5},{5,1},{2,6},{6,2},{3,7},{7,3},{8,12},{12,8},{9,1... | collective-permute-start | bytes 24584 | tf_op jit(solution)/shard_map/ppermute | solution.py:434
  22.2 0.8 copy-start.6
  23.0 26.6 %all-to-all-start = ((bf16[32,72,128]{2,1,0:T(8,128)(2,1)}), bf16[32,72,128]{2,1,0:T(8,128)(2,1)S(1)}, u32[]{:S(2)}, u32[]{:S(2)}) async-start(bf16[32,72,128]{2,1,0:T(8,128)(2,1)} %copy-done.6), calls=%async_computation | async-start | bytes 1179648 | tf_op jit(solution)/shard_map/all_to_all | solution.py:483
  36.0 8.7 %collective-permute-start.5 = (bf16[32,4096]{1,0:T(8,128)(2,1)}, bf16[32,4096]{1,0:T(8,128)(2,1)S(1)}, u32[]{:S(2)}, u32[]{:S(2)}) collective-permute-start(bf16[32,4096]{1,0:T(8,128)(2,1)} %bitcast.13), channel_id=1, source_target_pairs={{0,1},{1,2},{2,3},{3,0},{4,5},{5,6},{6,7},{7,4},{8,9},{9,10},{10,1... | collective-permute-start | bytes 786440 | tf_op jit(solution)/shard_map/ppermute | solution.py:438
  37.2 8.3 %collective-permute-start.6 = (bf16[32,4096]{1,0:T(8,128)(2,1)}, bf16[32,4096]{1,0:T(8,128)(2,1)}, u32[]{:S(2)}, u32[]{:S(2)}) collective-permute-start(bf16[32,4096]{1,0:T(8,128)(2,1)} %bitcast.14), channel_id=1, source_target_pairs={{0,3},{1,0},{2,1},{3,2},{4,7},{5,4},{6,5},{7,6},{8,11},{9,8},{10,9... | collective-permute-start | bytes 786440 | tf_op jit(solution)/shard_map/ppermute | solution.py:438
  39.7 33.0 %collective-permute-start.8 = (bf16[128,4096]{1,0:T(8,128)(2,1)S(1)}, bf16[128,4096]{1,0:T(8,128)(2,1)}, u32[]{:S(2)}, u32[]{:S(2)}) collective-permute-start(bf16[128,4096]{1,0:T(8,128)(2,1)S(1)} %constant_dynamic-update-slice_fusion.lo_in), channel_id=1, source_target_pairs={{0,4},{4,0},{1,5},{5,1},{2,6},{6,2},{3,7},{7,3},{8,12},{12,8},{9,1... | collective-permute-start | bytes 3145736 | tf_op jit(solution)/shard_map/ppermute | solution.py:434
  44.7 0.7 copy-start.15
  50.6 22.2 %all-to-all-start.1 = ((bf16[32,64,128]{2,1,0:T(8,128)(2,1)}), bf16[32,64,128]{2,1,0:T(8,128)(2,1)S(1)}, u32[]{:S(2)}, u32[]{:S(2)}) async-start(bf16[32,64,128]{2,1,0:T(8,128)(2,1)} %shard_map.138), calls=%async_computation.1 | async-start | bytes 1048576 | tf_op jit(solution)/shard_map/all_to_all | solution.py:504
  58.6 8.7 %collective-permute-start.7 = (bf16[32,4096]{1,0:T(8,128)(2,1)}, bf16[32,4096]{1,0:T(8,128)(2,1)}, u32[]{:S(2)}, u32[]{:S(2)}) collective-permute-start(bf16[32,4096]{1,0:T(8,128)(2,1)} %bitcast.15), channel_id=1, source_target_pairs={{0,2},{1,3},{2,0},{3,1},{4,6},{5,7},{6,4},{7,5},{8,10},{9,11},{10,... | collective-permute-start | bytes 786440 | tf_op jit(solution)/shard_map/ppermute | solution.py:438
  65.3 1.3 %copy-start = (bf16[4,2,128,1024]{3,2,1,0:T(8,128)(2,1)}, bf16[4,2,128,1024]{3,2,1,0:T(8,128)(2,1)S(1)}, u32[]{:S(2)}) copy-start(bf16[4,2,128,1024]{3,2,1,0:T(8,128)(2,1)S(1)} %get-tuple-element.75.wide_in) | copy-start | bytes 6291460
  66.6 0.7 copy-start.9
  77.4 17.3 %all-to-all-start.2 = ((bf16[32,24,128]{2,1,0:T(8,128)(2,1)}), bf16[32,24,128]{2,1,0:T(8,128)(2,1)S(1)}, u32[]{:S(2)}, u32[]{:S(2)}) async-start(bf16[32,24,128]{2,1,0:T(8,128)(2,1)} %get-tuple-element.68), calls=%async_computation.2 | async-start | bytes 393216 | tf_op jit(solution)/shard_map/all_to_all | solution.py:522
  85.2 1.6 %copy-start.1 = (bf16[4,2,128,1024]{3,2,1,0:T(8,128)(2,1)S(1)}, bf16[4,2,128,1024]{3,2,1,0:T(8,128)(2,1)}, u32[]{:S(2)}) copy-start(bf16[4,2,128,1024]{3,2,1,0:T(8,128)(2,1)} %copy-done) | copy-start | bytes 6291460
  86.8 0.9 copy-start.10
  89.4 3.5 %collective-permute-start.10 = (bf16[128,1280]{1,0:T(8,128)(2,1)S(1)}, bf16[128,1280]{1,0:T(8,128)(2,1)S(1)}, u32[]{:S(2)}, u32[]{:S(2)}) collective-permute-start(bf16[128,1280]{1,0:T(8,128)(2,1)S(1)} %get-tuple-element.79), channel_id=1, source_target_pairs={{0,4},{4,0},{1,5},{5,1},{2,6},{6,2},{3,7},{7,3},{8,12},{12,8},{9,1... | collective-permute-start | bytes 983048 | tf_op jit(solution)/shard_map/ppermute | solution.py:434
  91.0 1.3 %collective-permute-start.9 = (bf16[4,16,128]{2,1,0:T(8,128)(2,1)S(1)}, bf16[4,16,128]{2,1,0:T(8,128)(2,1)S(1)}, u32[]{:S(2)}, u32[]{:S(2)}) collective-permute-start(bf16[4,16,128]{2,1,0:T(8,128)(2,1)S(1)} %get-tuple-element.70), channel_id=1, source_target_pairs={{0,4},{4,0},{1,5},{5,1},{2,6},{6,2},{3,7},{7,3},{8,12},{12,8},{9,1... | collective-permute-start | bytes 49160 | tf_op jit(solution)/shard_map/ppermute | solution.py:434
  92.2 0.6 copy-start.14
  95.3 17.0 %all-to-all-start.3 = ((bf16[32,16,128]{2,1,0:T(8,128)(2,1)}), bf16[32,16,128]{2,1,0:T(8,128)(2,1)S(1)}, u32[]{:S(2)}, u32[]{:S(2)}) async-start(bf16[32,16,128]{2,1,0:T(8,128)(2,1)} %get-tuple-element.84), calls=%async_computation.3 | async-start | bytes 262144 | tf_op jit(solution)/shard_map/all_to_all | solution.py:540
  103.1 5.4 %collective-permute-start.11 = (bf16[32,128]{1,0:T(8,128)(2,1)S(1)}, bf16[32,128]{1,0:T(8,128)(2,1)S(1)}, u32[]{:S(2)}, u32[]{:S(2)}) collective-permute-start(bf16[32,128]{1,0:T(8,128)(2,1)S(1)} %get-tuple-element.90), channel_id=1, source_target_pairs={{0,1},{1,2},{2,3},{3,0},{4,5},{5,6},{6,7},{7,4},{8,9},{9,10},{10,1... | collective-permute-start | bytes 24584 | tf_op jit(solution)/shard_map/ppermute | solution.py:438
  104.2 4.3 %collective-permute-start.12 = (bf16[32,128]{1,0:T(8,128)(2,1)S(1)}, bf16[32,128]{1,0:T(8,128)(2,1)S(1)}, u32[]{:S(2)}, u32[]{:S(2)}) collective-permute-start(bf16[32,128]{1,0:T(8,128)(2,1)S(1)} %get-tuple-element.91), channel_id=1, source_target_pairs={{0,2},{1,3},{2,0},{3,1},{4,6},{5,7},{6,4},{7,5},{8,10},{9,11},{10,... | collective-permute-start | bytes 24584 | tf_op jit(solution)/shard_map/ppermute | solution.py:438
  106.7 2.8 %collective-permute-start.13 = (bf16[32,128]{1,0:T(8,128)(2,1)S(1)}, bf16[32,128]{1,0:T(8,128)(2,1)S(1)}, u32[]{:S(2)}, u32[]{:S(2)}) collective-permute-start(bf16[32,128]{1,0:T(8,128)(2,1)S(1)} %get-tuple-element.92), channel_id=1, source_target_pairs={{0,3},{1,0},{2,1},{3,2},{4,7},{5,4},{6,5},{7,6},{8,11},{9,8},{10,9... | collective-permute-start | bytes 24584 | tf_op jit(solution)/shard_map/ppermute | solution.py:438
  107.0 5.3 %collective-permute-start.14 = (f32[8,128]{1,0:T(8,128)S(1)}, f32[8,128]{1,0:T(8,128)S(1)}, u32[]{:S(2)}, u32[]{:S(2)}) collective-permute-start(f32[8,128]{1,0:T(8,128)S(1)} %get-tuple-element.83.t_own), channel_id=1, source_target_pairs={{0,4},{4,0},{1,5},{5,1},{2,6},{6,2},{3,7},{7,3},{8,12},{12,8},{9,1... | collective-permute-start | bytes 12296 | tf_op jit(solution)/shard_map/ppermute | solution.py:434
  108.5 1.0 copy-start.16
  108.5 1.0 copy-start.17
  109.5 0.6 copy-start.18
  112.4 3.1 %collective-permute-start.15 = (bf16[32,16,128]{2,1,0:T(8,128)(2,1)S(1)}, bf16[32,16,128]{2,1,0:T(8,128)(2,1)S(1)}, u32[]{:S(2)}, u32[]{:S(2)}) collective-permute-start(bf16[32,16,128]{2,1,0:T(8,128)(2,1)S(1)} %all-to-all-done.3.w_own), channel_id=1, source_target_pairs={{0,4},{4,0},{1,5},{5,1},{2,6},{6,2},{3,7},{7,3},{8,12},{12,8},{9,1... | collective-permute-start | bytes 393224 | tf_op jit(solution)/shard_map/ppermute | solution.py:434
